TPU v7x, 512 devices: a whole 4x4x16 slice. The times are simulated.
512 devices in a mesh: grp: 16 (over y, z_lo), dev: 32 (over z_hi, x, core).
Axes of the slice: x: 4, y: 4, z: 16 (z_hi: 4, z_lo: 4; z = z_hi * 4 + z_lo), core: 2. Of those that a mesh axis runs over, the one named last changes fastest.
Arguments:
- queries: bfloat16 [4096, 4096], P('dev', 'grp'), may hold values from -16 to 16
- passages: bfloat16 [8192, 4096], P('dev', 'grp'), may hold values from -8 to 8
- positive: int32 [4096], P('dev'), may hold values from 0 to 4095, each once
Outputs:
- query_grad: bfloat16 [4096, 4096], P('dev', 'grp')
- passage_grad: bfloat16 [8192, 4096], P('dev', 'grp')
Inputs may be any that keep to these rules, and one draw needn't show every extreme that they name: Every one of the first 4096 passages is the positive of exactly one query.
All inputs are finite; a program needn't handle non-finite values.
Results may differ from a plain program's by a relative error of at most 0.0035.
Values may be sent and summed in bfloat16 or wider, within the bound.
No kernel may reach another device: no remote copies, remote signals or barrier semaphores. Data moves between devices by JAX's collectives and lax.ppermute only.
A program may use at most 64 MiB of HBM per device.

v0:
```python
import math

import jax
import jax.numpy as jnp
from jax import lax
from jax.sharding import PartitionSpec as P


def per_device(queries, passages, positive):
    rows = queries.shape[0]
    width = queries.shape[1]
    full_width = width * lax.axis_size("grp")
    scale = 2.0 / math.sqrt(full_width)
    gathered = lax.all_gather(passages, "dev", axis=0, tiled=True)
    count = gathered.shape[0]
    partial_value = lax.dot_general(
        queries, gathered, (((1,), (1,)), ((), ())), preferred_element_type=jnp.float32
    )
    logits = lax.psum(partial_value, "grp") * scale
    top = jnp.max(logits, axis=1, keepdims=True)
    exps = jnp.exp(logits - top)
    prob = exps / jnp.sum(exps, axis=1, keepdims=True)
    columns = lax.broadcasted_iota(jnp.int32, (rows, count), 1)
    onehot = (columns == positive[:, None]).astype(jnp.float32)
    weights = (prob - onehot).astype(jnp.bfloat16)
    query_grad = jnp.dot(weights, gathered, preferred_element_type=jnp.float32).astype(jnp.bfloat16)
    by_query = lax.all_to_all(weights, "dev", split_axis=1, concat_axis=0, tiled=True)
    passage_sum = lax.dot_general(
        by_query,
        lax.all_gather(queries, "dev", axis=0, tiled=True),
        (((0,), (0,)), ((), ())),
        preferred_element_type=jnp.float32,
    )
    return (query_grad, passage_sum.astype(jnp.bfloat16))


def solution(mesh):
    in_specs = (P("dev", "grp"), P("dev", "grp"), P("dev"))
    out_specs = (P("dev", "grp"), P("dev", "grp"))
    return jax.shard_map(
        per_device, mesh=mesh, in_specs=in_specs, out_specs=out_specs, check_vma=False
    )
```

profile of v0, /device:TPU:6, one launch (start us, length us, event | category | flops | bytes accessed | tf_op | source)
XLA Modules:
  0.0 502.3 jit_solution(6084520516901241940)
XLA Ops:
  7.2 0.0 all-gather.3.cloned.1.call-start
  7.2 0.7 all-gather.3.cloned.1.call-update
  7.9 0.0 all-reduce.2.cloned.1.call-start
  7.9 102.8 %all-gather.3.cloned.1.call-done = bf16[8192,256]{1,0:T(8,128)(2,1)} async-done(((bf16[256,256]{1,0:T(8,128)(2,1)}), bf16[8192,256]{1,0:T(8,128)(2,1)}) %all-gather.3.cloned.1.call-update) | async-done | bytes 4194320 | tf_op jit(solution)/shard_map/all_gather | solution.py:14
  110.7 5.7 %fusion.1 = f32[128,8192]{1,0:T(8,128)} fusion(bf16[128,256]{1,0:T(8,128)(2,1)} %param.3, bf16[8192,256]{1,0:T(8,128)(2,1)} %all-gather.3.cloned.1.call-done), kind=kOutput, calls=%fused_computation.8 | convolution fusion | flops 536870912 | bytes 8454144 | tf_op jit(solution)/shard_map/dot_general | solution.py:16
  116.4 0.0 all-reduce.2.cloned.1.call-update
  116.4 0.0 copy-start.1
  116.4 209.1 %all-reduce.2.cloned.1.call-done = f32[128,8192]{1,0:T(8,128)} async-done(((f32[128,8192]{1,0:T(8,128)}), f32[128,8192]{1,0:T(8,128)}) %all-reduce.2.cloned.1.call-update) | async-done | bytes 4194320 | tf_op jit(solution)/shard_map/psum | solution.py:19
  325.5 0.0 copy-start
  325.5 2.7 multiply_reduce_fusion
  328.2 0.8 copy-done
  329.0 0.8 fusion
  329.8 0.0 copy-done.1
  329.8 1.4 subtract_convert_fusion
  331.2 1.6 copy.8
  332.8 12.7 %all-to-all-start = ((bf16[128,32,256]{2,0,1:T(8,128)(2,1)}), bf16[128,32,256]{2,0,1:T(8,128)(2,1)}, u32[]{:S(2)}, u32[]{:S(2)}) async-start(bf16[128,32,256]{2,0,1:T(8,128)(2,1)} %bitcast.14), calls=%async_computation | async-start | bytes 4194304 | tf_op jit(solution)/shard_map/all_to_all | solution.py:27
  345.5 0.0 all-gather.5.cloned.1.call-start
  345.5 0.7 all-gather.5.cloned.1.call-update
  346.2 3.5 convolution_convert_fusion.1
  349.8 142.4 %all-gather.5.cloned.1.call-done = bf16[4096,256]{1,0:T(8,128)(2,1)} async-done(((bf16[128,256]{1,0:T(8,128)(2,1)}), bf16[4096,256]{1,0:T(8,128)(2,1)}) %all-gather.5.cloned.1.call-update) | async-done | bytes 2097168 | tf_op jit(solution)/shard_map/all_gather | solution.py:30
  492.1 0.0 all-to-all-done
  492.1 3.6 convolution_convert_fusion
Async XLA Ops:
  7.2 103.6 %all-gather.3.cloned.1.call-start = ((), (), s32[]{:S(2)}) async-start(), calls=%async_computation.1 | async-start | bytes 4325376 | tf_op jit(solution)/shard_map/all_gather | solution.py:14
  7.9 317.6 %all-reduce.2.cloned.1.call-start = ((), (), s32[]{:S(2)}) async-start(), calls=%async_computation.2 | async-start | bytes 8388608 | tf_op jit(solution)/shard_map/psum | solution.py:19
  116.4 213.4 %copy-start.1 = (s32[128]{0:T(128)S(1)}, s32[128]{0:T(128)}, u32[]{:S(2)}) copy-start(s32[128]{0:T(128)} %param.5) | copy-start | bytes 1540
  325.5 3.4 copy-start
  332.8 159.3 %all-to-all-start = ((bf16[128,32,256]{2,0,1:T(8,128)(2,1)}), bf16[128,32,256]{2,0,1:T(8,128)(2,1)}, u32[]{:S(2)}, u32[]{:S(2)}) async-start(bf16[128,32,256]{2,0,1:T(8,128)(2,1)} %bitcast.14), calls=%async_computation | async-start | bytes 4194304 | tf_op jit(solution)/shard_map/all_to_all | solution.py:27
  345.5 146.6 %all-gather.5.cloned.1.call-start = ((), (), s32[]{:S(2)}) async-start(), calls=%async_computation.3 | async-start | bytes 2162688 | tf_op jit(solution)/shard_map/all_gather | solution.py:30
Sparse Core Ops, SparseCore 0:
  11.1 99.5 all-gather.2
  116.5 208.9 all-reduce.1
  349.5 142.6 all-gather.4
where the time goes:
time: 504 us; the launch traced here: 502 us
  waiting for transfers between devices  456 us (90%)
  between operations  13.8 us (3%)
  starting transfers between devices  12.8 us (3%)
  matrix products  12.8 us (3%)
    psum x1, waiting for transfers between devices, per_device(): logits = lax.psum(partial_value, 'grp') * scale  209 us
    all_gather x1, waiting for transfers between devices, per_device(): lax.all_gather(queries, 'dev', axis=0, tiled=True)  142 us
    all_gather x1, waiting for transfers between devices, per_device(): gathered = lax.all_gather(passages, 'dev', axis=0, tiled=True)  103 us
    all_to_all x1, starting transfers between devices, per_device(): lax.all_to_all(weights, 'dev', split_axis=1, concat_axis=0, tiled=True)  12.7 us
  transfers between devices with their start and end apart: 4, of which 3 were waited for; matrix products, arithmetic and copies ran while one was open for 1% of the time, Pallas kernels for 0%

commit v1 on v0

v1 whole, which is shorter than its diff:
```python
import math

import jax
import jax.numpy as jnp
from jax import lax
from jax.sharding import Mesh, PartitionSpec as P

ROWS = ("zh", "x", "c")
FEATS = ("y", "zl")
BF = jnp.bfloat16
F32 = jnp.float32


def shift(value, axis, step):
    n = lax.axis_size(axis)
    return lax.ppermute(value, axis, [(i, (i + step) % n) for i in range(n)])


def gather(value, axis, dim):
    n = lax.axis_size(axis)
    me = lax.axis_index(axis)
    size = value.shape[dim]
    whole = list(value.shape)
    whole[dim] = size * n
    out = jnp.zeros(whole, value.dtype)
    for step in range(n):
        block = value if step == 0 else shift(value, axis, step)
        out = lax.dynamic_update_slice_in_dim(out, block, ((me - step) % n) * size, dim)
    return out


def scatter_sum(piece, axis):
    n = lax.axis_size(axis)
    me = lax.axis_index(axis)
    moved = [shift(piece((me + step) % n).astype(BF), axis, step) for step in range(1, n)]
    total = piece(me)
    for block in moved:
        total = total + block.astype(F32)
    return total


def dot(a, b, over_a, over_b):
    return lax.dot_general(a, b, (((over_a,), (over_b,)), ((), ())), preferred_element_type=F32)


def per_device(queries, passages, positive):
    rows, width = queries.shape
    groups = lax.axis_size(FEATS)
    devs = lax.axis_size(ROWS)
    full = width * groups
    part = rows // groups
    scale = 2.0 / math.sqrt(full)
    core, x, y = lax.axis_index("c"), lax.axis_index("x"), lax.axis_index("y")
    group = lax.axis_index(FEATS)
    dev = lax.axis_index(ROWS)

    mine = lax.all_to_all(queries.reshape(groups, part, width), FEATS, 0, 0, tiled=True)
    mine = mine.transpose(1, 0, 2).reshape(part, full)
    half = gather(gather(mine, "zh", 0), "x", 0)
    q = gather(half, "c", 0)

    p = gather(gather(passages, "zl", 1), "y", 1)
    count = p.shape[0]

    logits = dot(q, p, 1, 1) * scale
    n_q = logits.shape[0]
    top = jnp.max(logits, axis=1)
    exps = jnp.exp(logits - top[:, None])
    total = jnp.sum(exps, axis=1)
    own_pos = lax.dynamic_slice_in_dim(positive, group * part, part).astype(F32)
    note = jnp.concatenate([top, total, jnp.pad(own_pos, (0, 128 - part))])
    notes = lax.all_to_all(
        jnp.broadcast_to(note, (devs, note.shape[0])), ("c", "x", "zh"), 0, 0, tiled=True
    )
    tops, totals = notes[:, :n_q], notes[:, n_q : 2 * n_q]
    pos = notes[:, 2 * n_q : 2 * n_q + part].reshape(n_q).astype(jnp.int32)
    peak = jnp.max(tops, axis=0)
    denom = jnp.sum(totals * jnp.exp(tops - peak), axis=0)
    factor = jnp.exp(top - peak) / denom
    columns = lax.broadcasted_iota(jnp.int32, (n_q, count), 1) + dev * count
    onehot = (columns == pos[:, None]).astype(F32)
    weights = (exps * factor[:, None] - onehot).astype(BF)

    strip = full // lax.axis_size("y")

    def passage_piece(owner):
        return dot(weights, lax.dynamic_slice_in_dim(q, owner * strip, strip, 1), 0, 0)

    by_y = scatter_sum(passage_piece, "y")
    passage_grad = scatter_sum(lambda owner: lax.dynamic_slice_in_dim(by_y, owner * width, width, 1), "zl")

    n_half = n_q // 2
    p_other = shift(p, "c", 1)
    w_mine = lax.dynamic_slice_in_dim(weights, core * n_half, n_half, 0)
    w_other = shift(lax.dynamic_slice_in_dim(weights, (1 - core) * n_half, n_half, 0), "c", 1)
    chip = dot(w_mine, p, 1, 0) + dot(w_other, p_other, 1, 0)
    n_x = n_half // lax.axis_size("x")
    by_x = scatter_sum(lambda owner: lax.dynamic_slice_in_dim(chip, owner * n_x, n_x, 0), "x")
    by_zh = scatter_sum(lambda owner: lax.dynamic_slice_in_dim(by_x, owner * part, part, 0), "zh")
    back = by_zh.astype(BF).reshape(part, groups, width).transpose(1, 0, 2)
    query_grad = lax.all_to_all(back, FEATS, 0, 0, tiled=True).reshape(rows, width)
    return query_grad, passage_grad.astype(BF)


def solution(mesh):
    fine = Mesh(mesh.devices.reshape(4, 4, 4, 4, 2), FEATS + ROWS)
    in_specs = (P(ROWS, FEATS), P(ROWS, FEATS), P(ROWS))
    out_specs = (P(ROWS, FEATS), P(ROWS, FEATS))
    return jax.shard_map(per_device, mesh=fine, in_specs=in_specs, out_specs=out_specs, check_vma=False)
```

time: 504 us -> 217 us (0.43)
  waiting for transfers between devices: 456 us -> 69.6 us
  starting transfers between devices: 12.8 us -> 126 us
  between operations: 13.8 us -> 1.4 us
  local copies, waits for them, and re-layouts: 2.37 us -> 8.32 us
    all_gather x2 -> x0, waiting for transfers between devices: 245 us -> none  [the longest x1 142 us: per_device(): lax.all_gather(queries, 'dev', axis=0, tiled=True)]
    psum x1 -> x0, waiting for transfers between devices: 209 us -> none  [per_device(): logits = lax.psum(partial_value, 'grp') * scale]
    ppermute x0 -> x27, starting transfers between devices: none -> 102 us  [shift(): return lax.ppermute(value, axis, [(i, (i + step) % n) for i in range(n)])]
    ppermute x0 -> x27, waiting for transfers between devices: none -> 44.1 us  [shift(): return lax.ppermute(value, axis, [(i, (i + step) % n) for i in range(n)])]
    all_to_all x1 -> x3, waiting for transfers between devices: 0.01 us -> 25.5 us  [the longest x1 12.7 us: per_device(): lax.all_to_all(jnp.broadcast_to(note, (devs, note.shape[0])), ('c', 'x',...]
    all_to_all x1 -> x3, starting transfers between devices: 12.7 us -> 23.4 us  [the longest x1 13.8 us: per_device(): lax.all_to_all(jnp.broadcast_to(note, (devs, note.shape[0])), ('c', 'x',...]
    dot_general x3 -> x7, matrix products: 12.8 us -> 7.88 us  [dot(): lax.dot_general(a, b, (((over_a,), (over_b,)), ((), ())), preferred_eleme...]
  transfers between devices with their start and end apart: 4 -> 30, of which waited for: 3 -> 17; matrix products, arithmetic and copies ran while one was open for 1% -> 8% of each run, Pallas kernels for 0% -> 0%
where the time goes in v1:
time: 217 us; the launch traced here: 215 us
  starting transfers between devices  126 us (58%)
  waiting for transfers between devices  69.6 us (32%)
  local copies, waits for them, and re-layouts  8.32 us (4%)
  matrix products  7.88 us (4%)
  other arithmetic  2.5 us (1%)
    ppermute x27, starting transfers between devices, shift(): return lax.ppermute(value, axis, [(i, (i + step) % n) for i in range(n)])  102 us
    ppermute x27, waiting for transfers between devices, shift(): return lax.ppermute(value, axis, [(i, (i + step) % n) for i in range(n)])  44.1 us
    all_to_all x1, starting transfers between devices, per_device(): lax.all_to_all(jnp.broadcast_to(note, (devs, note.shape[0])), ('c', 'x',...  13.8 us
    all_to_all x1, waiting for transfers between devices, per_device(): lax.all_to_all(jnp.broadcast_to(note, (devs, note.shape[0])), ('c', 'x',...  12.7 us
    dot_general x7, matrix products, dot(): lax.dot_general(a, b, (((over_a,), (over_b,)), ((), ())), preferred_eleme...  7.88 us
    all_to_all x1, waiting for transfers between devices, per_device(): lax.all_to_all(back, FEATS, 0, 0, tiled=True).reshape(rows, width)  6.44 us
    all_to_all x1, waiting for transfers between devices, per_device(): lax.all_to_all(queries.reshape(groups, part, width), FEATS, 0, 0, tiled=T...  6.33 us
    all_to_all x1, starting transfers between devices, per_device(): lax.all_to_all(queries.reshape(groups, part, width), FEATS, 0, 0, tiled=T...  5.04 us
  transfers between devices with their start and end apart: 30, of which 17 were waited for; matrix products, arithmetic and copies ran while one was open for 8% of the time, Pallas kernels for 0%

profile of v1, /device:TPU:6, one launch (start us, length us, event | category | flops | bytes accessed | tf_op | source)
XLA Modules:
  0.0 215.4 jit_solution(13943751956039655301)
XLA Ops:
  0.6 3.8 %collective-permute-start.7 = (bf16[256,256]{1,0:T(8,128)(2,1)}, bf16[256,256]{1,0:T(8,128)(2,1)S(1)}, u32[]{:S(2)}, u32[]{:S(2)}) collective-permute-start(bf16[256,256]{1,0:T(8,128)(2,1)} %param.4), channel_id=1, source_target_pairs={{0,32},{32,64},{64,96},{96,0},{1,33},{33,65},{65,97},{97,1},{2,34}... | collective-permute-start | bytes 393224 | tf_op jit(solution)/shard_map/ppermute | solution.py:16
  4.5 5.2 %collective-permute-start.8 = (bf16[256,256]{1,0:T(8,128)(2,1)}, bf16[256,256]{1,0:T(8,128)(2,1)S(1)}, u32[]{:S(2)}, u32[]{:S(2)}) collective-permute-start(bf16[256,256]{1,0:T(8,128)(2,1)} %param.4), channel_id=1, source_target_pairs={{0,64},{32,96},{64,0},{96,32},{1,65},{33,97},{65,1},{97,33},{2,66}... | collective-permute-start | bytes 393224 | tf_op jit(solution)/shard_map/ppermute | solution.py:16
  9.7 2.9 %collective-permute-start.9 = (bf16[256,256]{1,0:T(8,128)(2,1)}, bf16[256,256]{1,0:T(8,128)(2,1)S(1)}, u32[]{:S(2)}, u32[]{:S(2)}) collective-permute-start(bf16[256,256]{1,0:T(8,128)(2,1)} %param.4), channel_id=1, source_target_pairs={{0,96},{32,0},{64,32},{96,64},{1,97},{33,1},{65,33},{97,65},{2,98}... | collective-permute-start | bytes 393224 | tf_op jit(solution)/shard_map/ppermute | solution.py:16
  12.6 5.0 %all-to-all-start = ((bf16[16,8,256]{2,1,0:T(8,128)(2,1)}), bf16[16,8,256]{2,1,0:T(8,128)(2,1)S(1)}, u32[]{:S(2)}, u32[]{:S(2)}) async-start(bf16[16,8,256]{2,1,0:T(8,128)(2,1)} %bitcast.28), calls=%async_computation | async-start | bytes 131072 | tf_op jit(solution)/shard_map/all_to_all | solution.py:57
  19.4 6.3 %all-to-all-done = bf16[16,8,256]{2,1,0:T(8,128)(2,1)S(1)} async-done(((bf16[16,8,256]{2,1,0:T(8,128)(2,1)}), bf16[16,8,256]{2,1,0:T(8,128)(2,1)S(1)}, u32[]{:S(2)}, u32[]{:S(2)}) %all-to-all-start) | async-done | bytes 65568 | tf_op jit(solution)/shard_map/all_to_all | solution.py:57
  25.8 9.1 %collective-permute-start = (bf16[8,4096]{1,0:T(8,128)(2,1)S(1)}, bf16[8,4096]{1,0:T(8,128)(2,1)S(1)}, u32[]{:S(2)}, u32[]{:S(2)}) collective-permute-start(bf16[8,4096]{1,0:T(8,128)(2,1)S(1)} %bitcast.23), channel_id=1, source_target_pairs={{0,8},{8,16},{16,24},{24,0},{1,9},{9,17},{17,25},{25,1},{2,10},{10... | collective-permute-start | bytes 196616 | tf_op jit(solution)/shard_map/ppermute | solution.py:16
  34.9 9.6 %collective-permute-start.1 = (bf16[8,4096]{1,0:T(8,128)(2,1)S(1)}, bf16[8,4096]{1,0:T(8,128)(2,1)S(1)}, u32[]{:S(2)}, u32[]{:S(2)}) collective-permute-start(bf16[8,4096]{1,0:T(8,128)(2,1)S(1)} %bitcast.24), channel_id=1, source_target_pairs={{0,16},{8,24},{16,0},{24,8},{1,17},{9,25},{17,1},{25,9},{2,18},{10... | collective-permute-start | bytes 196616 | tf_op jit(solution)/shard_map/ppermute | solution.py:16
  44.4 5.5 %collective-permute-start.2 = (bf16[8,4096]{1,0:T(8,128)(2,1)S(1)}, bf16[8,4096]{1,0:T(8,128)(2,1)S(1)}, u32[]{:S(2)}, u32[]{:S(2)}) collective-permute-start(bf16[8,4096]{1,0:T(8,128)(2,1)S(1)} %bitcast.25), channel_id=1, source_target_pairs={{0,24},{8,0},{16,8},{24,16},{1,25},{9,1},{17,9},{25,17},{2,26},{10... | collective-permute-start | bytes 196616 | tf_op jit(solution)/shard_map/ppermute | solution.py:16
  50.5 6.2 %collective-permute-done.2 = bf16[8,4096]{1,0:T(8,128)(2,1)S(1)} collective-permute-done((bf16[8,4096]{1,0:T(8,128)(2,1)S(1)}, bf16[8,4096]{1,0:T(8,128)(2,1)S(1)}, u32[]{:S(2)}, u32[]{:S(2)}) %collective-permute-start.2) | collective-permute-done | bytes 65568 | tf_op jit(solution)/shard_map/ppermute | solution.py:16
  56.7 2.4 %collective-permute-start.3 = (bf16[32,4096]{1,0:T(8,128)(2,1)S(1)}, bf16[32,4096]{1,0:T(8,128)(2,1)S(1)}, u32[]{:S(2)}, u32[]{:S(2)}) collective-permute-start(bf16[32,4096]{1,0:T(8,128)(2,1)S(1)} %constant_dynamic-update-slice_fusion.14), channel_id=1, source_target_pairs={{0,2},{2,4},{4,6},{6,0},{1,3},{3,5},{5,7},{7,1},{8,10},{10,12},{12... | collective-permute-start | bytes 786440 | tf_op jit(solution)/shard_map/ppermute | solution.py:16
  59.1 4.3 %collective-permute-start.4 = (bf16[32,4096]{1,0:T(8,128)(2,1)S(1)}, bf16[32,4096]{1,0:T(8,128)(2,1)S(1)}, u32[]{:S(2)}, u32[]{:S(2)}) collective-permute-start(bf16[32,4096]{1,0:T(8,128)(2,1)S(1)} %constant_dynamic-update-slice_fusion.14), channel_id=1, source_target_pairs={{0,4},{2,6},{4,0},{6,2},{1,5},{3,7},{5,1},{7,3},{8,12},{10,14},{12... | collective-permute-start | bytes 786440 | tf_op jit(solution)/shard_map/ppermute | solution.py:16
  65.7 4.6 %collective-permute-done.4 = bf16[32,4096]{1,0:T(8,128)(2,1)S(1)} collective-permute-done((bf16[32,4096]{1,0:T(8,128)(2,1)S(1)}, bf16[32,4096]{1,0:T(8,128)(2,1)S(1)}, u32[]{:S(2)}, u32[]{:S(2)}) %collective-permute-start.4) | collective-permute-done | bytes 262176 | tf_op jit(solution)/shard_map/ppermute | solution.py:16
  70.4 2.8 %collective-permute-done.5 = bf16[32,4096]{1,0:T(8,128)(2,1)S(1)} collective-permute-done((bf16[32,4096]{1,0:T(8,128)(2,1)S(1)}, bf16[32,4096]{1,0:T(8,128)(2,1)S(1)}, u32[]{:S(2)}, u32[]{:S(2)}) %collective-permute-start.5) | collective-permute-done | bytes 262176 | tf_op jit(solution)/shard_map/ppermute | solution.py:16
  75.1 2.5 %collective-permute-start.10 = (bf16[256,1024]{1,0:T(8,128)(2,1)S(1)}, bf16[256,1024]{1,0:T(8,128)(2,1)S(1)}, u32[]{:S(2)}, u32[]{:S(2)}) collective-permute-start(bf16[256,1024]{1,0:T(8,128)(2,1)S(1)} %constant_dynamic-update-slice_fusion.4), channel_id=1, source_target_pairs={{0,128},{128,256},{256,384},{384,0},{1,129},{129,257},{257,385},{3... | collective-permute-start | bytes 1572872 | tf_op jit(solution)/shard_map/ppermute | solution.py:16
  77.6 4.0 %collective-permute-start.11 = (bf16[256,1024]{1,0:T(8,128)(2,1)S(1)}, bf16[256,1024]{1,0:T(8,128)(2,1)S(1)}, u32[]{:S(2)}, u32[]{:S(2)}) collective-permute-start(bf16[256,1024]{1,0:T(8,128)(2,1)S(1)} %constant_dynamic-update-slice_fusion.4), channel_id=1, source_target_pairs={{0,256},{128,384},{256,0},{384,128},{1,257},{129,385},{257,1},{385... | collective-permute-start | bytes 1572872 | tf_op jit(solution)/shard_map/ppermute | solution.py:16
  81.6 3.2 %collective-permute-start.12 = (bf16[256,1024]{1,0:T(8,128)(2,1)S(1)}, bf16[256,1024]{1,0:T(8,128)(2,1)S(1)}, u32[]{:S(2)}, u32[]{:S(2)}) collective-permute-start(bf16[256,1024]{1,0:T(8,128)(2,1)S(1)} %constant_dynamic-update-slice_fusion.4), channel_id=1, source_target_pairs={{0,384},{128,0},{256,128},{384,256},{1,385},{129,1},{257,129},{385... | collective-permute-start | bytes 1572872 | tf_op jit(solution)/shard_map/ppermute | solution.py:16
  87.6 16.2 %collective-permute-done.10 = bf16[256,1024]{1,0:T(8,128)(2,1)S(1)} collective-permute-done((bf16[256,1024]{1,0:T(8,128)(2,1)S(1)}, bf16[256,1024]{1,0:T(8,128)(2,1)S(1)}, u32[]{:S(2)}, u32[]{:S(2)}) %collective-permute-start.10) | collective-permute-done | bytes 524320 | tf_op jit(solution)/shard_map/ppermute | solution.py:16
  109.2 2.3 %fusion.14 = (f32[256]{0:T(256)S(1)}, f32[256,256]{0,1:T(8,128)S(1)}) fusion(bf16[256,4096]{1,0:T(8,128)(2,1)S(1)} %constant_dynamic-update-slice_fusion.8, bf16[256,4096]{1,0:T(8,128)(2,1)} %constant_dynamic-update-slice_fusion), kind=kOutput, calls=%fused_computation.62 | convolution fusion | flops 537001728 | bytes 4457472 | tf_op jit(solution)/shard_map/dot_general | solution.py:43
  112.3 13.8 %all-to-all-start.1 = ((f32[32,1,640]{2,1,0:T(1,128)}), f32[32,1,640]{2,1,0:T(1,128)S(1)}, u32[]{:S(2)}, u32[]{:S(2)}) async-start(f32[32,1,640]{2,1,0:T(1,128)} %broadcast_in_dim.19), calls=%async_computation.1 | async-start | bytes 163840 | tf_op jit(solution)/shard_map/all_to_all | solution.py:72
  126.3 12.7 %all-to-all-done.1 = f32[32,1,640]{2,1,0:T(1,128)S(1)} async-done(((f32[32,1,640]{2,1,0:T(1,128)}), f32[32,1,640]{2,1,0:T(1,128)S(1)}, u32[]{:S(2)}, u32[]{:S(2)}) %all-to-all-start.1) | async-done | bytes 81952 | tf_op jit(solution)/shard_map/all_to_all | solution.py:72
  142.2 5.7 %collective-permute-start.22 = (bf16[256,1024]{1,0:T(8,128)(2,1)S(1)}, bf16[256,1024]{1,0:T(8,128)(2,1)S(1)}, u32[]{:S(2)}, u32[]{:S(2)}) collective-permute-start(bf16[256,1024]{1,0:T(8,128)(2,1)S(1)} %convolution_convert_fusion.1), channel_id=1, source_target_pairs={{0,256},{128,384},{256,0},{384,128},{1,257},{129,385},{257,1},{385... | collective-permute-start | bytes 1572872 | tf_op jit(solution)/shard_map/ppermute | solution.py:16
  156.4 4.2 %collective-permute-start.15 = (bf16[32,4096]{1,0:T(8,128)(2,1)S(1)}, bf16[32,4096]{1,0:T(8,128)(2,1)S(1)}, u32[]{:S(2)}, u32[]{:S(2)}) collective-permute-start(bf16[32,4096]{1,0:T(8,128)(2,1)S(1)} %get-tuple-element.2), channel_id=1, source_target_pairs={{0,2},{2,4},{4,6},{6,0},{1,3},{3,5},{5,7},{7,1},{8,10},{10,12},{12... | collective-permute-start | bytes 786440 | tf_op jit(solution)/shard_map/ppermute | solution.py:16
  160.6 2.8 %collective-permute-start.16 = (bf16[32,4096]{1,0:T(8,128)(2,1)S(1)}, bf16[32,4096]{1,0:T(8,128)(2,1)S(1)}, u32[]{:S(2)}, u32[]{:S(2)}) collective-permute-start(bf16[32,4096]{1,0:T(8,128)(2,1)S(1)} %get-tuple-element.4), channel_id=1, source_target_pairs={{0,4},{2,6},{4,0},{6,2},{1,5},{3,7},{5,1},{7,3},{8,12},{10,14},{12... | collective-permute-start | bytes 786440 | tf_op jit(solution)/shard_map/ppermute | solution.py:16
  163.5 2.4 %collective-permute-start.17 = (bf16[32,4096]{1,0:T(8,128)(2,1)S(1)}, bf16[32,4096]{1,0:T(8,128)(2,1)S(1)}, u32[]{:S(2)}, u32[]{:S(2)}) collective-permute-start(bf16[32,4096]{1,0:T(8,128)(2,1)S(1)} %get-tuple-element.3), channel_id=1, source_target_pairs={{0,6},{2,0},{4,2},{6,4},{1,7},{3,1},{5,3},{7,5},{8,14},{10,8},{12,... | collective-permute-start | bytes 786440 | tf_op jit(solution)/shard_map/ppermute | solution.py:16
  165.9 2.9 %collective-permute-done.22 = bf16[256,1024]{1,0:T(8,128)(2,1)S(1)} collective-permute-done((bf16[256,1024]{1,0:T(8,128)(2,1)S(1)}, bf16[256,1024]{1,0:T(8,128)(2,1)S(1)}, u32[]{:S(2)}, u32[]{:S(2)}) %collective-permute-start.22) | collective-permute-done | bytes 524320 | tf_op jit(solution)/shard_map/ppermute | solution.py:16
  173.2 4.9 %collective-permute-done.17 = bf16[32,4096]{1,0:T(8,128)(2,1)S(1)} collective-permute-done((bf16[32,4096]{1,0:T(8,128)(2,1)S(1)}, bf16[32,4096]{1,0:T(8,128)(2,1)S(1)}, u32[]{:S(2)}, u32[]{:S(2)}) %collective-permute-start.17) | collective-permute-done | bytes 262176 | tf_op jit(solution)/shard_map/ppermute | solution.py:16
  178.2 3.8 %collective-permute-start.18 = (bf16[8,4096]{1,0:T(8,128)(2,1)S(1)}, bf16[8,4096]{1,0:T(8,128)(2,1)S(1)}, u32[]{:S(2)}, u32[]{:S(2)}) collective-permute-start(bf16[8,4096]{1,0:T(8,128)(2,1)S(1)} %get-tuple-element.8), channel_id=1, source_target_pairs={{0,8},{8,16},{16,24},{24,0},{1,9},{9,17},{17,25},{25,1},{2,10},{10... | collective-permute-start | bytes 196616 | tf_op jit(solution)/shard_map/ppermute | solution.py:16
  182.1 6.2 %collective-permute-start.19 = (bf16[8,4096]{1,0:T(8,128)(2,1)S(1)}, bf16[8,4096]{1,0:T(8,128)(2,1)S(1)}, u32[]{:S(2)}, u32[]{:S(2)}) collective-permute-start(bf16[8,4096]{1,0:T(8,128)(2,1)S(1)} %get-tuple-element.10), channel_id=1, source_target_pairs={{0,16},{8,24},{16,0},{24,8},{1,17},{9,25},{17,1},{25,9},{2,18},{10... | collective-permute-start | bytes 196616 | tf_op jit(solution)/shard_map/ppermute | solution.py:16
  188.3 3.4 %collective-permute-start.20 = (bf16[8,4096]{1,0:T(8,128)(2,1)S(1)}, bf16[8,4096]{1,0:T(8,128)(2,1)S(1)}, u32[]{:S(2)}, u32[]{:S(2)}) collective-permute-start(bf16[8,4096]{1,0:T(8,128)(2,1)S(1)} %get-tuple-element.9), channel_id=1, source_target_pairs={{0,24},{8,0},{16,8},{24,16},{1,25},{9,1},{17,9},{25,17},{2,26},{10... | collective-permute-start | bytes 196616 | tf_op jit(solution)/shard_map/ppermute | solution.py:16
  195.6 5.7 %collective-permute-start.26 = (bf16[256,256]{1,0:T(8,128)(2,1)S(1)}, bf16[256,256]{1,0:T(8,128)(2,1)S(1)}, u32[]{:S(2)}, u32[]{:S(2)}) collective-permute-start(bf16[256,256]{1,0:T(8,128)(2,1)S(1)} %get-tuple-element.6), channel_id=1, source_target_pairs={{0,96},{32,0},{64,32},{96,64},{1,97},{33,1},{65,33},{97,65},{2,98}... | collective-permute-start | bytes 393224 | tf_op jit(solution)/shard_map/ppermute | solution.py:16
  202.0 4.6 %all-to-all-start.2 = ((bf16[16,8,256]{2,1,0:T(8,128)(2,1)}), bf16[16,8,256]{2,1,0:T(8,128)(2,1)S(1)}, u32[]{:S(2)}, u32[]{:S(2)}) async-start(bf16[16,8,256]{2,1,0:T(8,128)(2,1)} %bitcast.5), calls=%async_computation.2 | async-start | bytes 131072 | tf_op jit(solution)/shard_map/all_to_all | solution.py:101
  208.3 6.4 %all-to-all-done.2 = bf16[16,8,256]{2,1,0:T(8,128)(2,1)S(1)} async-done(((bf16[16,8,256]{2,1,0:T(8,128)(2,1)}), bf16[16,8,256]{2,1,0:T(8,128)(2,1)S(1)}, u32[]{:S(2)}, u32[]{:S(2)}) %all-to-all-start.2) | async-done | bytes 65568 | tf_op jit(solution)/shard_map/all_to_all | solution.py:101
  (78 shorter events, 38.7 us)
Async XLA Ops:
  0.6 18.8 %collective-permute-start.7 = (bf16[256,256]{1,0:T(8,128)(2,1)}, bf16[256,256]{1,0:T(8,128)(2,1)S(1)}, u32[]{:S(2)}, u32[]{:S(2)}) collective-permute-start(bf16[256,256]{1,0:T(8,128)(2,1)} %param.4), channel_id=1, source_target_pairs={{0,32},{32,64},{64,96},{96,0},{1,33},{33,65},{65,97},{97,1},{2,34}... | collective-permute-start | bytes 393224 | tf_op jit(solution)/shard_map/ppermute | solution.py:16
  4.5 14.9 %collective-permute-start.8 = (bf16[256,256]{1,0:T(8,128)(2,1)}, bf16[256,256]{1,0:T(8,128)(2,1)S(1)}, u32[]{:S(2)}, u32[]{:S(2)}) collective-permute-start(bf16[256,256]{1,0:T(8,128)(2,1)} %param.4), channel_id=1, source_target_pairs={{0,64},{32,96},{64,0},{96,32},{1,65},{33,97},{65,1},{97,33},{2,66}... | collective-permute-start | bytes 393224 | tf_op jit(solution)/shard_map/ppermute | solution.py:16
  9.7 65.4 %collective-permute-start.9 = (bf16[256,256]{1,0:T(8,128)(2,1)}, bf16[256,256]{1,0:T(8,128)(2,1)S(1)}, u32[]{:S(2)}, u32[]{:S(2)}) collective-permute-start(bf16[256,256]{1,0:T(8,128)(2,1)} %param.4), channel_id=1, source_target_pairs={{0,96},{32,0},{64,32},{96,64},{1,97},{33,1},{65,33},{97,65},{2,98}... | collective-permute-start | bytes 393224 | tf_op jit(solution)/shard_map/ppermute | solution.py:16
  12.6 13.2 %all-to-all-start = ((bf16[16,8,256]{2,1,0:T(8,128)(2,1)}), bf16[16,8,256]{2,1,0:T(8,128)(2,1)S(1)}, u32[]{:S(2)}, u32[]{:S(2)}) async-start(bf16[16,8,256]{2,1,0:T(8,128)(2,1)} %bitcast.28), calls=%async_computation | async-start | bytes 131072 | tf_op jit(solution)/shard_map/all_to_all | solution.py:57
  25.8 24.2 %collective-permute-start = (bf16[8,4096]{1,0:T(8,128)(2,1)S(1)}, bf16[8,4096]{1,0:T(8,128)(2,1)S(1)}, u32[]{:S(2)}, u32[]{:S(2)}) collective-permute-start(bf16[8,4096]{1,0:T(8,128)(2,1)S(1)} %bitcast.23), channel_id=1, source_target_pairs={{0,8},{8,16},{16,24},{24,0},{1,9},{9,17},{17,25},{25,1},{2,10},{10... | collective-permute-start | bytes 196616 | tf_op jit(solution)/shard_map/ppermute | solution.py:16
  34.9 15.6 %collective-permute-start.1 = (bf16[8,4096]{1,0:T(8,128)(2,1)S(1)}, bf16[8,4096]{1,0:T(8,128)(2,1)S(1)}, u32[]{:S(2)}, u32[]{:S(2)}) collective-permute-start(bf16[8,4096]{1,0:T(8,128)(2,1)S(1)} %bitcast.24), channel_id=1, source_target_pairs={{0,16},{8,24},{16,0},{24,8},{1,17},{9,25},{17,1},{25,9},{2,18},{10... | collective-permute-start | bytes 196616 | tf_op jit(solution)/shard_map/ppermute | solution.py:16
  44.4 12.3 %collective-permute-start.2 = (bf16[8,4096]{1,0:T(8,128)(2,1)S(1)}, bf16[8,4096]{1,0:T(8,128)(2,1)S(1)}, u32[]{:S(2)}, u32[]{:S(2)}) collective-permute-start(bf16[8,4096]{1,0:T(8,128)(2,1)S(1)} %bitcast.25), channel_id=1, source_target_pairs={{0,24},{8,0},{16,8},{24,16},{1,25},{9,1},{17,9},{25,17},{2,26},{10... | collective-permute-start | bytes 196616 | tf_op jit(solution)/shard_map/ppermute | solution.py:16
  56.7 9.0 %collective-permute-start.3 = (bf16[32,4096]{1,0:T(8,128)(2,1)S(1)}, bf16[32,4096]{1,0:T(8,128)(2,1)S(1)}, u32[]{:S(2)}, u32[]{:S(2)}) collective-permute-start(bf16[32,4096]{1,0:T(8,128)(2,1)S(1)} %constant_dynamic-update-slice_fusion.14), channel_id=1, source_target_pairs={{0,2},{2,4},{4,6},{6,0},{1,3},{3,5},{5,7},{7,1},{8,10},{10,12},{12... | collective-permute-start | bytes 786440 | tf_op jit(solution)/shard_map/ppermute | solution.py:16
  59.1 11.2 %collective-permute-start.4 = (bf16[32,4096]{1,0:T(8,128)(2,1)S(1)}, bf16[32,4096]{1,0:T(8,128)(2,1)S(1)}, u32[]{:S(2)}, u32[]{:S(2)}) collective-permute-start(bf16[32,4096]{1,0:T(8,128)(2,1)S(1)} %constant_dynamic-update-slice_fusion.14), channel_id=1, source_target_pairs={{0,4},{2,6},{4,0},{6,2},{1,5},{3,7},{5,1},{7,3},{8,12},{10,14},{12... | collective-permute-start | bytes 786440 | tf_op jit(solution)/shard_map/ppermute | solution.py:16
  63.4 9.7 %collective-permute-start.5 = (bf16[32,4096]{1,0:T(8,128)(2,1)S(1)}, bf16[32,4096]{1,0:T(8,128)(2,1)S(1)}, u32[]{:S(2)}, u32[]{:S(2)}) collective-permute-start(bf16[32,4096]{1,0:T(8,128)(2,1)S(1)} %constant_dynamic-update-slice_fusion.14), channel_id=1, source_target_pairs={{0,6},{2,0},{4,2},{6,4},{1,7},{3,1},{5,3},{7,5},{8,14},{10,8},{12,... | collective-permute-start | bytes 786440 | tf_op jit(solution)/shard_map/ppermute | solution.py:16
  73.2 35.9 %collective-permute-start.6 = (bf16[128,4096]{1,0:T(8,128)(2,1)S(1)}, bf16[128,4096]{1,0:T(8,128)(2,1)S(1)}, u32[]{:S(2)}, u32[]{:S(2)}) collective-permute-start(bf16[128,4096]{1,0:T(8,128)(2,1)S(1)} %constant_dynamic-update-slice_fusion.10), channel_id=1, source_target_pairs={{0,1},{1,0},{2,3},{3,2},{4,5},{5,4},{6,7},{7,6},{8,9},{9,8},{10,11... | collective-permute-start | bytes 3145736 | tf_op jit(solution)/shard_map/ppermute | solution.py:16
  75.1 28.7 %collective-permute-start.10 = (bf16[256,1024]{1,0:T(8,128)(2,1)S(1)}, bf16[256,1024]{1,0:T(8,128)(2,1)S(1)}, u32[]{:S(2)}, u32[]{:S(2)}) collective-permute-start(bf16[256,1024]{1,0:T(8,128)(2,1)S(1)} %constant_dynamic-update-slice_fusion.4), channel_id=1, source_target_pairs={{0,128},{128,256},{256,384},{384,0},{1,129},{129,257},{257,385},{3... | collective-permute-start | bytes 1572872 | tf_op jit(solution)/shard_map/ppermute | solution.py:16
  77.6 27.0 %collective-permute-start.11 = (bf16[256,1024]{1,0:T(8,128)(2,1)S(1)}, bf16[256,1024]{1,0:T(8,128)(2,1)S(1)}, u32[]{:S(2)}, u32[]{:S(2)}) collective-permute-start(bf16[256,1024]{1,0:T(8,128)(2,1)S(1)} %constant_dynamic-update-slice_fusion.4), channel_id=1, source_target_pairs={{0,256},{128,384},{256,0},{384,128},{1,257},{129,385},{257,1},{385... | collective-permute-start | bytes 1572872 | tf_op jit(solution)/shard_map/ppermute | solution.py:16
  81.6 24.7 %collective-permute-start.12 = (bf16[256,1024]{1,0:T(8,128)(2,1)S(1)}, bf16[256,1024]{1,0:T(8,128)(2,1)S(1)}, u32[]{:S(2)}, u32[]{:S(2)}) collective-permute-start(bf16[256,1024]{1,0:T(8,128)(2,1)S(1)} %constant_dynamic-update-slice_fusion.4), channel_id=1, source_target_pairs={{0,384},{128,0},{256,128},{384,256},{1,385},{129,1},{257,129},{385... | collective-permute-start | bytes 1572872 | tf_op jit(solution)/shard_map/ppermute | solution.py:16
  107.2 44.9 %collective-permute-start.14 = (bf16[256,4096]{1,0:T(8,128)(2,1)}, bf16[256,4096]{1,0:T(8,128)(2,1)}, u32[]{:S(2)}, u32[]{:S(2)}) collective-permute-start(bf16[256,4096]{1,0:T(8,128)(2,1)} %constant_dynamic-update-slice_fusion), channel_id=1, source_target_pairs={{0,1},{1,0},{2,3},{3,2},{4,5},{5,4},{6,7},{7,6},{8,9},{9,8},{10,11... | collective-permute-start | bytes 6291464 | tf_op jit(solution)/shard_map/ppermute | solution.py:16
  112.3 26.7 %all-to-all-start.1 = ((f32[32,1,640]{2,1,0:T(1,128)}), f32[32,1,640]{2,1,0:T(1,128)S(1)}, u32[]{:S(2)}, u32[]{:S(2)}) async-start(f32[32,1,640]{2,1,0:T(1,128)} %broadcast_in_dim.19), calls=%async_computation.1 | async-start | bytes 163840 | tf_op jit(solution)/shard_map/all_to_all | solution.py:72
  139.6 23.9 %collective-permute-start.21 = (bf16[256,1024]{1,0:T(8,128)(2,1)S(1)}, bf16[256,1024]{1,0:T(8,128)(2,1)S(1)}, u32[]{:S(2)}, u32[]{:S(2)}) collective-permute-start(bf16[256,1024]{1,0:T(8,128)(2,1)S(1)} %convolution_convert_fusion.2), channel_id=1, source_target_pairs={{0,128},{128,256},{256,384},{384,0},{1,129},{129,257},{257,385},{3... | collective-permute-start | bytes 1572872 | tf_op jit(solution)/shard_map/ppermute | solution.py:16
  142.2 26.6 %collective-permute-start.22 = (bf16[256,1024]{1,0:T(8,128)(2,1)S(1)}, bf16[256,1024]{1,0:T(8,128)(2,1)S(1)}, u32[]{:S(2)}, u32[]{:S(2)}) collective-permute-start(bf16[256,1024]{1,0:T(8,128)(2,1)S(1)} %convolution_convert_fusion.1), channel_id=1, source_target_pairs={{0,256},{128,384},{256,0},{384,128},{1,257},{129,385},{257,1},{385... | collective-permute-start | bytes 1572872 | tf_op jit(solution)/shard_map/ppermute | solution.py:16
  147.9 4.2 %collective-permute-start.13 = (bf16[128,256]{0,1:T(8,128)(2,1)S(1)}, bf16[128,256]{0,1:T(8,128)(2,1)S(1)}, u32[]{:S(2)}, u32[]{:S(2)}) collective-permute-start(bf16[128,256]{0,1:T(8,128)(2,1)S(1)} %constant_dynamic-slice_fusion), channel_id=1, source_target_pairs={{0,1},{1,0},{2,3},{3,2},{4,5},{5,4},{6,7},{7,6},{8,9},{9,8},{10,11... | collective-permute-start | bytes 196616 | tf_op jit(solution)/shard_map/ppermute | solution.py:16
  150.1 20.6 %collective-permute-start.23 = (bf16[256,1024]{1,0:T(8,128)(2,1)S(1)}, bf16[256,1024]{1,0:T(8,128)(2,1)S(1)}, u32[]{:S(2)}, u32[]{:S(2)}) collective-permute-start(bf16[256,1024]{1,0:T(8,128)(2,1)S(1)} %convolution_convert_fusion), channel_id=1, source_target_pairs={{0,384},{128,0},{256,128},{384,256},{1,385},{129,1},{257,129},{385... | collective-permute-start | bytes 1572872 | tf_op jit(solution)/shard_map/ppermute | solution.py:16
  156.4 16.1 %collective-permute-start.15 = (bf16[32,4096]{1,0:T(8,128)(2,1)S(1)}, bf16[32,4096]{1,0:T(8,128)(2,1)S(1)}, u32[]{:S(2)}, u32[]{:S(2)}) collective-permute-start(bf16[32,4096]{1,0:T(8,128)(2,1)S(1)} %get-tuple-element.2), channel_id=1, source_target_pairs={{0,2},{2,4},{4,6},{6,0},{1,3},{3,5},{5,7},{7,1},{8,10},{10,12},{12... | collective-permute-start | bytes 786440 | tf_op jit(solution)/shard_map/ppermute | solution.py:16
  160.6 12.6 %collective-permute-start.16 = (bf16[32,4096]{1,0:T(8,128)(2,1)S(1)}, bf16[32,4096]{1,0:T(8,128)(2,1)S(1)}, u32[]{:S(2)}, u32[]{:S(2)}) collective-permute-start(bf16[32,4096]{1,0:T(8,128)(2,1)S(1)} %get-tuple-element.4), channel_id=1, source_target_pairs={{0,4},{2,6},{4,0},{6,2},{1,5},{3,7},{5,1},{7,3},{8,12},{10,14},{12... | collective-permute-start | bytes 786440 | tf_op jit(solution)/shard_map/ppermute | solution.py:16
  163.5 14.6 %collective-permute-start.17 = (bf16[32,4096]{1,0:T(8,128)(2,1)S(1)}, bf16[32,4096]{1,0:T(8,128)(2,1)S(1)}, u32[]{:S(2)}, u32[]{:S(2)}) collective-permute-start(bf16[32,4096]{1,0:T(8,128)(2,1)S(1)} %get-tuple-element.3), channel_id=1, source_target_pairs={{0,6},{2,0},{4,2},{6,4},{1,7},{3,1},{5,3},{7,5},{8,14},{10,8},{12,... | collective-permute-start | bytes 786440 | tf_op jit(solution)/shard_map/ppermute | solution.py:16
  178.2 17.3 %collective-permute-start.18 = (bf16[8,4096]{1,0:T(8,128)(2,1)S(1)}, bf16[8,4096]{1,0:T(8,128)(2,1)S(1)}, u32[]{:S(2)}, u32[]{:S(2)}) collective-permute-start(bf16[8,4096]{1,0:T(8,128)(2,1)S(1)} %get-tuple-element.8), channel_id=1, source_target_pairs={{0,8},{8,16},{16,24},{24,0},{1,9},{9,17},{17,25},{25,1},{2,10},{10... | collective-permute-start | bytes 196616 | tf_op jit(solution)/shard_map/ppermute | solution.py:16
  182.1 19.2 %collective-permute-start.19 = (bf16[8,4096]{1,0:T(8,128)(2,1)S(1)}, bf16[8,4096]{1,0:T(8,128)(2,1)S(1)}, u32[]{:S(2)}, u32[]{:S(2)}) collective-permute-start(bf16[8,4096]{1,0:T(8,128)(2,1)S(1)} %get-tuple-element.10), channel_id=1, source_target_pairs={{0,16},{8,24},{16,0},{24,8},{1,17},{9,25},{17,1},{25,9},{2,18},{10... | collective-permute-start | bytes 196616 | tf_op jit(solution)/shard_map/ppermute | solution.py:16
  188.3 13.0 %collective-permute-start.20 = (bf16[8,4096]{1,0:T(8,128)(2,1)S(1)}, bf16[8,4096]{1,0:T(8,128)(2,1)S(1)}, u32[]{:S(2)}, u32[]{:S(2)}) collective-permute-start(bf16[8,4096]{1,0:T(8,128)(2,1)S(1)} %get-tuple-element.9), channel_id=1, source_target_pairs={{0,24},{8,0},{16,8},{24,16},{1,25},{9,1},{17,9},{25,17},{2,26},{10... | collective-permute-start | bytes 196616 | tf_op jit(solution)/shard_map/ppermute | solution.py:16
  191.7 14.9 %collective-permute-start.24 = (bf16[256,256]{1,0:T(8,128)(2,1)S(1)}, bf16[256,256]{1,0:T(8,128)(2,1)S(1)}, u32[]{:S(2)}, u32[]{:S(2)}) collective-permute-start(bf16[256,256]{1,0:T(8,128)(2,1)S(1)} %get-tuple-element.5), channel_id=1, source_target_pairs={{0,32},{32,64},{64,96},{96,0},{1,33},{33,65},{65,97},{97,1},{2,34}... | collective-permute-start | bytes 393224 | tf_op jit(solution)/shard_map/ppermute | solution.py:16
  193.6 13.7 %collective-permute-start.25 = (bf16[256,256]{1,0:T(8,128)(2,1)S(1)}, bf16[256,256]{1,0:T(8,128)(2,1)S(1)}, u32[]{:S(2)}, u32[]{:S(2)}) collective-permute-start(bf16[256,256]{1,0:T(8,128)(2,1)S(1)} %get-tuple-element.7), channel_id=1, source_target_pairs={{0,64},{32,96},{64,0},{96,32},{1,65},{33,97},{65,1},{97,33},{2,66}... | collective-permute-start | bytes 393224 | tf_op jit(solution)/shard_map/ppermute | solution.py:16
  195.6 12.0 %collective-permute-start.26 = (bf16[256,256]{1,0:T(8,128)(2,1)S(1)}, bf16[256,256]{1,0:T(8,128)(2,1)S(1)}, u32[]{:S(2)}, u32[]{:S(2)}) collective-permute-start(bf16[256,256]{1,0:T(8,128)(2,1)S(1)} %get-tuple-element.6), channel_id=1, source_target_pairs={{0,96},{32,0},{64,32},{96,64},{1,97},{33,1},{65,33},{97,65},{2,98}... | collective-permute-start | bytes 393224 | tf_op jit(solution)/shard_map/ppermute | solution.py:16
  202.0 12.7 %all-to-all-start.2 = ((bf16[16,8,256]{2,1,0:T(8,128)(2,1)}), bf16[16,8,256]{2,1,0:T(8,128)(2,1)S(1)}, u32[]{:S(2)}, u32[]{:S(2)}) async-start(bf16[16,8,256]{2,1,0:T(8,128)(2,1)} %bitcast.5), calls=%async_computation.2 | async-start | bytes 131072 | tf_op jit(solution)/shard_map/all_to_all | solution.py:101

commit v2 on v0

v2 whole, which is shorter than its diff:
```python
import math

import jax
import jax.numpy as jnp
from jax import lax
from jax.experimental import pallas as pl
from jax.experimental.pallas import tpu as pltpu
from jax.sharding import Mesh, PartitionSpec as P

ROWS = ("zh", "x", "c")
FEATS = ("y", "zl")
COLUMN = ("zh", "zl")
BF = jnp.bfloat16
F32 = jnp.float32


def shift(value, axis, step):
    n = lax.axis_size(axis)
    return lax.ppermute(value, axis, [(i, (i + step) % n) for i in range(n)])


def exchange(blocks, axis):
    return lax.all_to_all(blocks, axis, 0, 0, tiled=True)


def gather(value, axis):
    n = lax.axis_size(axis)
    return exchange(jnp.broadcast_to(value, (n, *value.shape)), axis)


def dot(a, b, over_a, over_b):
    return lax.dot_general(a, b, (((over_a,), (over_b,)), ((), ())), preferred_element_type=F32)


def call(kernel, outs, flops, place, *arrays):
    size = sum(a.size * a.dtype.itemsize for a in (*arrays, *outs))
    return pl.pallas_call(
        kernel,
        out_shape=outs,
        in_specs=[pl.BlockSpec(memory_space=pltpu.SMEM)] + [pl.BlockSpec(memory_space=pltpu.VMEM)] * len(arrays),
        out_specs=[pl.BlockSpec(memory_space=pltpu.VMEM)] * len(outs),
        cost_estimate=pl.CostEstimate(flops=flops, bytes_accessed=size, transcendentals=0),
        compiler_params=pltpu.CompilerParams(vmem_limit_bytes=32 * 2**20),
    )(place.reshape(1), *arrays)


def in_x_order(w_ref, half):
    n_zh, _, n_x = w_ref.shape[:3]
    return jnp.concatenate([w_ref[z, half, x] for x in range(n_x) for z in range(n_zh)], axis=0)


def passage_kernel(zl_ref, w_ref, near_ref, far_ref, own_ref, send_ref):
    n_zl, width = send_ref.shape[0] + 1, own_ref.shape[1]
    w_near, w_far = in_x_order(w_ref, 0), in_x_order(w_ref, 1)
    for t in range(n_zl):
        at = pl.ds(pl.multiple_of((zl_ref[0] + t) % n_zl * width, width), width)
        block = dot(w_near, near_ref[:, at], 0, 0) + dot(w_far, far_ref[:, at], 0, 0)
        if t == 0:
            own_ref[...] = block
        else:
            send_ref[t - 1] = block.astype(BF)


def query_kernel(x_ref, w_ref, other_ref, p_ref, p_other_ref, own_ref, send_ref):
    n_zh, _, n_x = w_ref.shape[:3]
    for x in range(n_x):
        mine = jnp.concatenate([w_ref[z, 0, x] for z in range(n_zh)], axis=0)
        theirs = jnp.concatenate([other_ref[z, x] for z in range(n_zh)], axis=0)
        block = dot(mine, p_ref[...], 1, 0) + dot(theirs, p_other_ref[...], 1, 0)
        send_ref[x] = block.astype(BF)

        @pl.when(x_ref[0] == x)
        def _():
            own_ref[...] = block


def total_kernel(x_ref, own_ref, moved_ref, out_ref):
    n_x = moved_ref.shape[0]
    n_blocks, band, width = out_ref.shape
    n_zl = own_ref.shape[1] // width
    for z in range(n_blocks // n_zl):
        rows = pl.ds(z * band, band)
        total = own_ref[rows, :]
        for x in range(n_x):
            total = total + jnp.where(x_ref[0] == x, 0.0, moved_ref[x, rows, :].astype(F32))
        for l in range(n_zl):
            out_ref[z * n_zl + l] = total[:, l * width : (l + 1) * width].astype(BF)


def per_device(queries, passages, positive):
    rows, width = queries.shape
    count = passages.shape[0]
    n_x, n_y, n_zh, n_zl = (lax.axis_size(a) for a in ("x", "y", "zh", "zl"))
    assert n_zh == n_y
    devs = lax.axis_size(ROWS)
    strip = width * n_zl
    scale = 2.0 / math.sqrt(strip * n_y)
    band = rows // n_zl
    n_q = 2 * n_x * band
    n_half = band * n_zh * n_x
    core, x, y, zl = (lax.axis_index(a) for a in ("c", "x", "y", "zl"))
    dev = lax.axis_index(ROWS)

    bands = jnp.broadcast_to(queries.reshape(n_zl, band, width), (n_zh, n_zl, band, width))
    mine = exchange(bands.reshape(n_zh * n_zl, band, width), COLUMN).reshape(n_zh, n_zl, band, width)
    mine = mine.transpose(0, 2, 1, 3).reshape(n_zh * band, strip)
    near = gather(mine, "x").reshape(n_half, strip)

    p = jnp.zeros((count, strip), BF)
    for t in range(n_zl):
        block = passages if t == 0 else shift(passages, "zl", t)
        p = lax.dynamic_update_slice_in_dim(p, block, (zl - t) % n_zl * width, 1)
    near, p = lax.optimization_barrier((near, p))
    far = shift(near, "c", 1)
    p_other = shift(p, "c", 1)

    partial = jnp.stack([dot(near, p, 1, 1), dot(far, p, 1, 1)])
    partial = partial.reshape(2 * n_x, n_zh, band, count).transpose(1, 0, 2, 3)
    moved = exchange(partial.reshape(n_y, n_q, count), "y")
    logits = moved[0]
    for i in range(1, n_y):
        logits = logits + moved[i]
    logits = logits * scale

    top = jnp.max(logits, axis=1)
    exps = jnp.exp(logits - top[:, None])
    total = jnp.sum(exps, axis=1)

    def flip_cores(row_values):
        return jnp.where(core == 0, row_values, jnp.roll(row_values, n_q // 2))

    own_pos = lax.dynamic_slice_in_dim(positive, zl * band, band).astype(F32)
    note = jnp.concatenate([flip_cores(top), flip_cores(total), jnp.pad(own_pos, (0, 128 - band))])
    notes = exchange(jnp.broadcast_to(note, (devs, note.shape[0])), ("c", "x", "zh"))
    tops, totals = notes[:, :n_q], notes[:, n_q : 2 * n_q]
    pos = notes[:, 2 * n_q : 2 * n_q + band].reshape(2 * n_x, n_zh, band)
    pos = lax.dynamic_index_in_dim(pos, y, 1, keepdims=False).reshape(n_q).astype(jnp.int32)
    peak = jnp.max(tops, axis=0)
    denom = jnp.sum(totals * jnp.exp(tops - peak), axis=0)
    factor = jnp.exp(top - flip_cores(peak)) / flip_cores(denom)
    columns = lax.broadcasted_iota(jnp.int32, (n_q, count), 1) + dev * count
    onehot = (columns == flip_cores(pos)[:, None]).astype(F32)
    weights = (exps * factor[:, None] - onehot).astype(BF)
    weights = gather(weights, "y").reshape(n_zh, 2, n_x, band, count)
    w_other = shift(weights[:, 1], "c", 1)

    flops = 4 * n_half * count * strip
    by_x, chip = call(
        query_kernel,
        [jax.ShapeDtypeStruct((n_zh * band, strip), F32), jax.ShapeDtypeStruct((n_x, n_zh * band, strip), BF)],
        flops, x, weights, w_other, p, p_other,
    )
    moved = exchange(chip, "x")
    (back,) = call(
        total_kernel, [jax.ShapeDtypeStruct((n_zh * n_zl, band, width), BF)], 0, x, by_x, moved
    )

    passage_grad, ahead = call(
        passage_kernel,
        [jax.ShapeDtypeStruct((count, width), F32), jax.ShapeDtypeStruct((n_zl - 1, count, width), BF)],
        flops, zl, weights, near, far,
    )
    for t in range(1, n_zl):
        passage_grad = passage_grad + shift(ahead[t - 1], "zl", t).astype(F32)
    back, passage_grad = lax.optimization_barrier((back, passage_grad))

    back = exchange(back, COLUMN).reshape(n_zh, rows, width)
    query_grad = jnp.sum(back.astype(F32), axis=0)
    return query_grad.astype(BF), passage_grad.astype(BF)


def solution(mesh):
    fine = Mesh(mesh.devices.reshape(4, 4, 4, 4, 2), FEATS + ROWS)
    in_specs = (P(ROWS, FEATS), P(ROWS, FEATS), P(ROWS))
    out_specs = (P(ROWS, FEATS), P(ROWS, FEATS))
    return jax.shard_map(per_device, mesh=fine, in_specs=in_specs, out_specs=out_specs, check_vma=False)
```

time: 504 us -> 180 us (0.36)
  waiting for transfers between devices: 456 us -> 50.2 us
  blocking collectives: 0 us -> 55.7 us
  starting transfers between devices: 12.8 us -> 55 us
  between operations: 13.8 us -> 1.03 us
  matrix products: 12.8 us -> 0.96 us
  local copies, waits for them, and re-layouts: 2.37 us -> 8.22 us
    all_gather x2 -> x0, waiting for transfers between devices: 245 us -> none  [the longest x1 142 us: per_device(): lax.all_gather(queries, 'dev', axis=0, tiled=True)]
    psum x1 -> x0, waiting for transfers between devices: 209 us -> none  [per_device(): logits = lax.psum(partial_value, 'grp') * scale]
    all_to_all x0 -> x2, blocking collectives: none -> 55.7 us  [exchange(): return lax.all_to_all(blocks, axis, 0, 0, tiled=True)]
    all_to_all x1 -> x5, waiting for transfers between devices: 0.01 us -> 36.2 us  [exchange(): return lax.all_to_all(blocks, axis, 0, 0, tiled=True)]
    ppermute x0 -> x9, starting transfers between devices: none -> 26.9 us  [shift(): return lax.ppermute(value, axis, [(i, (i + step) % n) for i in range(n)])]
    all_to_all x1 -> x5, starting transfers between devices: 12.7 us -> 28.1 us  [exchange(): return lax.all_to_all(blocks, axis, 0, 0, tiled=True)]
    ppermute x0 -> x9, waiting for transfers between devices: none -> 14 us  [shift(): return lax.ppermute(value, axis, [(i, (i + step) % n) for i in range(n)])]
    dot_general x3 -> x2, matrix products: 12.8 us -> 0.96 us  [dot(): lax.dot_general(a, b, (((over_a,), (over_b,)), ((), ())), preferred_eleme...]
  transfers between devices with their start and end apart: 4 -> 14, of which waited for: 3 -> 10; matrix products, arithmetic and copies ran while one was open for 1% -> 1% of each run, Pallas kernels for 0% -> 0%
where the time goes in v2:
time: 180 us
  blocking collectives  55.7 us (31%)
  starting transfers between devices  55 us (31%)
  waiting for transfers between devices  50.2 us (28%)
  local copies, waits for them, and re-layouts  8.22 us (5%)
  Pallas kernels  4.5 us (2%)
  other arithmetic  3.96 us (2%)
    all_to_all x2, blocking collectives, exchange(): return lax.all_to_all(blocks, axis, 0, 0, tiled=True)  55.7 us
    all_to_all x5, waiting for transfers between devices, exchange(): return lax.all_to_all(blocks, axis, 0, 0, tiled=True)  36.2 us
    all_to_all x5, starting transfers between devices, exchange(): return lax.all_to_all(blocks, axis, 0, 0, tiled=True)  28.1 us
    ppermute x9, starting transfers between devices, shift(): return lax.ppermute(value, axis, [(i, (i + step) % n) for i in range(n)])  26.9 us
    ppermute x9, waiting for transfers between devices, shift(): return lax.ppermute(value, axis, [(i, (i + step) % n) for i in range(n)])  14 us
    pallas_call x3, Pallas kernels, call(): pl.pallas_call(kernel, out_shape=outs, in_specs=[pl.BlockSpec(memory_spac...  4.5 us
  transfers between devices with their start and end apart: 14, of which 10 were waited for; matrix products, arithmetic and copies ran while one was open for 1% of the time, Pallas kernels for 0%

profile of v2, /device:TPU:6, one launch (start us, length us, event | category | flops | bytes accessed | tf_op | source)
XLA Modules:
  0.0 179.5 jit_solution(14497402873724727055)
XLA Ops:
  0.6 0.9 broadcast_in_dim.19
  1.5 33.4 %all_to_all.39 = bf16[16,32,256]{2,1,0:T(8,128)(2,1)S(1)} all-to-all(bf16[16,32,256]{2,1,0:T(8,128)(2,1)S(1)} %bitcast.57), channel_id=1, replica_groups=mesh['y'=4,'zl'=4,'zh'=4,'x'=4,'c'=2] {'zh','zl'}, dimensions={0} | all-to-all | bytes 524288 | tf_op jit(solution)/shard_map/all_to_all | solution.py:23
  35.1 1.1 broadcast_in_dim.20
  36.2 4.9 %all-to-all-start.1 = ((bf16[4,128,1024]{2,1,0:T(8,128)(2,1)}), bf16[4,128,1024]{2,1,0:T(8,128)(2,1)S(1)}, u32[]{:S(2)}, u32[]{:S(2)}) async-start(bf16[4,128,1024]{2,1,0:T(8,128)(2,1)} %broadcast_in_dim.20), calls=%async_computation.1 | async-start | bytes 2097152 | tf_op jit(solution)/shard_map/all_to_all | solution.py:23
  41.1 3.4 %collective-permute-start = (bf16[256,256]{1,0:T(8,128)(2,1)S(1)}, bf16[256,256]{1,0:T(8,128)(2,1)S(1)}, u32[]{:S(2)}, u32[]{:S(2)}) collective-permute-start(bf16[256,256]{1,0:T(8,128)(2,1)S(1)} %copy-done.3), channel_id=1, source_target_pairs={{0,32},{32,64},{64,96},{96,0},{1,33},{33,65},{65,97},{97,1},{2,34}... | collective-permute-start | bytes 393224 | tf_op jit(solution)/shard_map/ppermute | solution.py:19
  44.5 4.1 %collective-permute-start.1 = (bf16[256,256]{1,0:T(8,128)(2,1)S(1)}, bf16[256,256]{1,0:T(8,128)(2,1)S(1)}, u32[]{:S(2)}, u32[]{:S(2)}) collective-permute-start(bf16[256,256]{1,0:T(8,128)(2,1)S(1)} %copy-done.3), channel_id=1, source_target_pairs={{0,64},{32,96},{64,0},{96,32},{1,65},{33,97},{65,1},{97,33},{2,66}... | collective-permute-start | bytes 393224 | tf_op jit(solution)/shard_map/ppermute | solution.py:19
  48.6 3.8 %collective-permute-start.2 = (bf16[256,256]{1,0:T(8,128)(2,1)S(1)}, bf16[256,256]{1,0:T(8,128)(2,1)S(1)}, u32[]{:S(2)}, u32[]{:S(2)}) collective-permute-start(bf16[256,256]{1,0:T(8,128)(2,1)S(1)} %copy-done.3), channel_id=1, source_target_pairs={{0,96},{32,0},{64,32},{96,64},{1,97},{33,1},{65,33},{97,65},{2,98}... | collective-permute-start | bytes 393224 | tf_op jit(solution)/shard_map/ppermute | solution.py:19
  52.6 2.5 %collective-permute-done.1 = bf16[256,256]{1,0:T(8,128)(2,1)S(1)} collective-permute-done((bf16[256,256]{1,0:T(8,128)(2,1)S(1)}, bf16[256,256]{1,0:T(8,128)(2,1)S(1)}, u32[]{:S(2)}, u32[]{:S(2)}) %collective-permute-start.1) | collective-permute-done | bytes 131104 | tf_op jit(solution)/shard_map/ppermute | solution.py:19
  55.1 1.1 collective-permute-done.2
  56.2 1.9 %collective-permute-start.3 = (bf16[512,1024]{1,0:T(8,128)(2,1)S(1)}, bf16[512,1024]{1,0:T(8,128)(2,1)S(1)}, u32[]{:S(2)}, u32[]{:S(2)}) collective-permute-start(bf16[512,1024]{1,0:T(8,128)(2,1)S(1)} %bitcast.47), channel_id=1, source_target_pairs={{0,1},{1,0},{2,3},{3,2},{4,5},{5,4},{6,7},{7,6},{8,9},{9,8},{10,11... | collective-permute-start | bytes 3145736 | tf_op jit(solution)/shard_map/ppermute | solution.py:19
  58.6 2.1 %collective-permute-done.3.far_ref = bf16[512,1024]{1,0:T(8,128)(2,1)S(1)} collective-permute-done((bf16[512,1024]{1,0:T(8,128)(2,1)S(1)}, bf16[512,1024]{1,0:T(8,128)(2,1)S(1)}, u32[]{:S(2)}, u32[]{:S(2)}) %collective-permute-start.3) | collective-permute-done | bytes 1048608 | tf_op jit(solution)/shard_map/ppermute | solution.py:19
  61.3 1.1 copy.9
  62.4 4.5 %all-to-all-start.2 = ((f32[4,256,256]{2,1,0:T(8,128)}), f32[4,256,256]{2,1,0:T(8,128)}, u32[]{:S(2)}, u32[]{:S(2)}) async-start(f32[4,256,256]{2,1,0:T(8,128)} %bitcast.53), calls=%async_computation.2 | async-start | bytes 2097152 | tf_op jit(solution)/shard_map/all_to_all | solution.py:23
  67.6 14.8 %all-to-all-done.2 = f32[4,256,256]{2,1,0:T(8,128)} async-done(((f32[4,256,256]{2,1,0:T(8,128)}), f32[4,256,256]{2,1,0:T(8,128)}, u32[]{:S(2)}, u32[]{:S(2)}) %all-to-all-start.2) | async-done | bytes 1048608 | tf_op jit(solution)/shard_map/all_to_all | solution.py:23
  82.4 1.3 fusion.8
  84.7 9.0 %all-to-all-start.3 = ((f32[32,1,640]{2,1,0:T(1,128)}), f32[32,1,640]{2,1,0:T(1,128)S(1)}, u32[]{:S(2)}, u32[]{:S(2)}) async-start(f32[32,1,640]{2,1,0:T(1,128)} %broadcast_in_dim.22), calls=%async_computation.3 | async-start | bytes 163840 | tf_op jit(solution)/shard_map/all_to_all | solution.py:23
  93.7 13.4 %all-to-all-done.3 = f32[32,1,640]{2,1,0:T(1,128)S(1)} async-done(((f32[32,1,640]{2,1,0:T(1,128)}), f32[32,1,640]{2,1,0:T(1,128)S(1)}, u32[]{:S(2)}, u32[]{:S(2)}) %all-to-all-start.3) | async-done | bytes 81952 | tf_op jit(solution)/shard_map/all_to_all | solution.py:23
  109.7 3.5 %all-to-all-start.4 = ((bf16[4,256,256]{2,1,0:T(8,128)(2,1)}), bf16[4,256,256]{2,1,0:T(8,128)(2,1)S(1)}, u32[]{:S(2)}, u32[]{:S(2)}) async-start(bf16[4,256,256]{2,1,0:T(8,128)(2,1)} %broadcast_in_dim.23), calls=%async_computation.4 | async-start | bytes 1048576 | tf_op jit(solution)/shard_map/all_to_all | solution.py:23
  113.2 2.0 %collective-permute-start.5 = (bf16[256,1024]{1,0:T(8,128)(2,1)S(1)}, bf16[256,1024]{1,0:T(8,128)(2,1)}, u32[]{:S(2)}, u32[]{:S(2)}) collective-permute-start(bf16[256,1024]{1,0:T(8,128)(2,1)S(1)} %constant_dynamic-update-slice_fusion.p_ref), channel_id=1, source_target_pairs={{0,1},{1,0},{2,3},{3,2},{4,5},{5,4},{6,7},{7,6},{8,9},{9,8},{10,11... | collective-permute-start | bytes 1572872 | tf_op jit(solution)/shard_map/ppermute | solution.py:19
  115.2 8.0 %all-to-all-done.4 = bf16[4,256,256]{2,1,0:T(8,128)(2,1)S(1)} async-done(((bf16[4,256,256]{2,1,0:T(8,128)(2,1)}), bf16[4,256,256]{2,1,0:T(8,128)(2,1)S(1)}, u32[]{:S(2)}, u32[]{:S(2)}) %all-to-all-start.4) | async-done | bytes 524320 | tf_op jit(solution)/shard_map/all_to_all | solution.py:23
  123.2 1.9 %collective-permute-start.4 = (bf16[4,4,32,256]{3,2,1,0:T(8,128)(2,1)S(1)}, bf16[4,4,32,256]{3,2,1,0:T(8,128)(2,1)S(1)}, u32[]{:S(2)}, u32[]{:S(2)}) collective-permute-start(bf16[4,4,32,256]{3,2,1,0:T(8,128)(2,1)S(1)} %slice_bitcast_fusion), channel_id=1, source_target_pairs={{0,1},{1,0},{2,3},{3,2},{4,5},{5,4},{6,7},{7,6},{8,9},{9,8},{10,11... | collective-permute-start | bytes 786440 | tf_op jit(solution)/shard_map/ppermute | solution.py:19
  125.1 1.5 collective-permute-done.4.other_ref
  126.6 2.3 %shard_map.50 = (f32[128,1024]{1,0:T(8,128)S(1)}, bf16[4,128,1024]{2,1,0:T(8,128)(2,1)S(1)}) custom-call(s32[1]{0:T(128)} %bitcast.x_ref, bf16[4,2,4,32,256]{4,3,2,1,0:T(8,128)(2,1)S(1)} %bitcast.51, bf16[4,4,32,256]{3,2,1,0:T(8,128)(2,1)S(1)} %collective-permute-done.4.other_ref, bf16[256,1024]{1,0:T(8,128)(2,1)S(1)} %constant_dynamic-update-slice_fusion.p_ref, ...), custom_call_target="tpu_custom_call" | custom-call | flops 536870912 | bytes 3407872 | tf_op jit(solution)/shard_map/pallas_call | solution.py:37
  128.9 1.0 copy-done
  130.7 6.3 %all-to-all-start.5 = ((bf16[4,128,1024]{2,1,0:T(8,128)(2,1)}), bf16[4,128,1024]{2,1,0:T(8,128)(2,1)}, u32[]{:S(2)}, u32[]{:S(2)}) async-start(bf16[4,128,1024]{2,1,0:T(8,128)(2,1)} %copy-done), calls=%async_computation.5 | async-start | bytes 2097152 | tf_op jit(solution)/shard_map/all_to_all | solution.py:23
  137.8 3.6 %collective-permute-start.6 = (bf16[256,256]{1,0:T(8,128)(2,1)S(1)}, bf16[256,256]{1,0:T(8,128)(2,1)S(1)}, u32[]{:S(2)}, u32[]{:S(2)}) collective-permute-start(bf16[256,256]{1,0:T(8,128)(2,1)S(1)} %get-tuple-element.24), channel_id=1, source_target_pairs={{0,32},{32,64},{64,96},{96,0},{1,33},{33,65},{65,97},{97,1},{2,34}... | collective-permute-start | bytes 393224 | tf_op jit(solution)/shard_map/ppermute | solution.py:19
  141.4 3.6 %collective-permute-start.7 = (bf16[256,256]{1,0:T(8,128)(2,1)S(1)}, bf16[256,256]{1,0:T(8,128)(2,1)S(1)}, u32[]{:S(2)}, u32[]{:S(2)}) collective-permute-start(bf16[256,256]{1,0:T(8,128)(2,1)S(1)} %get-tuple-element.26), channel_id=1, source_target_pairs={{0,64},{32,96},{64,0},{96,32},{1,65},{33,97},{65,1},{97,33},{2,66}... | collective-permute-start | bytes 393224 | tf_op jit(solution)/shard_map/ppermute | solution.py:19
  145.1 2.5 %collective-permute-start.8 = (bf16[256,256]{1,0:T(8,128)(2,1)S(1)}, bf16[256,256]{1,0:T(8,128)(2,1)S(1)}, u32[]{:S(2)}, u32[]{:S(2)}) collective-permute-start(bf16[256,256]{1,0:T(8,128)(2,1)S(1)} %get-tuple-element.25), channel_id=1, source_target_pairs={{0,96},{32,0},{64,32},{96,64},{1,97},{33,1},{65,33},{97,65},{2,98}... | collective-permute-start | bytes 393224 | tf_op jit(solution)/shard_map/ppermute | solution.py:19
  147.9 4.8 %collective-permute-done.7 = bf16[256,256]{1,0:T(8,128)(2,1)S(1)} collective-permute-done((bf16[256,256]{1,0:T(8,128)(2,1)S(1)}, bf16[256,256]{1,0:T(8,128)(2,1)S(1)}, u32[]{:S(2)}, u32[]{:S(2)}) %collective-permute-start.7) | collective-permute-done | bytes 131104 | tf_op jit(solution)/shard_map/ppermute | solution.py:19
  152.7 1.7 collective-permute-done.8
  155.1 1.4 shard_map.51
  156.5 22.3 %all_to_all.40 = bf16[16,32,256]{2,1,0:T(8,128)(2,1)S(1)} all-to-all(bf16[16,32,256]{2,1,0:T(8,128)(2,1)S(1)} %shard_map.51), channel_id=1, replica_groups=mesh['y'=4,'zl'=4,'zh'=4,'x'=4,'c'=2] {'zh','zl'}, dimensions={0} | all-to-all | bytes 524288 | tf_op jit(solution)/shard_map/all_to_all | solution.py:23
  (53 shorter events, 8.8 us)
Async XLA Ops:
  36.2 4.9 %copy-start.3 = (bf16[256,256]{1,0:T(8,128)(2,1)S(1)}, bf16[256,256]{1,0:T(8,128)(2,1)}, u32[]{:S(2)}) copy-start(bf16[256,256]{1,0:T(8,128)(2,1)} %param.4) | copy-start | bytes 393220
  36.2 20.0 %all-to-all-start.1 = ((bf16[4,128,1024]{2,1,0:T(8,128)(2,1)}), bf16[4,128,1024]{2,1,0:T(8,128)(2,1)S(1)}, u32[]{:S(2)}, u32[]{:S(2)}) async-start(bf16[4,128,1024]{2,1,0:T(8,128)(2,1)} %broadcast_in_dim.20), calls=%async_computation.1 | async-start | bytes 2097152 | tf_op jit(solution)/shard_map/all_to_all | solution.py:23
  41.1 11.5 %collective-permute-start = (bf16[256,256]{1,0:T(8,128)(2,1)S(1)}, bf16[256,256]{1,0:T(8,128)(2,1)S(1)}, u32[]{:S(2)}, u32[]{:S(2)}) collective-permute-start(bf16[256,256]{1,0:T(8,128)(2,1)S(1)} %copy-done.3), channel_id=1, source_target_pairs={{0,32},{32,64},{64,96},{96,0},{1,33},{33,65},{65,97},{97,1},{2,34}... | collective-permute-start | bytes 393224 | tf_op jit(solution)/shard_map/ppermute | solution.py:19
  44.5 10.6 %collective-permute-start.1 = (bf16[256,256]{1,0:T(8,128)(2,1)S(1)}, bf16[256,256]{1,0:T(8,128)(2,1)S(1)}, u32[]{:S(2)}, u32[]{:S(2)}) collective-permute-start(bf16[256,256]{1,0:T(8,128)(2,1)S(1)} %copy-done.3), channel_id=1, source_target_pairs={{0,64},{32,96},{64,0},{96,32},{1,65},{33,97},{65,1},{97,33},{2,66}... | collective-permute-start | bytes 393224 | tf_op jit(solution)/shard_map/ppermute | solution.py:19
  48.6 7.6 %collective-permute-start.2 = (bf16[256,256]{1,0:T(8,128)(2,1)S(1)}, bf16[256,256]{1,0:T(8,128)(2,1)S(1)}, u32[]{:S(2)}, u32[]{:S(2)}) collective-permute-start(bf16[256,256]{1,0:T(8,128)(2,1)S(1)} %copy-done.3), channel_id=1, source_target_pairs={{0,96},{32,0},{64,32},{96,64},{1,97},{33,1},{65,33},{97,65},{2,98}... | collective-permute-start | bytes 393224 | tf_op jit(solution)/shard_map/ppermute | solution.py:19
  56.2 4.6 %collective-permute-start.3 = (bf16[512,1024]{1,0:T(8,128)(2,1)S(1)}, bf16[512,1024]{1,0:T(8,128)(2,1)S(1)}, u32[]{:S(2)}, u32[]{:S(2)}) collective-permute-start(bf16[512,1024]{1,0:T(8,128)(2,1)S(1)} %bitcast.47), channel_id=1, source_target_pairs={{0,1},{1,0},{2,3},{3,2},{4,5},{5,4},{6,7},{7,6},{8,9},{9,8},{10,11... | collective-permute-start | bytes 3145736 | tf_op jit(solution)/shard_map/ppermute | solution.py:19
  62.4 20.0 %all-to-all-start.2 = ((f32[4,256,256]{2,1,0:T(8,128)}), f32[4,256,256]{2,1,0:T(8,128)}, u32[]{:S(2)}, u32[]{:S(2)}) async-start(f32[4,256,256]{2,1,0:T(8,128)} %bitcast.53), calls=%async_computation.2 | async-start | bytes 2097152 | tf_op jit(solution)/shard_map/all_to_all | solution.py:23
  66.9 0.7 copy-start.4
  84.7 22.4 %all-to-all-start.3 = ((f32[32,1,640]{2,1,0:T(1,128)}), f32[32,1,640]{2,1,0:T(1,128)S(1)}, u32[]{:S(2)}, u32[]{:S(2)}) async-start(f32[32,1,640]{2,1,0:T(1,128)} %broadcast_in_dim.22), calls=%async_computation.3 | async-start | bytes 163840 | tf_op jit(solution)/shard_map/all_to_all | solution.py:23
  109.7 13.5 %all-to-all-start.4 = ((bf16[4,256,256]{2,1,0:T(8,128)(2,1)}), bf16[4,256,256]{2,1,0:T(8,128)(2,1)S(1)}, u32[]{:S(2)}, u32[]{:S(2)}) async-start(bf16[4,256,256]{2,1,0:T(8,128)(2,1)} %broadcast_in_dim.23), calls=%async_computation.4 | async-start | bytes 1048576 | tf_op jit(solution)/shard_map/all_to_all | solution.py:23
  113.2 12.0 %collective-permute-start.5 = (bf16[256,1024]{1,0:T(8,128)(2,1)S(1)}, bf16[256,1024]{1,0:T(8,128)(2,1)}, u32[]{:S(2)}, u32[]{:S(2)}) collective-permute-start(bf16[256,1024]{1,0:T(8,128)(2,1)S(1)} %constant_dynamic-update-slice_fusion.p_ref), channel_id=1, source_target_pairs={{0,1},{1,0},{2,3},{3,2},{4,5},{5,4},{6,7},{7,6},{8,9},{9,8},{10,11... | collective-permute-start | bytes 1572872 | tf_op jit(solution)/shard_map/ppermute | solution.py:19
  123.2 3.4 %collective-permute-start.4 = (bf16[4,4,32,256]{3,2,1,0:T(8,128)(2,1)S(1)}, bf16[4,4,32,256]{3,2,1,0:T(8,128)(2,1)S(1)}, u32[]{:S(2)}, u32[]{:S(2)}) collective-permute-start(bf16[4,4,32,256]{3,2,1,0:T(8,128)(2,1)S(1)} %slice_bitcast_fusion), channel_id=1, source_target_pairs={{0,1},{1,0},{2,3},{3,2},{4,5},{5,4},{6,7},{7,6},{8,9},{9,8},{10,11... | collective-permute-start | bytes 786440 | tf_op jit(solution)/shard_map/ppermute | solution.py:19
  128.9 1.0 copy-start
  129.9 0.8 copy-start.1
  130.7 24.4 %all-to-all-start.5 = ((bf16[4,128,1024]{2,1,0:T(8,128)(2,1)}), bf16[4,128,1024]{2,1,0:T(8,128)(2,1)}, u32[]{:S(2)}, u32[]{:S(2)}) async-start(bf16[4,128,1024]{2,1,0:T(8,128)(2,1)} %copy-done), calls=%async_computation.5 | async-start | bytes 2097152 | tf_op jit(solution)/shard_map/all_to_all | solution.py:23
  137.8 17.3 %copy-start.2 = (f32[128,1024]{1,0:T(8,128)S(1)}, f32[128,1024]{1,0:T(8,128)}, u32[]{:S(2)}) copy-start(f32[128,1024]{1,0:T(8,128)} %copy-done.1) | copy-start | bytes 1572868
  137.8 10.0 %collective-permute-start.6 = (bf16[256,256]{1,0:T(8,128)(2,1)S(1)}, bf16[256,256]{1,0:T(8,128)(2,1)S(1)}, u32[]{:S(2)}, u32[]{:S(2)}) collective-permute-start(bf16[256,256]{1,0:T(8,128)(2,1)S(1)} %get-tuple-element.24), channel_id=1, source_target_pairs={{0,32},{32,64},{64,96},{96,0},{1,33},{33,65},{65,97},{97,1},{2,34}... | collective-permute-start | bytes 393224 | tf_op jit(solution)/shard_map/ppermute | solution.py:19
  141.4 11.3 %collective-permute-start.7 = (bf16[256,256]{1,0:T(8,128)(2,1)S(1)}, bf16[256,256]{1,0:T(8,128)(2,1)S(1)}, u32[]{:S(2)}, u32[]{:S(2)}) collective-permute-start(bf16[256,256]{1,0:T(8,128)(2,1)S(1)} %get-tuple-element.26), channel_id=1, source_target_pairs={{0,64},{32,96},{64,0},{96,32},{1,65},{33,97},{65,1},{97,33},{2,66}... | collective-permute-start | bytes 393224 | tf_op jit(solution)/shard_map/ppermute | solution.py:19
  145.1 9.3 %collective-permute-start.8 = (bf16[256,256]{1,0:T(8,128)(2,1)S(1)}, bf16[256,256]{1,0:T(8,128)(2,1)S(1)}, u32[]{:S(2)}, u32[]{:S(2)}) collective-permute-start(bf16[256,256]{1,0:T(8,128)(2,1)S(1)} %get-tuple-element.25), channel_id=1, source_target_pairs={{0,96},{32,0},{64,32},{96,64},{1,97},{33,1},{65,33},{97,65},{2,98}... | collective-permute-start | bytes 393224 | tf_op jit(solution)/shard_map/ppermute | solution.py:19

commit v3 on v2

v3 whole, which is shorter than its diff:
```python
import math

import jax
import jax.numpy as jnp
from jax import lax
from jax.experimental import pallas as pl
from jax.experimental.pallas import tpu as pltpu
from jax.sharding import Mesh, PartitionSpec as P

ROWS = ("zh", "x", "c")
FEATS = ("y", "zl")
COLUMN = ("zh", "zl")
BF = jnp.bfloat16
F32 = jnp.float32
BAND = 32


def shift(value, axis, step):
    n = lax.axis_size(axis)
    return lax.ppermute(value, axis, [(i, (i + step) % n) for i in range(n)])


def exchange(blocks, axis):
    return lax.all_to_all(blocks, axis, 0, 0, tiled=True)


def gather(value, axis):
    n = lax.axis_size(axis)
    return exchange(jnp.broadcast_to(value, (n, *value.shape)), axis)


def dot(a, b, over_a, over_b):
    return lax.dot_general(a, b, (((over_a,), (over_b,)), ((), ())), preferred_element_type=F32)


def call(kernel, outs, flops, place, *arrays, out_space=pltpu.VMEM, scratch=()):
    size = sum(a.size * a.dtype.itemsize for a in (*arrays, *outs))
    return pl.pallas_call(
        kernel,
        out_shape=outs,
        in_specs=[pl.BlockSpec(memory_space=pltpu.SMEM)] + [pl.BlockSpec(memory_space=pltpu.VMEM)] * len(arrays),
        out_specs=[pl.BlockSpec(memory_space=out_space)] * len(outs),
        scratch_shapes=list(scratch),
        cost_estimate=pl.CostEstimate(flops=flops, bytes_accessed=size, transcendentals=0),
        compiler_params=pltpu.CompilerParams(vmem_limit_bytes=32 * 2**20),
    )(place.reshape(1), *arrays)


def logits_kernel(place_ref, q_ref, p_ref, p_other_ref, out_ref):
    del place_ref
    n_zh, block, _ = out_ref.shape
    count = p_ref.shape[0]
    n_x = q_ref.shape[0] // n_zh // BAND
    for z in range(n_zh):
        rows = [q_ref[pl.ds((x * n_zh + z) * BAND, BAND), :] for x in range(n_x)]
        rows = jnp.concatenate(rows, axis=0)
        out_ref[z, :, :count] = dot(rows, p_ref[...], 1, 1)
        out_ref[z, :, count:] = dot(rows, p_other_ref[...], 1, 1)


def passage_kernel(zl_ref, w_ref, far_w_ref, near_ref, far_ref, own_ref, send_ref):
    n_zl, width, count = send_ref.shape[0] + 1, own_ref.shape[1], own_ref.shape[0]
    n_zh, n_x = w_ref.shape[:2]
    order = [(z, x) for x in range(n_x) for z in range(n_zh)]
    w_near = jnp.concatenate([w_ref[z, x, :, :count] for z, x in order], axis=0)
    w_far = jnp.concatenate([far_w_ref[z, x] for z, x in order], axis=0)
    for t in range(n_zl):
        at = pl.ds(pl.multiple_of((zl_ref[0] + t) % n_zl * width, width), width)
        block = dot(w_near, near_ref[:, at], 0, 0) + dot(w_far, far_ref[:, at], 0, 0)
        if t == 0:
            own_ref[...] = block
        else:
            send_ref[t - 1] = block.astype(BF)


def query_kernel(x_ref, w_ref, p_ref, p_other_ref, own_ref, send_ref, own, blocks, sems):
    n_zh, n_x = w_ref.shape[:2]
    count = p_ref.shape[0]
    copies = []
    for x in range(n_x):
        rows = jnp.concatenate([w_ref[z, x] for z in range(n_zh)], axis=0)
        block = dot(rows[:, :count], p_ref[...], 1, 0) + dot(rows[:, count:], p_other_ref[...], 1, 0)
        blocks[x] = block.astype(BF)
        copies.append(pltpu.make_async_copy(blocks.at[x], send_ref.at[x], sems.at[x]))
        copies[-1].start()

        @pl.when(x_ref[0] == x)
        def _():
            own[...] = block

    copies.append(pltpu.make_async_copy(own, own_ref, sems.at[n_x]))
    copies[-1].start()
    for copy in copies:
        copy.wait()


def total_kernel(x_ref, own_ref, moved_ref, out_ref):
    n_x = moved_ref.shape[0]
    n_blocks, band, width = out_ref.shape
    n_zl = own_ref.shape[1] // width
    for z in range(n_blocks // n_zl):
        rows = pl.ds(z * band, band)
        total = own_ref[rows, :]
        for x in range(n_x):
            total = total + jnp.where(x_ref[0] == x, 0.0, moved_ref[x, rows, :].astype(F32))
        for l in range(n_zl):
            out_ref[z * n_zl + l] = total[:, l * width : (l + 1) * width].astype(BF)


def per_device(queries, passages, positive):
    rows, width = queries.shape
    count = passages.shape[0]
    n_x, n_y, n_zh, n_zl = (lax.axis_size(a) for a in ("x", "y", "zh", "zl"))
    strip = width * n_zl
    scale = 2.0 / math.sqrt(strip * n_y)
    band = rows // n_zl
    assert n_zh == n_y and band == BAND
    n_q = n_x * band
    n_half = band * n_zh * n_x
    x, y, zl = (lax.axis_index(a) for a in ("x", "y", "zl"))
    dev = lax.axis_index(ROWS)

    bands = jnp.broadcast_to(queries.reshape(n_zl, band, width), (n_zh, n_zl, band, width))
    mine = exchange(bands.reshape(n_zh * n_zl, band, width), COLUMN).reshape(n_zh, n_zl, band, width)
    mine = mine.transpose(0, 2, 1, 3).reshape(n_zh * band, strip)
    near = gather(mine, "x").reshape(n_half, strip)

    p = jnp.zeros((count, strip), BF)
    for t in range(n_zl):
        block = passages if t == 0 else shift(passages, "zl", t)
        p = lax.dynamic_update_slice_in_dim(p, block, (zl - t) % n_zl * width, 1)
    p_other = shift(p, "c", 1)
    near, p = lax.optimization_barrier((near, p))
    far = shift(near, "c", 1)

    flops = 4 * n_half * count * strip
    (partial,) = call(
        logits_kernel, [jax.ShapeDtypeStruct((n_zh, n_q, 2 * count), F32)], flops, x, near, p, p_other
    )
    moved = exchange(partial, "y")
    logits = moved[0]
    for i in range(1, n_y):
        logits = logits + moved[i]
    logits = logits * scale

    top = jnp.max(logits, axis=1)
    exps = jnp.exp(logits - top[:, None])
    total = jnp.sum(exps, axis=1)
    own_pos = lax.dynamic_slice_in_dim(positive, zl * band, band).astype(F32)
    note = jnp.concatenate([top, total, jnp.pad(own_pos, (0, 128 - band))])
    notes = exchange(jnp.broadcast_to(note, (n_x * n_zh, note.shape[0])), ("x", "zh"))
    tops, totals = notes[:, :n_q], notes[:, n_q : 2 * n_q]
    pos = notes[:, 2 * n_q : 2 * n_q + band].reshape(n_x, n_zh, band)
    pos = lax.dynamic_index_in_dim(pos, y, 1, keepdims=False).reshape(n_q).astype(jnp.int32)
    peak = jnp.max(tops, axis=0)
    denom = jnp.sum(totals * jnp.exp(tops - peak), axis=0)
    factor = jnp.exp(top - peak) / denom
    columns = lax.broadcasted_iota(jnp.int32, (n_q, 2 * count), 1)
    columns = jnp.where(columns < count, columns + dev * count, columns - count + (dev ^ 1) * count)
    onehot = (columns == pos[:, None]).astype(F32)
    weights = (exps * factor[:, None] - onehot).astype(BF)
    weights = gather(weights, "y").reshape(n_zh, n_x, band, 2 * count)
    far_weights = shift(weights[..., count:], "c", 1)

    block = (n_zh * band, strip)
    by_x, chip = call(
        query_kernel,
        [jax.ShapeDtypeStruct(block, F32), jax.ShapeDtypeStruct((n_x, *block), BF)],
        flops, x, weights, p, p_other,
        out_space=pltpu.HBM,
        scratch=[pltpu.VMEM(block, F32), pltpu.VMEM((n_x, *block), BF), pltpu.SemaphoreType.DMA((n_x + 1,))],
    )
    moved = exchange(chip, "x")
    (back,) = call(
        total_kernel, [jax.ShapeDtypeStruct((n_zh * n_zl, band, width), BF)], 0, x, by_x, moved
    )

    passage_grad, ahead = call(
        passage_kernel,
        [jax.ShapeDtypeStruct((count, width), F32), jax.ShapeDtypeStruct((n_zl - 1, count, width), BF)],
        flops, zl, weights, far_weights, near, far,
    )
    arrived = [shift(ahead[t - 1], "zl", t) for t in range(1, n_zl)]
    back, arrived[0] = lax.optimization_barrier((back, arrived[0]))
    for block in arrived:
        passage_grad = passage_grad + block.astype(F32)

    back = exchange(back, COLUMN).reshape(n_zh, rows, width)
    query_grad = jnp.sum(back.astype(F32), axis=0)
    return query_grad.astype(BF), passage_grad.astype(BF)


def solution(mesh):
    fine = Mesh(mesh.devices.reshape(4, 4, 4, 4, 2), FEATS + ROWS)
    in_specs = (P(ROWS, FEATS), P(ROWS, FEATS), P(ROWS))
    out_specs = (P(ROWS, FEATS), P(ROWS, FEATS))
    return jax.shard_map(per_device, mesh=fine, in_specs=in_specs, out_specs=out_specs, check_vma=False)
```

time: 180 us -> 163 us (0.906)
  blocking collectives: 55.7 us -> 10.6 us
  starting transfers between devices: 55 us -> 79.9 us
  waiting for transfers between devices: 50.2 us -> 55.5 us
  Pallas kernels: 4.5 us -> 6.85 us
  other arithmetic: 3.96 us -> 2.02 us
  local copies, waits for them, and re-layouts: 8.22 us -> 6.29 us
    all_to_all x2 -> x1, blocking collectives: 55.7 us -> 10.6 us  [exchange(): return lax.all_to_all(blocks, axis, 0, 0, tiled=True)]
    all_to_all x5 -> x6, starting transfers between devices: 28.1 us -> 43.4 us  [exchange(): return lax.all_to_all(blocks, axis, 0, 0, tiled=True)]
    ppermute x9, starting transfers between devices: 26.9 us -> 36.5 us  [shift(): return lax.ppermute(value, axis, [(i, (i + step) % n) for i in range(n)])]
    ppermute x9, waiting for transfers between devices: 14 us -> 18.4 us  [shift(): return lax.ppermute(value, axis, [(i, (i + step) % n) for i in range(n)])]
    pallas_call x3 -> x4, Pallas kernels: 4.5 us -> 6.85 us  [call(): pl.pallas_call(kernel, out_shape=outs, in_specs=[pl.BlockSpec(memory_spac...]
    all_to_all x5 -> x6, waiting for transfers between devices: 36.2 us -> 37.1 us  [exchange(): return lax.all_to_all(blocks, axis, 0, 0, tiled=True)]
  transfers between devices with their start and end apart: 14 -> 15, of which waited for: 10 -> 8; matrix products, arithmetic and copies ran while one was open for 1% -> 2% of each run, Pallas kernels for 0% -> 3%
where the time goes in v3:
time: 163 us; the launch traced here: 162 us
  starting transfers between devices  79.9 us (49%)
  waiting for transfers between devices  55.5 us (34%)
  blocking collectives  10.6 us (7%)
  Pallas kernels  6.85 us (4%)
  local copies, waits for them, and re-layouts  6.29 us (4%)
  other arithmetic  2.02 us (1%)
    all_to_all x6, starting transfers between devices, exchange(): return lax.all_to_all(blocks, axis, 0, 0, tiled=True)  43.4 us
    all_to_all x6, waiting for transfers between devices, exchange(): return lax.all_to_all(blocks, axis, 0, 0, tiled=True)  37.1 us
    ppermute x9, starting transfers between devices, shift(): return lax.ppermute(value, axis, [(i, (i + step) % n) for i in range(n)])  36.5 us
    ppermute x9, waiting for transfers between devices, shift(): return lax.ppermute(value, axis, [(i, (i + step) % n) for i in range(n)])  18.4 us
    all_to_all x1, blocking collectives, exchange(): return lax.all_to_all(blocks, axis, 0, 0, tiled=True)  10.6 us
    pallas_call x4, Pallas kernels, call(): pl.pallas_call(kernel, out_shape=outs, in_specs=[pl.BlockSpec(memory_spac...  6.85 us
  transfers between devices with their start and end apart: 15, of which 8 were waited for; matrix products, arithmetic and copies ran while one was open for 2% of the time, Pallas kernels for 3%

profile of v3, /device:TPU:6, one launch (start us, length us, event | category | flops | bytes accessed | tf_op | source)
XLA Modules:
  0.0 162.2 jit_solution(4308724139701924468)
XLA Ops:
  0.6 1.6 broadcast_in_dim.19
  2.2 15.3 %all-to-all-start = ((bf16[16,32,256]{2,1,0:T(8,128)(2,1)}), bf16[16,32,256]{2,1,0:T(8,128)(2,1)S(1)}, u32[]{:S(2)}, u32[]{:S(2)}) async-start(bf16[16,32,256]{2,1,0:T(8,128)(2,1)} %bitcast.2), calls=%async_computation | async-start | bytes 524288 | tf_op jit(solution)/shard_map/all_to_all | solution.py:24
  17.5 3.8 %collective-permute-start = (bf16[256,256]{1,0:T(8,128)(2,1)S(1)}, bf16[256,256]{1,0:T(8,128)(2,1)S(1)}, u32[]{:S(2)}, u32[]{:S(2)}) collective-permute-start(bf16[256,256]{1,0:T(8,128)(2,1)S(1)} %copy-done.5), channel_id=1, source_target_pairs={{0,32},{32,64},{64,96},{96,0},{1,33},{33,65},{65,97},{97,1},{2,34}... | collective-permute-start | bytes 393224 | tf_op jit(solution)/shard_map/ppermute | solution.py:20
  21.4 4.3 %collective-permute-start.1 = (bf16[256,256]{1,0:T(8,128)(2,1)S(1)}, bf16[256,256]{1,0:T(8,128)(2,1)S(1)}, u32[]{:S(2)}, u32[]{:S(2)}) collective-permute-start(bf16[256,256]{1,0:T(8,128)(2,1)S(1)} %copy-done.5), channel_id=1, source_target_pairs={{0,64},{32,96},{64,0},{96,32},{1,65},{33,97},{65,1},{97,33},{2,66}... | collective-permute-start | bytes 393224 | tf_op jit(solution)/shard_map/ppermute | solution.py:20
  25.7 3.4 %collective-permute-start.2 = (bf16[256,256]{1,0:T(8,128)(2,1)S(1)}, bf16[256,256]{1,0:T(8,128)(2,1)S(1)}, u32[]{:S(2)}, u32[]{:S(2)}) collective-permute-start(bf16[256,256]{1,0:T(8,128)(2,1)S(1)} %copy-done.5), channel_id=1, source_target_pairs={{0,96},{32,0},{64,32},{96,64},{1,97},{33,1},{65,33},{97,65},{2,98}... | collective-permute-start | bytes 393224 | tf_op jit(solution)/shard_map/ppermute | solution.py:20
  29.2 9.2 %all-to-all-done = bf16[16,32,256]{2,1,0:T(8,128)(2,1)S(1)} async-done(((bf16[16,32,256]{2,1,0:T(8,128)(2,1)}), bf16[16,32,256]{2,1,0:T(8,128)(2,1)S(1)}, u32[]{:S(2)}, u32[]{:S(2)}) %all-to-all-start) | async-done | bytes 262176 | tf_op jit(solution)/shard_map/all_to_all | solution.py:24
  38.6 1.1 broadcast_in_dim.20
  39.7 4.8 %all-to-all-start.1 = ((bf16[4,128,1024]{2,1,0:T(8,128)(2,1)}), bf16[4,128,1024]{2,1,0:T(8,128)(2,1)S(1)}, u32[]{:S(2)}, u32[]{:S(2)}) async-start(bf16[4,128,1024]{2,1,0:T(8,128)(2,1)} %broadcast_in_dim.20), calls=%async_computation.1 | async-start | bytes 2097152 | tf_op jit(solution)/shard_map/all_to_all | solution.py:24
  44.6 1.9 %collective-permute-start.3 = (bf16[256,1024]{1,0:T(8,128)(2,1)S(1)}, bf16[256,1024]{1,0:T(8,128)(2,1)S(1)}, u32[]{:S(2)}, u32[]{:S(2)}) collective-permute-start(bf16[256,1024]{1,0:T(8,128)(2,1)S(1)} %constant_dynamic-update-slice_fusion.p_ref), channel_id=1, source_target_pairs={{0,1},{1,0},{2,3},{3,2},{4,5},{5,4},{6,7},{7,6},{8,9},{9,8},{10,11... | collective-permute-start | bytes 1572872 | tf_op jit(solution)/shard_map/ppermute | solution.py:20
  46.5 6.8 %all-to-all-done.1 = bf16[4,128,1024]{2,1,0:T(8,128)(2,1)S(1)} async-done(((bf16[4,128,1024]{2,1,0:T(8,128)(2,1)}), bf16[4,128,1024]{2,1,0:T(8,128)(2,1)S(1)}, u32[]{:S(2)}, u32[]{:S(2)}) %all-to-all-start.1) | async-done | bytes 1048608 | tf_op jit(solution)/shard_map/all_to_all | solution.py:24
  53.3 2.5 %shard_map.50 = f32[4,128,512]{2,1,0:T(8,128)} custom-call(s32[1]{0:T(128)} %bitcast.place_ref.x_ref, bf16[512,1024]{1,0:T(8,128)(2,1)S(1)} %bitcast.33, bf16[256,1024]{1,0:T(8,128)(2,1)S(1)} %constant_dynamic-update-slice_fusion.p_ref, bf16[256,1024]{1,0:T(8,128)(2,1)S(1)} %collective-permute-done.3.p_other_ref), custom_call_target="tpu_custom_call" | custom-call | flops 536870912 | bytes 3145728 | tf_op jit(solution)/shard_map/pallas_call | solution.py:38
  55.8 4.5 %all-to-all-start.2 = ((f32[4,128,512]{2,1,0:T(8,128)}), f32[4,128,512]{2,1,0:T(8,128)S(1)}, u32[]{:S(2)}, u32[]{:S(2)}) async-start(f32[4,128,512]{2,1,0:T(8,128)} %shard_map.50), calls=%async_computation.2 | async-start | bytes 2097152 | tf_op jit(solution)/shard_map/all_to_all | solution.py:24
  61.0 10.2 %all-to-all-done.2 = f32[4,128,512]{2,1,0:T(8,128)S(1)} async-done(((f32[4,128,512]{2,1,0:T(8,128)}), f32[4,128,512]{2,1,0:T(8,128)S(1)}, u32[]{:S(2)}, u32[]{:S(2)}) %all-to-all-start.2) | async-done | bytes 1048608 | tf_op jit(solution)/shard_map/all_to_all | solution.py:24
  72.2 9.3 %all-to-all-start.3 = ((f32[16,1,384]{2,1,0:T(1,128)}), f32[16,1,384]{2,1,0:T(1,128)S(1)}, u32[]{:S(2)}, u32[]{:S(2)}) async-start(f32[16,1,384]{2,1,0:T(1,128)} %broadcast_in_dim.22), calls=%async_computation.3 | async-start | bytes 49152 | tf_op jit(solution)/shard_map/all_to_all | solution.py:24
  81.5 1.9 %collective-permute-start.5 = (bf16[512,1024]{1,0:T(8,128)(2,1)S(1)}, bf16[512,1024]{1,0:T(8,128)(2,1)}, u32[]{:S(2)}, u32[]{:S(2)}) collective-permute-start(bf16[512,1024]{1,0:T(8,128)(2,1)S(1)} %bitcast.34), channel_id=1, source_target_pairs={{0,1},{1,0},{2,3},{3,2},{4,5},{5,4},{6,7},{7,6},{8,9},{9,8},{10,11... | collective-permute-start | bytes 3145736 | tf_op jit(solution)/shard_map/ppermute | solution.py:20
  83.4 11.0 %all-to-all-done.3 = f32[16,1,384]{2,1,0:T(1,128)S(1)} async-done(((f32[16,1,384]{2,1,0:T(1,128)}), f32[16,1,384]{2,1,0:T(1,128)S(1)}, u32[]{:S(2)}, u32[]{:S(2)}) %all-to-all-start.3) | async-done | bytes 24608 | tf_op jit(solution)/shard_map/all_to_all | solution.py:24
  94.8 10.6 %all_to_all.39 = bf16[4,128,512]{2,1,0:T(8,128)(2,1)S(1)} all-to-all(bf16[4,128,512]{2,1,0:T(8,128)(2,1)S(1)} %broadcast_in_dim.23), channel_id=1, replica_groups=mesh['y'=4,'zl'=4,'zh'=4,'x'=4,'c'=2] {'y'}, dimensions={0} | all-to-all | bytes 1048576 | tf_op jit(solution)/shard_map/all_to_all | solution.py:24
  105.4 1.5 shard_map.51
  106.9 1.0 copy-done
  107.9 0.8 copy-done.3
  108.7 5.6 %all-to-all-start.5 = ((bf16[4,128,1024]{2,1,0:T(8,128)(2,1)}), bf16[4,128,1024]{2,1,0:T(8,128)(2,1)S(1)}, u32[]{:S(2)}, u32[]{:S(2)}) async-start(bf16[4,128,1024]{2,1,0:T(8,128)(2,1)} %copy-done), calls=%async_computation.5 | async-start | bytes 2097152 | tf_op jit(solution)/shard_map/all_to_all | solution.py:24
  114.2 1.9 %collective-permute-start.4 = (bf16[4,4,32,256]{3,2,1,0:T(8,128)(2,1)S(1)}, bf16[4,4,32,256]{3,2,1,0:T(8,128)(2,1)S(1)}, u32[]{:S(2)}, u32[]{:S(2)}) collective-permute-start(bf16[4,4,32,256]{3,2,1,0:T(8,128)(2,1)S(1)} %slice.51), channel_id=1, source_target_pairs={{0,1},{1,0},{2,3},{3,2},{4,5},{5,4},{6,7},{7,6},{8,9},{9,8},{10,11... | collective-permute-start | bytes 786440 | tf_op jit(solution)/shard_map/ppermute | solution.py:20
  116.2 1.5 collective-permute-done.4.far_w_ref
  117.7 2.0 %shard_map.53 = (f32[256,256]{1,0:T(8,128)S(1)}, bf16[3,256,256]{2,1,0:T(8,128)(2,1)S(1)}) custom-call(s32[1]{0:T(128)} %bitcast.9.zl_ref, bf16[4,4,32,512]{3,2,1,0:T(8,128)(2,1)S(1)} %bitcast.38, bf16[4,4,32,256]{3,2,1,0:T(8,128)(2,1)S(1)} %collective-permute-done.4.far_w_ref, bf16[512,1024]{1,0:T(8,128)(2,1)S(1)} %bitcast.35, ...), custom_call_target="tpu_custom_call" | custom-call | flops 536870912 | bytes 3538944 | tf_op jit(solution)/shard_map/pallas_call | solution.py:38
  119.7 11.7 %collective-permute-start.6 = (bf16[256,256]{1,0:T(8,128)(2,1)S(1)}, bf16[256,256]{1,0:T(8,128)(2,1)S(1)}, u32[]{:S(2)}, u32[]{:S(2)}) collective-permute-start(bf16[256,256]{1,0:T(8,128)(2,1)S(1)} %get-tuple-element.22), channel_id=1, source_target_pairs={{0,32},{32,64},{64,96},{96,0},{1,33},{33,65},{65,97},{97,1},{2,34}... | collective-permute-start | bytes 393224 | tf_op jit(solution)/shard_map/ppermute | solution.py:20
  131.5 0.9 shard_map.52
  132.4 2.1 %collective-permute-done.6 = bf16[256,256]{1,0:T(8,128)(2,1)S(1)} collective-permute-done((bf16[256,256]{1,0:T(8,128)(2,1)S(1)}, bf16[256,256]{1,0:T(8,128)(2,1)S(1)}, u32[]{:S(2)}, u32[]{:S(2)}) %collective-permute-start.6) | collective-permute-done | bytes 131104 | tf_op jit(solution)/shard_map/ppermute | solution.py:20
  134.5 4.0 %all-to-all-start.6 = ((bf16[16,32,256]{2,1,0:T(8,128)(2,1)}), bf16[16,32,256]{2,1,0:T(8,128)(2,1)S(1)}, u32[]{:S(2)}, u32[]{:S(2)}) async-start(bf16[16,32,256]{2,1,0:T(8,128)(2,1)} %shard_map.52), calls=%async_computation.6 | async-start | bytes 524288 | tf_op jit(solution)/shard_map/all_to_all | solution.py:24
  138.5 5.6 %collective-permute-start.8 = (bf16[256,256]{1,0:T(8,128)(2,1)S(1)}, bf16[256,256]{1,0:T(8,128)(2,1)S(1)}, u32[]{:S(2)}, u32[]{:S(2)}) collective-permute-start(bf16[256,256]{1,0:T(8,128)(2,1)S(1)} %get-tuple-element.21), channel_id=1, source_target_pairs={{0,96},{32,0},{64,32},{96,64},{1,97},{33,1},{65,33},{97,65},{2,98}... | collective-permute-start | bytes 393224 | tf_op jit(solution)/shard_map/ppermute | solution.py:20
  144.1 1.9 %collective-permute-start.7 = (bf16[256,256]{1,0:T(8,128)(2,1)S(1)}, bf16[256,256]{1,0:T(8,128)(2,1)S(1)}, u32[]{:S(2)}, u32[]{:S(2)}) collective-permute-start(bf16[256,256]{1,0:T(8,128)(2,1)S(1)} %get-tuple-element.20), channel_id=1, source_target_pairs={{0,64},{32,96},{64,0},{96,32},{1,65},{33,97},{65,1},{97,33},{2,66}... | collective-permute-start | bytes 393224 | tf_op jit(solution)/shard_map/ppermute | solution.py:20
  146.0 9.0 %collective-permute-done.8 = bf16[256,256]{1,0:T(8,128)(2,1)S(1)} collective-permute-done((bf16[256,256]{1,0:T(8,128)(2,1)S(1)}, bf16[256,256]{1,0:T(8,128)(2,1)S(1)}, u32[]{:S(2)}, u32[]{:S(2)}) %collective-permute-start.8) | collective-permute-done | bytes 131104 | tf_op jit(solution)/shard_map/ppermute | solution.py:20
  155.0 5.8 %collective-permute-done.7 = bf16[256,256]{1,0:T(8,128)(2,1)S(1)} collective-permute-done((bf16[256,256]{1,0:T(8,128)(2,1)S(1)}, bf16[256,256]{1,0:T(8,128)(2,1)S(1)}, u32[]{:S(2)}, u32[]{:S(2)}) %collective-permute-start.7) | collective-permute-done | bytes 131104 | tf_op jit(solution)/shard_map/ppermute | solution.py:20
  (46 shorter events, 3.9 us)
Async XLA Ops:
  2.2 15.3 %copy-start.5 = (bf16[256,256]{1,0:T(8,128)(2,1)S(1)}, bf16[256,256]{1,0:T(8,128)(2,1)}, u32[]{:S(2)}) copy-start(bf16[256,256]{1,0:T(8,128)(2,1)} %param.4) | copy-start | bytes 393220
  2.2 36.2 %all-to-all-start = ((bf16[16,32,256]{2,1,0:T(8,128)(2,1)}), bf16[16,32,256]{2,1,0:T(8,128)(2,1)S(1)}, u32[]{:S(2)}, u32[]{:S(2)}) async-start(bf16[16,32,256]{2,1,0:T(8,128)(2,1)} %bitcast.2), calls=%async_computation | async-start | bytes 524288 | tf_op jit(solution)/shard_map/all_to_all | solution.py:24
  17.5 27.0 %collective-permute-start = (bf16[256,256]{1,0:T(8,128)(2,1)S(1)}, bf16[256,256]{1,0:T(8,128)(2,1)S(1)}, u32[]{:S(2)}, u32[]{:S(2)}) collective-permute-start(bf16[256,256]{1,0:T(8,128)(2,1)S(1)} %copy-done.5), channel_id=1, source_target_pairs={{0,32},{32,64},{64,96},{96,0},{1,33},{33,65},{65,97},{97,1},{2,34}... | collective-permute-start | bytes 393224 | tf_op jit(solution)/shard_map/ppermute | solution.py:20
  21.4 23.1 %collective-permute-start.1 = (bf16[256,256]{1,0:T(8,128)(2,1)S(1)}, bf16[256,256]{1,0:T(8,128)(2,1)S(1)}, u32[]{:S(2)}, u32[]{:S(2)}) collective-permute-start(bf16[256,256]{1,0:T(8,128)(2,1)S(1)} %copy-done.5), channel_id=1, source_target_pairs={{0,64},{32,96},{64,0},{96,32},{1,65},{33,97},{65,1},{97,33},{2,66}... | collective-permute-start | bytes 393224 | tf_op jit(solution)/shard_map/ppermute | solution.py:20
  25.7 18.9 %collective-permute-start.2 = (bf16[256,256]{1,0:T(8,128)(2,1)S(1)}, bf16[256,256]{1,0:T(8,128)(2,1)S(1)}, u32[]{:S(2)}, u32[]{:S(2)}) collective-permute-start(bf16[256,256]{1,0:T(8,128)(2,1)S(1)} %copy-done.5), channel_id=1, source_target_pairs={{0,96},{32,0},{64,32},{96,64},{1,97},{33,1},{65,33},{97,65},{2,98}... | collective-permute-start | bytes 393224 | tf_op jit(solution)/shard_map/ppermute | solution.py:20
  39.7 13.6 %all-to-all-start.1 = ((bf16[4,128,1024]{2,1,0:T(8,128)(2,1)}), bf16[4,128,1024]{2,1,0:T(8,128)(2,1)S(1)}, u32[]{:S(2)}, u32[]{:S(2)}) async-start(bf16[4,128,1024]{2,1,0:T(8,128)(2,1)} %broadcast_in_dim.20), calls=%async_computation.1 | async-start | bytes 2097152 | tf_op jit(solution)/shard_map/all_to_all | solution.py:24
  44.6 8.7 %collective-permute-start.3 = (bf16[256,1024]{1,0:T(8,128)(2,1)S(1)}, bf16[256,1024]{1,0:T(8,128)(2,1)S(1)}, u32[]{:S(2)}, u32[]{:S(2)}) collective-permute-start(bf16[256,1024]{1,0:T(8,128)(2,1)S(1)} %constant_dynamic-update-slice_fusion.p_ref), channel_id=1, source_target_pairs={{0,1},{1,0},{2,3},{3,2},{4,5},{5,4},{6,7},{7,6},{8,9},{9,8},{10,11... | collective-permute-start | bytes 1572872 | tf_op jit(solution)/shard_map/ppermute | solution.py:20
  53.3 2.5 %copy-start.1 = (bf16[256,1024]{1,0:T(8,128)(2,1)}, bf16[256,1024]{1,0:T(8,128)(2,1)S(1)}, u32[]{:S(2)}) copy-start(bf16[256,1024]{1,0:T(8,128)(2,1)S(1)} %collective-permute-done.3.p_other_ref) | copy-start | bytes 1572868
  55.8 15.4 %all-to-all-start.2 = ((f32[4,128,512]{2,1,0:T(8,128)}), f32[4,128,512]{2,1,0:T(8,128)S(1)}, u32[]{:S(2)}, u32[]{:S(2)}) async-start(f32[4,128,512]{2,1,0:T(8,128)} %shard_map.50), calls=%async_computation.2 | async-start | bytes 2097152 | tf_op jit(solution)/shard_map/all_to_all | solution.py:24
  60.3 0.7 copy-start.6
  72.2 22.2 %all-to-all-start.3 = ((f32[16,1,384]{2,1,0:T(1,128)}), f32[16,1,384]{2,1,0:T(1,128)S(1)}, u32[]{:S(2)}, u32[]{:S(2)}) async-start(f32[16,1,384]{2,1,0:T(1,128)} %broadcast_in_dim.22), calls=%async_computation.3 | async-start | bytes 49152 | tf_op jit(solution)/shard_map/all_to_all | solution.py:24
  81.5 34.7 %collective-permute-start.5 = (bf16[512,1024]{1,0:T(8,128)(2,1)S(1)}, bf16[512,1024]{1,0:T(8,128)(2,1)}, u32[]{:S(2)}, u32[]{:S(2)}) collective-permute-start(bf16[512,1024]{1,0:T(8,128)(2,1)S(1)} %bitcast.34), channel_id=1, source_target_pairs={{0,1},{1,0},{2,3},{3,2},{4,5},{5,4},{6,7},{7,6},{8,9},{9,8},{10,11... | collective-permute-start | bytes 3145736 | tf_op jit(solution)/shard_map/ppermute | solution.py:20
  94.8 10.6 %copy-start.2 = (bf16[256,1024]{1,0:T(8,128)(2,1)S(1)}, bf16[256,1024]{1,0:T(8,128)(2,1)}, u32[]{:S(2)}) copy-start(bf16[256,1024]{1,0:T(8,128)(2,1)} %copy-done.1) | copy-start | bytes 1572868
  106.9 1.0 copy-start
  107.9 0.8 copy-start.3
  108.7 22.8 %all-to-all-start.5 = ((bf16[4,128,1024]{2,1,0:T(8,128)(2,1)}), bf16[4,128,1024]{2,1,0:T(8,128)(2,1)S(1)}, u32[]{:S(2)}, u32[]{:S(2)}) async-start(bf16[4,128,1024]{2,1,0:T(8,128)(2,1)} %copy-done), calls=%async_computation.5 | async-start | bytes 2097152 | tf_op jit(solution)/shard_map/all_to_all | solution.py:24
  114.2 3.4 %collective-permute-start.4 = (bf16[4,4,32,256]{3,2,1,0:T(8,128)(2,1)S(1)}, bf16[4,4,32,256]{3,2,1,0:T(8,128)(2,1)S(1)}, u32[]{:S(2)}, u32[]{:S(2)}) collective-permute-start(bf16[4,4,32,256]{3,2,1,0:T(8,128)(2,1)S(1)} %slice.51), channel_id=1, source_target_pairs={{0,1},{1,0},{2,3},{3,2},{4,5},{5,4},{6,7},{7,6},{8,9},{9,8},{10,11... | collective-permute-start | bytes 786440 | tf_op jit(solution)/shard_map/ppermute | solution.py:20
  119.7 11.8 %copy-start.4 = (f32[128,1024]{1,0:T(8,128)S(1)}, f32[128,1024]{1,0:T(8,128)}, u32[]{:S(2)}) copy-start(f32[128,1024]{1,0:T(8,128)} %copy-done.3) | copy-start | bytes 1572868
  119.7 14.8 %collective-permute-start.6 = (bf16[256,256]{1,0:T(8,128)(2,1)S(1)}, bf16[256,256]{1,0:T(8,128)(2,1)S(1)}, u32[]{:S(2)}, u32[]{:S(2)}) collective-permute-start(bf16[256,256]{1,0:T(8,128)(2,1)S(1)} %get-tuple-element.22), channel_id=1, source_target_pairs={{0,32},{32,64},{64,96},{96,0},{1,33},{33,65},{65,97},{97,1},{2,34}... | collective-permute-start | bytes 393224 | tf_op jit(solution)/shard_map/ppermute | solution.py:20
  134.5 27.1 %all-to-all-start.6 = ((bf16[16,32,256]{2,1,0:T(8,128)(2,1)}), bf16[16,32,256]{2,1,0:T(8,128)(2,1)S(1)}, u32[]{:S(2)}, u32[]{:S(2)}) async-start(bf16[16,32,256]{2,1,0:T(8,128)(2,1)} %shard_map.52), calls=%async_computation.6 | async-start | bytes 524288 | tf_op jit(solution)/shard_map/all_to_all | solution.py:24
  138.5 16.5 %collective-permute-start.8 = (bf16[256,256]{1,0:T(8,128)(2,1)S(1)}, bf16[256,256]{1,0:T(8,128)(2,1)S(1)}, u32[]{:S(2)}, u32[]{:S(2)}) collective-permute-start(bf16[256,256]{1,0:T(8,128)(2,1)S(1)} %get-tuple-element.21), channel_id=1, source_target_pairs={{0,96},{32,0},{64,32},{96,64},{1,97},{33,1},{65,33},{97,65},{2,98}... | collective-permute-start | bytes 393224 | tf_op jit(solution)/shard_map/ppermute | solution.py:20
  144.1 16.7 %collective-permute-start.7 = (bf16[256,256]{1,0:T(8,128)(2,1)S(1)}, bf16[256,256]{1,0:T(8,128)(2,1)S(1)}, u32[]{:S(2)}, u32[]{:S(2)}) collective-permute-start(bf16[256,256]{1,0:T(8,128)(2,1)S(1)} %get-tuple-element.20), channel_id=1, source_target_pairs={{0,64},{32,96},{64,0},{96,32},{1,65},{33,97},{65,1},{97,33},{2,66}... | collective-permute-start | bytes 393224 | tf_op jit(solution)/shard_map/ppermute | solution.py:20

commit v4 on v3

v4 whole, which is shorter than its diff:
```python
import math

import jax
import jax.numpy as jnp
from jax import lax
from jax.experimental import pallas as pl
from jax.experimental.pallas import tpu as pltpu
from jax.sharding import Mesh, PartitionSpec as P

ROWS = ("zh", "x", "c")
FEATS = ("y", "zl")
COLUMN = ("zh", "zl")
BF = jnp.bfloat16
F32 = jnp.float32
BAND = 32


def shift(value, axis, step):
    n = lax.axis_size(axis)
    return lax.ppermute(value, axis, [(i, (i + step) % n) for i in range(n)])


def flip(value, axis, bit):
    return lax.ppermute(value, axis, [(i, i ^ bit) for i in range(lax.axis_size(axis))])


def exchange(blocks, axis):
    return lax.all_to_all(blocks, axis, 0, 0, tiled=True)


def gather(value, axis):
    n = lax.axis_size(axis)
    return exchange(jnp.broadcast_to(value, (n, *value.shape)), axis)


def dot(a, b, over_a, over_b):
    return lax.dot_general(a, b, (((over_a,), (over_b,)), ((), ())), preferred_element_type=F32)


def call(kernel, outs, flops, place, *arrays):
    size = sum(a.size * a.dtype.itemsize for a in (*arrays, *outs))
    return pl.pallas_call(
        kernel,
        out_shape=outs,
        in_specs=[pl.BlockSpec(memory_space=pltpu.SMEM)] + [pl.BlockSpec(memory_space=pltpu.VMEM)] * len(arrays),
        out_specs=[pl.BlockSpec(memory_space=pltpu.VMEM)] * len(outs),
        cost_estimate=pl.CostEstimate(flops=flops, bytes_accessed=size, transcendentals=0),
        compiler_params=pltpu.CompilerParams(vmem_limit_bytes=32 * 2**20),
    )(place.reshape(1), *arrays)


def logits_kernel(place_ref, q_ref, p_ref, p_other_ref, out_ref):
    del place_ref
    n_zh = out_ref.shape[0]
    count = p_ref.shape[0]
    n_x = q_ref.shape[0] // n_zh // BAND
    for side, side_ref in enumerate((p_ref, p_other_ref)):
        block = dot(q_ref[...], side_ref[...], 1, 1)
        for x in range(n_x):
            for z in range(n_zh):
                at = (x * n_zh + z) * BAND
                out_ref[z, x * BAND : (x + 1) * BAND, side * count : (side + 1) * count] = block[at : at + BAND]


def passage_kernel(zl_ref, w_ref, far_w_ref, near_ref, far_ref, keep_ref, send_ref):
    _, count, width = keep_ref.shape
    n_zh, n_x = w_ref.shape[:2]
    order = [(z, x) for x in range(n_x) for z in range(n_zh)]
    w_near = jnp.concatenate([w_ref[z, x, :, :count] for z, x in order], axis=0)
    w_far = jnp.concatenate([far_w_ref[z, x] for z, x in order], axis=0)
    for i, flip in enumerate((0, 2, 1, 3)):
        at = pl.ds(pl.multiple_of((zl_ref[0] ^ flip) * width, width), width)
        block = dot(w_near, near_ref[:, at], 0, 0) + dot(w_far, far_ref[:, at], 0, 0)
        if i < 2:
            keep_ref[i] = block
        else:
            send_ref[i - 2] = block.astype(BF)


def spread_kernel(place_ref, in_ref, out_ref):
    del place_ref
    n, band, _ = out_ref.shape
    n_bands = in_ref.shape[0] // band
    for i in range(n):
        out_ref[i] = in_ref[pl.ds(i % n_bands * band, band), :]


def collect_kernel(place_ref, in_ref, out_ref):
    del place_ref
    n, band, width = in_ref.shape
    n_zl = out_ref.shape[2] // width
    for i in range(n):
        for x in range(out_ref.shape[0]):
            at = i // n_zl * band
            out_ref[x, at : at + band, i % n_zl * width : (i % n_zl + 1) * width] = in_ref[i]


def query_block(w_ref, p_ref, p_other_ref, x):
    count = p_ref.shape[0]
    rows = jnp.concatenate([w_ref[z, x] for z in range(w_ref.shape[0])], axis=0)
    return dot(rows[:, :count], p_ref[...], 1, 0) + dot(rows[:, count:], p_other_ref[...], 1, 0)


def query_kernel(x_ref, w_ref, p_ref, p_other_ref, send_ref):
    del x_ref
    for x in range(send_ref.shape[0]):
        send_ref[x] = query_block(w_ref, p_ref, p_other_ref, x).astype(BF)


def own_kernel(x_ref, w_ref, p_ref, p_other_ref, out_ref):
    out_ref[...] = query_block(w_ref, p_ref, p_other_ref, x_ref[0])


def total_kernel(x_ref, own_ref, moved_ref, out_ref):
    n_x, n_rows, strip = moved_ref.shape
    n_blocks, band, width = out_ref.shape
    n_zl = strip // width
    total = own_ref[...]
    for x in range(n_x):
        total = total + jnp.where(x_ref[0] == x, 0.0, moved_ref[x].astype(F32))
    for z in range(n_blocks // n_zl):
        for l in range(n_zl):
            out_ref[z * n_zl + l] = total[z * band : (z + 1) * band, l * width : (l + 1) * width].astype(BF)


def per_device(queries, passages, positive):
    rows, width = queries.shape
    count = passages.shape[0]
    n_x, n_y, n_zh, n_zl = (lax.axis_size(a) for a in ("x", "y", "zh", "zl"))
    strip = width * n_zl
    scale = 2.0 / math.sqrt(strip * n_y)
    band = rows // n_zl
    assert n_zh == n_y and band == BAND
    n_q = n_x * band
    n_half = band * n_zh * n_x
    x, y, zl = (lax.axis_index(a) for a in ("x", "y", "zl"))
    dev = lax.axis_index(ROWS)

    bands = jax.ShapeDtypeStruct((n_zh * n_zl, band, width), BF)
    spread = jax.ShapeDtypeStruct((n_x, n_zh * band, strip), BF)
    (mine,) = call(spread_kernel, [bands], 0, x, queries)
    (mine,) = call(collect_kernel, [spread], 0, x, exchange(mine, COLUMN))
    near = exchange(mine, "x").reshape(n_half, strip)

    p = jnp.zeros((count, strip), BF)
    for t in range(n_zl):
        block = passages if t == 0 else shift(passages, "zl", t)
        p = lax.dynamic_update_slice_in_dim(p, block, (zl - t) % n_zl * width, 1)
    p_other = shift(p, "c", 1)
    near, p = lax.optimization_barrier((near, p))
    far = shift(near, "c", 1)

    flops = 4 * n_half * count * strip
    (partial,) = call(
        logits_kernel, [jax.ShapeDtypeStruct((n_zh, n_q, 2 * count), F32)], flops, x, near, p, p_other
    )
    moved = exchange(partial, "y")
    logits = moved[0]
    for i in range(1, n_y):
        logits = logits + moved[i]
    logits = logits * scale

    top = jnp.max(logits, axis=1)
    exps = jnp.exp(logits - top[:, None])
    total = jnp.sum(exps, axis=1)
    own_pos = lax.dynamic_slice_in_dim(positive, zl * band, band).astype(F32)
    note = jnp.concatenate([top, total, jnp.pad(own_pos, (0, 128 - band))])
    notes = exchange(jnp.broadcast_to(note, (n_x * n_zh, note.shape[0])), ("x", "zh"))
    tops, totals = notes[:, :n_q], notes[:, n_q : 2 * n_q]
    pos = notes[:, 2 * n_q : 2 * n_q + band].reshape(n_x, n_zh, band)
    pos = lax.dynamic_index_in_dim(pos, y, 1, keepdims=False).reshape(n_q).astype(jnp.int32)
    peak = jnp.max(tops, axis=0)
    denom = jnp.sum(totals * jnp.exp(tops - peak), axis=0)
    factor = jnp.exp(top - peak) / denom
    columns = lax.broadcasted_iota(jnp.int32, (n_q, 2 * count), 1)
    columns = jnp.where(columns < count, columns + dev * count, columns - count + (dev ^ 1) * count)
    onehot = (columns == pos[:, None]).astype(F32)
    weights = (exps * factor[:, None] - onehot).astype(BF)
    weights = gather(weights, "y").reshape(n_zh, n_x, band, 2 * count)
    far_weights = shift(weights[..., count:], "c", 1)

    block = (n_zh * band, strip)
    (chip,) = call(query_kernel, [jax.ShapeDtypeStruct((n_x, *block), BF)], flops, x, weights, p, p_other)
    moved = exchange(chip, "x")
    (own,) = call(own_kernel, [jax.ShapeDtypeStruct(block, F32)], flops // n_x, x, weights, p, p_other)
    (back,) = call(total_kernel, [bands], 0, x, own, moved)

    pair = (2, count, width)
    keep, send = call(
        passage_kernel,
        [jax.ShapeDtypeStruct(pair, F32), jax.ShapeDtypeStruct(pair, BF)],
        flops, zl, weights, far_weights, near, far,
    )
    arrived = flip(send, "zl", 1)
    back, arrived = lax.optimization_barrier((back, arrived))
    passage_grad = keep[0] + arrived[0].astype(F32)
    passage_grad += flip((keep[1] + arrived[1].astype(F32)).astype(BF), "zl", 2).astype(F32)

    back = exchange(back, COLUMN).reshape(n_zh, rows, width)
    query_grad = jnp.sum(back.astype(F32), axis=0)
    return query_grad.astype(BF), passage_grad.astype(BF)


def solution(mesh):
    fine = Mesh(mesh.devices.reshape(4, 4, 4, 4, 2), FEATS + ROWS)
    in_specs = (P(ROWS, FEATS), P(ROWS, FEATS), P(ROWS))
    out_specs = (P(ROWS, FEATS), P(ROWS, FEATS))
    return jax.shard_map(per_device, mesh=fine, in_specs=in_specs, out_specs=out_specs, check_vma=False)
```

time: 163 us -> 162 us (level)
  local copies, waits for them, and re-layouts: 6.29 us -> 3.4 us
  starting transfers between devices: 79.9 us -> 77.1 us
  waiting for transfers between devices: 55.5 us -> 58.1 us
  Pallas kernels: 6.85 us -> 8.63 us
    ppermute x0 -> x2, waiting for transfers between devices: none -> 19.5 us  [flip(): lax.ppermute(value, axis, [(i, i ^ bit) for i in range(lax.axis_size(axis...]
    ppermute x9 -> x6, starting transfers between devices: 36.5 us -> 17.2 us  [shift(): return lax.ppermute(value, axis, [(i, (i + step) % n) for i in range(n)])]
    ppermute x9 -> x6, waiting for transfers between devices: 18.4 us -> 1.5 us  [shift(): return lax.ppermute(value, axis, [(i, (i + step) % n) for i in range(n)])]
    ppermute x0 -> x2, starting transfers between devices: none -> 16.2 us  [flip(): lax.ppermute(value, axis, [(i, i ^ bit) for i in range(lax.axis_size(axis...]
    pallas_call x4 -> x7, Pallas kernels: 6.85 us -> 8.63 us  [call(): pl.pallas_call(kernel, out_shape=outs, in_specs=[pl.BlockSpec(memory_spac...]
  transfers between devices with their start and end apart: 15 -> 14, of which waited for: 8 -> 7; matrix products, arithmetic and copies ran while one was open for 2% -> 1% of each run, Pallas kernels for 3% -> 4%
where the time goes in v4:
time: 162 us; the launch traced here: 161 us
  starting transfers between devices  77.1 us (48%)
  waiting for transfers between devices  58.1 us (36%)
  blocking collectives  10.5 us (6%)
  Pallas kernels  8.63 us (5%)
  local copies, waits for them, and re-layouts  3.4 us (2%)
  other arithmetic  2.03 us (1%)
    all_to_all x6, starting transfers between devices, exchange(): return lax.all_to_all(blocks, axis, 0, 0, tiled=True)  43.7 us
    all_to_all x6, waiting for transfers between devices, exchange(): return lax.all_to_all(blocks, axis, 0, 0, tiled=True)  37.1 us
    ppermute x2, waiting for transfers between devices, flip(): lax.ppermute(value, axis, [(i, i ^ bit) for i in range(lax.axis_size(axis...  19.5 us
    ppermute x6, starting transfers between devices, shift(): return lax.ppermute(value, axis, [(i, (i + step) % n) for i in range(n)])  17.2 us
    ppermute x2, starting transfers between devices, flip(): lax.ppermute(value, axis, [(i, i ^ bit) for i in range(lax.axis_size(axis...  16.2 us
    all_to_all x1, blocking collectives, exchange(): return lax.all_to_all(blocks, axis, 0, 0, tiled=True)  10.5 us
    pallas_call x7, Pallas kernels, call(): pl.pallas_call(kernel, out_shape=outs, in_specs=[pl.BlockSpec(memory_spac...  8.63 us
  transfers between devices with their start and end apart: 14, of which 7 were waited for; matrix products, arithmetic and copies ran while one was open for 1% of the time, Pallas kernels for 4%

profile of v4, /device:TPU:6, one launch (start us, length us, event | category | flops | bytes accessed | tf_op | source)
XLA Modules:
  0.0 160.7 jit_solution(17878288943088474794)
XLA Ops:
  0.6 0.8 copy-done.1
  1.5 0.7 shard_map.50
  2.2 15.3 %all-to-all-start = ((bf16[16,32,256]{2,1,0:T(8,128)(2,1)}), bf16[16,32,256]{2,1,0:T(8,128)(2,1)S(1)}, u32[]{:S(2)}, u32[]{:S(2)}) async-start(bf16[16,32,256]{2,1,0:T(8,128)(2,1)} %shard_map.50), calls=%async_computation | async-start | bytes 524288 | tf_op jit(solution)/shard_map/all_to_all | solution.py:28
  17.5 3.8 %collective-permute-start = (bf16[256,256]{1,0:T(8,128)(2,1)S(1)}, bf16[256,256]{1,0:T(8,128)(2,1)S(1)}, u32[]{:S(2)}, u32[]{:S(2)}) collective-permute-start(bf16[256,256]{1,0:T(8,128)(2,1)S(1)} %copy-done.2), channel_id=1, source_target_pairs={{0,32},{32,64},{64,96},{96,0},{1,33},{33,65},{65,97},{97,1},{2,34}... | collective-permute-start | bytes 393224 | tf_op jit(solution)/shard_map/ppermute | solution.py:20
  21.4 4.3 %collective-permute-start.1 = (bf16[256,256]{1,0:T(8,128)(2,1)S(1)}, bf16[256,256]{1,0:T(8,128)(2,1)S(1)}, u32[]{:S(2)}, u32[]{:S(2)}) collective-permute-start(bf16[256,256]{1,0:T(8,128)(2,1)S(1)} %copy-done.2), channel_id=1, source_target_pairs={{0,64},{32,96},{64,0},{96,32},{1,65},{33,97},{65,1},{97,33},{2,66}... | collective-permute-start | bytes 393224 | tf_op jit(solution)/shard_map/ppermute | solution.py:20
  25.7 3.4 %collective-permute-start.2 = (bf16[256,256]{1,0:T(8,128)(2,1)S(1)}, bf16[256,256]{1,0:T(8,128)(2,1)S(1)}, u32[]{:S(2)}, u32[]{:S(2)}) collective-permute-start(bf16[256,256]{1,0:T(8,128)(2,1)S(1)} %copy-done.2), channel_id=1, source_target_pairs={{0,96},{32,0},{64,32},{96,64},{1,97},{33,1},{65,33},{97,65},{2,98}... | collective-permute-start | bytes 393224 | tf_op jit(solution)/shard_map/ppermute | solution.py:20
  29.2 9.2 %all-to-all-done.in_ref = bf16[16,32,256]{2,1,0:T(8,128)(2,1)S(1)} async-done(((bf16[16,32,256]{2,1,0:T(8,128)(2,1)}), bf16[16,32,256]{2,1,0:T(8,128)(2,1)S(1)}, u32[]{:S(2)}, u32[]{:S(2)}) %all-to-all-start) | async-done | bytes 262176 | tf_op jit(solution)/shard_map/all_to_all | solution.py:28
  38.4 1.1 shard_map.51
  39.4 4.8 %all-to-all-start.1 = ((bf16[4,128,1024]{2,1,0:T(8,128)(2,1)}), bf16[4,128,1024]{2,1,0:T(8,128)(2,1)S(1)}, u32[]{:S(2)}, u32[]{:S(2)}) async-start(bf16[4,128,1024]{2,1,0:T(8,128)(2,1)} %shard_map.51), calls=%async_computation.1 | async-start | bytes 2097152 | tf_op jit(solution)/shard_map/all_to_all | solution.py:28
  44.3 1.9 %collective-permute-start.3 = (bf16[256,1024]{1,0:T(8,128)(2,1)S(1)}, bf16[256,1024]{1,0:T(8,128)(2,1)S(1)}, u32[]{:S(2)}, u32[]{:S(2)}) collective-permute-start(bf16[256,1024]{1,0:T(8,128)(2,1)S(1)} %constant_dynamic-update-slice_fusion.p_ref), channel_id=1, source_target_pairs={{0,1},{1,0},{2,3},{3,2},{4,5},{5,4},{6,7},{7,6},{8,9},{9,8},{10,11... | collective-permute-start | bytes 1572872 | tf_op jit(solution)/shard_map/ppermute | solution.py:20
  46.2 6.8 %all-to-all-done.1 = bf16[4,128,1024]{2,1,0:T(8,128)(2,1)S(1)} async-done(((bf16[4,128,1024]{2,1,0:T(8,128)(2,1)}), bf16[4,128,1024]{2,1,0:T(8,128)(2,1)S(1)}, u32[]{:S(2)}, u32[]{:S(2)}) %all-to-all-start.1) | async-done | bytes 1048608 | tf_op jit(solution)/shard_map/all_to_all | solution.py:28
  53.0 1.7 %shard_map.52 = f32[4,128,512]{2,1,0:T(8,128)} custom-call(s32[1]{0:T(128)} %bitcast.place_ref.x_ref, bf16[512,1024]{1,0:T(8,128)(2,1)S(1)} %bitcast.29, bf16[256,1024]{1,0:T(8,128)(2,1)S(1)} %constant_dynamic-update-slice_fusion.p_ref, bf16[256,1024]{1,0:T(8,128)(2,1)S(1)} %collective-permute-done.3.p_other_ref), custom_call_target="tpu_custom_call" | custom-call | flops 536870912 | bytes 3145728 | tf_op jit(solution)/shard_map/pallas_call | solution.py:42
  54.7 4.5 %all-to-all-start.2 = ((f32[4,128,512]{2,1,0:T(8,128)}), f32[4,128,512]{2,1,0:T(8,128)S(1)}, u32[]{:S(2)}, u32[]{:S(2)}) async-start(f32[4,128,512]{2,1,0:T(8,128)} %shard_map.52), calls=%async_computation.2 | async-start | bytes 2097152 | tf_op jit(solution)/shard_map/all_to_all | solution.py:28
  59.9 10.2 %all-to-all-done.2 = f32[4,128,512]{2,1,0:T(8,128)S(1)} async-done(((f32[4,128,512]{2,1,0:T(8,128)}), f32[4,128,512]{2,1,0:T(8,128)S(1)}, u32[]{:S(2)}, u32[]{:S(2)}) %all-to-all-start.2) | async-done | bytes 1048608 | tf_op jit(solution)/shard_map/all_to_all | solution.py:28
  71.1 9.3 %all-to-all-start.3 = ((f32[16,1,384]{2,1,0:T(1,128)}), f32[16,1,384]{2,1,0:T(1,128)S(1)}, u32[]{:S(2)}, u32[]{:S(2)}) async-start(f32[16,1,384]{2,1,0:T(1,128)} %broadcast_in_dim.14), calls=%async_computation.3 | async-start | bytes 49152 | tf_op jit(solution)/shard_map/all_to_all | solution.py:28
  80.4 1.9 %collective-permute-start.5 = (bf16[512,1024]{1,0:T(8,128)(2,1)S(1)}, bf16[512,1024]{1,0:T(8,128)(2,1)}, u32[]{:S(2)}, u32[]{:S(2)}) collective-permute-start(bf16[512,1024]{1,0:T(8,128)(2,1)S(1)} %bitcast.30), channel_id=1, source_target_pairs={{0,1},{1,0},{2,3},{3,2},{4,5},{5,4},{6,7},{7,6},{8,9},{9,8},{10,11... | collective-permute-start | bytes 3145736 | tf_op jit(solution)/shard_map/ppermute | solution.py:20
  82.3 11.0 %all-to-all-done.3 = f32[16,1,384]{2,1,0:T(1,128)S(1)} async-done(((f32[16,1,384]{2,1,0:T(1,128)}), f32[16,1,384]{2,1,0:T(1,128)S(1)}, u32[]{:S(2)}, u32[]{:S(2)}) %all-to-all-start.3) | async-done | bytes 24608 | tf_op jit(solution)/shard_map/all_to_all | solution.py:28
  93.7 10.5 %all_to_all.39 = bf16[4,128,512]{2,1,0:T(8,128)(2,1)S(1)} all-to-all(bf16[4,128,512]{2,1,0:T(8,128)(2,1)S(1)} %broadcast_in_dim.15), channel_id=1, replica_groups=mesh['y'=4,'zl'=4,'zh'=4,'x'=4,'c'=2] {'y'}, dimensions={0} | all-to-all | bytes 1048576 | tf_op jit(solution)/shard_map/all_to_all | solution.py:28
  104.2 0.7 shard_map.54
  104.9 1.0 copy-done
  105.9 6.3 %all-to-all-start.5 = ((bf16[4,128,1024]{2,1,0:T(8,128)(2,1)}), bf16[4,128,1024]{2,1,0:T(8,128)(2,1)}, u32[]{:S(2)}, u32[]{:S(2)}) async-start(bf16[4,128,1024]{2,1,0:T(8,128)(2,1)} %copy-done), calls=%async_computation.5 | async-start | bytes 2097152 | tf_op jit(solution)/shard_map/all_to_all | solution.py:28
  112.2 1.9 %collective-permute-start.4 = (bf16[4,4,32,256]{3,2,1,0:T(8,128)(2,1)S(1)}, bf16[4,4,32,256]{3,2,1,0:T(8,128)(2,1)S(1)}, u32[]{:S(2)}, u32[]{:S(2)}) collective-permute-start(bf16[4,4,32,256]{3,2,1,0:T(8,128)(2,1)S(1)} %slice.55), channel_id=1, source_target_pairs={{0,1},{1,0},{2,3},{3,2},{4,5},{5,4},{6,7},{7,6},{8,9},{9,8},{10,11... | collective-permute-start | bytes 786440 | tf_op jit(solution)/shard_map/ppermute | solution.py:20
  114.1 1.5 collective-permute-done.4.far_w_ref
  115.6 2.0 %shard_map.56 = (f32[2,256,256]{2,1,0:T(8,128)S(1)}, bf16[2,256,256]{2,1,0:T(8,128)(2,1)S(1)}) custom-call(s32[1]{0:T(128)} %bitcast.5.zl_ref, bf16[4,4,32,512]{3,2,1,0:T(8,128)(2,1)S(1)} %bitcast.27, bf16[4,4,32,256]{3,2,1,0:T(8,128)(2,1)S(1)} %collective-permute-done.4.far_w_ref, bf16[512,1024]{1,0:T(8,128)(2,1)S(1)} %bitcast.31, ...), custom_call_target="tpu_custom_call" | custom-call | flops 536870912 | bytes 3670016 | tf_op jit(solution)/shard_map/pallas_call | solution.py:42
  117.6 11.6 %collective-permute-start.6 = (bf16[2,256,256]{2,1,0:T(8,128)(2,1)S(1)}, bf16[2,256,256]{2,1,0:T(8,128)(2,1)S(1)}, u32[]{:S(2)}, u32[]{:S(2)}) collective-permute-start(bf16[2,256,256]{2,1,0:T(8,128)(2,1)S(1)} %get-tuple-element.10), channel_id=1, source_target_pairs={{0,32},{32,0},{64,96},{96,64},{1,33},{33,1},{65,97},{97,65},{2,34}... | collective-permute-start | bytes 786440 | tf_op jit(solution)/shard_map/ppermute | solution.py:24
  129.5 2.2 %shard_map.55 = bf16[16,32,256]{2,1,0:T(8,128)(2,1)} custom-call(s32[1]{0:T(128)} %bitcast.place_ref.x_ref, f32[128,1024]{1,0:T(8,128)S(1)} %shard_map.53.own_ref, bf16[4,128,1024]{2,1,0:T(8,128)(2,1)} %all-to-all-done.5.moved_ref), custom_call_target="tpu_custom_call" | custom-call | bytes 1835008 | tf_op jit(solution)/shard_map/pallas_call | solution.py:42
  131.7 4.1 %collective-permute-done.6 = bf16[2,256,256]{2,1,0:T(8,128)(2,1)S(1)} collective-permute-done((bf16[2,256,256]{2,1,0:T(8,128)(2,1)S(1)}, bf16[2,256,256]{2,1,0:T(8,128)(2,1)S(1)}, u32[]{:S(2)}, u32[]{:S(2)}) %collective-permute-start.6) | collective-permute-done | bytes 262176 | tf_op jit(solution)/shard_map/ppermute | solution.py:24
  135.8 3.5 %all-to-all-start.6 = ((bf16[16,32,256]{2,1,0:T(8,128)(2,1)}), bf16[16,32,256]{2,1,0:T(8,128)(2,1)S(1)}, u32[]{:S(2)}, u32[]{:S(2)}) async-start(bf16[16,32,256]{2,1,0:T(8,128)(2,1)} %shard_map.55), calls=%async_computation.6 | async-start | bytes 524288 | tf_op jit(solution)/shard_map/all_to_all | solution.py:28
  139.4 4.6 %collective-permute-start.7 = (bf16[256,256]{1,0:T(8,128)(2,1)S(1)}, bf16[256,256]{1,0:T(8,128)(2,1)S(1)}, u32[]{:S(2)}, u32[]{:S(2)}) collective-permute-start(bf16[256,256]{1,0:T(8,128)(2,1)S(1)} %fusion.4), channel_id=1, source_target_pairs={{0,64},{32,96},{64,0},{96,32},{1,65},{33,97},{65,1},{97,33},{2,66}... | collective-permute-start | bytes 393224 | tf_op jit(solution)/shard_map/ppermute | solution.py:24
  144.0 15.4 %collective-permute-done.7 = bf16[256,256]{1,0:T(8,128)(2,1)S(1)} collective-permute-done((bf16[256,256]{1,0:T(8,128)(2,1)S(1)}, bf16[256,256]{1,0:T(8,128)(2,1)S(1)}, u32[]{:S(2)}, u32[]{:S(2)}) %collective-permute-start.7) | collective-permute-done | bytes 131104 | tf_op jit(solution)/shard_map/ppermute | solution.py:24
  159.4 0.7 fusion.1
  160.1 0.7 bitcast_reduce_fusion
  (37 shorter events, 2.5 us)
Async XLA Ops:
  0.6 0.8 copy-start.1
  2.2 15.3 %copy-start.2 = (bf16[256,256]{1,0:T(8,128)(2,1)S(1)}, bf16[256,256]{1,0:T(8,128)(2,1)}, u32[]{:S(2)}) copy-start(bf16[256,256]{1,0:T(8,128)(2,1)} %param.4) | copy-start | bytes 393220
  2.2 36.2 %all-to-all-start = ((bf16[16,32,256]{2,1,0:T(8,128)(2,1)}), bf16[16,32,256]{2,1,0:T(8,128)(2,1)S(1)}, u32[]{:S(2)}, u32[]{:S(2)}) async-start(bf16[16,32,256]{2,1,0:T(8,128)(2,1)} %shard_map.50), calls=%async_computation | async-start | bytes 524288 | tf_op jit(solution)/shard_map/all_to_all | solution.py:28
  17.5 26.7 %collective-permute-start = (bf16[256,256]{1,0:T(8,128)(2,1)S(1)}, bf16[256,256]{1,0:T(8,128)(2,1)S(1)}, u32[]{:S(2)}, u32[]{:S(2)}) collective-permute-start(bf16[256,256]{1,0:T(8,128)(2,1)S(1)} %copy-done.2), channel_id=1, source_target_pairs={{0,32},{32,64},{64,96},{96,0},{1,33},{33,65},{65,97},{97,1},{2,34}... | collective-permute-start | bytes 393224 | tf_op jit(solution)/shard_map/ppermute | solution.py:20
  21.4 22.9 %collective-permute-start.1 = (bf16[256,256]{1,0:T(8,128)(2,1)S(1)}, bf16[256,256]{1,0:T(8,128)(2,1)S(1)}, u32[]{:S(2)}, u32[]{:S(2)}) collective-permute-start(bf16[256,256]{1,0:T(8,128)(2,1)S(1)} %copy-done.2), channel_id=1, source_target_pairs={{0,64},{32,96},{64,0},{96,32},{1,65},{33,97},{65,1},{97,33},{2,66}... | collective-permute-start | bytes 393224 | tf_op jit(solution)/shard_map/ppermute | solution.py:20
  25.7 18.6 %collective-permute-start.2 = (bf16[256,256]{1,0:T(8,128)(2,1)S(1)}, bf16[256,256]{1,0:T(8,128)(2,1)S(1)}, u32[]{:S(2)}, u32[]{:S(2)}) collective-permute-start(bf16[256,256]{1,0:T(8,128)(2,1)S(1)} %copy-done.2), channel_id=1, source_target_pairs={{0,96},{32,0},{64,32},{96,64},{1,97},{33,1},{65,33},{97,65},{2,98}... | collective-permute-start | bytes 393224 | tf_op jit(solution)/shard_map/ppermute | solution.py:20
  39.4 13.6 %all-to-all-start.1 = ((bf16[4,128,1024]{2,1,0:T(8,128)(2,1)}), bf16[4,128,1024]{2,1,0:T(8,128)(2,1)S(1)}, u32[]{:S(2)}, u32[]{:S(2)}) async-start(bf16[4,128,1024]{2,1,0:T(8,128)(2,1)} %shard_map.51), calls=%async_computation.1 | async-start | bytes 2097152 | tf_op jit(solution)/shard_map/all_to_all | solution.py:28
  44.3 8.7 %collective-permute-start.3 = (bf16[256,1024]{1,0:T(8,128)(2,1)S(1)}, bf16[256,1024]{1,0:T(8,128)(2,1)S(1)}, u32[]{:S(2)}, u32[]{:S(2)}) collective-permute-start(bf16[256,1024]{1,0:T(8,128)(2,1)S(1)} %constant_dynamic-update-slice_fusion.p_ref), channel_id=1, source_target_pairs={{0,1},{1,0},{2,3},{3,2},{4,5},{5,4},{6,7},{7,6},{8,9},{9,8},{10,11... | collective-permute-start | bytes 1572872 | tf_op jit(solution)/shard_map/ppermute | solution.py:20
  54.7 15.4 %all-to-all-start.2 = ((f32[4,128,512]{2,1,0:T(8,128)}), f32[4,128,512]{2,1,0:T(8,128)S(1)}, u32[]{:S(2)}, u32[]{:S(2)}) async-start(f32[4,128,512]{2,1,0:T(8,128)} %shard_map.52), calls=%async_computation.2 | async-start | bytes 2097152 | tf_op jit(solution)/shard_map/all_to_all | solution.py:28
  59.2 0.7 copy-start.3
  71.1 22.2 %all-to-all-start.3 = ((f32[16,1,384]{2,1,0:T(1,128)}), f32[16,1,384]{2,1,0:T(1,128)S(1)}, u32[]{:S(2)}, u32[]{:S(2)}) async-start(f32[16,1,384]{2,1,0:T(1,128)} %broadcast_in_dim.14), calls=%async_computation.3 | async-start | bytes 49152 | tf_op jit(solution)/shard_map/all_to_all | solution.py:28
  80.4 33.7 %collective-permute-start.5 = (bf16[512,1024]{1,0:T(8,128)(2,1)S(1)}, bf16[512,1024]{1,0:T(8,128)(2,1)}, u32[]{:S(2)}, u32[]{:S(2)}) collective-permute-start(bf16[512,1024]{1,0:T(8,128)(2,1)S(1)} %bitcast.30), channel_id=1, source_target_pairs={{0,1},{1,0},{2,3},{3,2},{4,5},{5,4},{6,7},{7,6},{8,9},{9,8},{10,11... | collective-permute-start | bytes 3145736 | tf_op jit(solution)/shard_map/ppermute | solution.py:20
  104.9 1.0 copy-start
  105.9 23.6 %all-to-all-start.5 = ((bf16[4,128,1024]{2,1,0:T(8,128)(2,1)}), bf16[4,128,1024]{2,1,0:T(8,128)(2,1)}, u32[]{:S(2)}, u32[]{:S(2)}) async-start(bf16[4,128,1024]{2,1,0:T(8,128)(2,1)} %copy-done), calls=%async_computation.5 | async-start | bytes 2097152 | tf_op jit(solution)/shard_map/all_to_all | solution.py:28
  112.2 3.4 %collective-permute-start.4 = (bf16[4,4,32,256]{3,2,1,0:T(8,128)(2,1)S(1)}, bf16[4,4,32,256]{3,2,1,0:T(8,128)(2,1)S(1)}, u32[]{:S(2)}, u32[]{:S(2)}) collective-permute-start(bf16[4,4,32,256]{3,2,1,0:T(8,128)(2,1)S(1)} %slice.55), channel_id=1, source_target_pairs={{0,1},{1,0},{2,3},{3,2},{4,5},{5,4},{6,7},{7,6},{8,9},{9,8},{10,11... | collective-permute-start | bytes 786440 | tf_op jit(solution)/shard_map/ppermute | solution.py:20
  117.6 18.2 %collective-permute-start.6 = (bf16[2,256,256]{2,1,0:T(8,128)(2,1)S(1)}, bf16[2,256,256]{2,1,0:T(8,128)(2,1)S(1)}, u32[]{:S(2)}, u32[]{:S(2)}) collective-permute-start(bf16[2,256,256]{2,1,0:T(8,128)(2,1)S(1)} %get-tuple-element.10), channel_id=1, source_target_pairs={{0,32},{32,0},{64,96},{96,64},{1,33},{33,1},{65,97},{97,65},{2,34}... | collective-permute-start | bytes 786440 | tf_op jit(solution)/shard_map/ppermute | solution.py:24
  135.8 24.3 %all-to-all-start.6 = ((bf16[16,32,256]{2,1,0:T(8,128)(2,1)}), bf16[16,32,256]{2,1,0:T(8,128)(2,1)S(1)}, u32[]{:S(2)}, u32[]{:S(2)}) async-start(bf16[16,32,256]{2,1,0:T(8,128)(2,1)} %shard_map.55), calls=%async_computation.6 | async-start | bytes 524288 | tf_op jit(solution)/shard_map/all_to_all | solution.py:28
  139.4 20.0 %collective-permute-start.7 = (bf16[256,256]{1,0:T(8,128)(2,1)S(1)}, bf16[256,256]{1,0:T(8,128)(2,1)S(1)}, u32[]{:S(2)}, u32[]{:S(2)}) collective-permute-start(bf16[256,256]{1,0:T(8,128)(2,1)S(1)} %fusion.4), channel_id=1, source_target_pairs={{0,64},{32,96},{64,0},{96,32},{1,65},{33,97},{65,1},{97,33},{2,66}... | collective-permute-start | bytes 393224 | tf_op jit(solution)/shard_map/ppermute | solution.py:24

commit v5 on v4

--- a/solution.py
+++ b/solution.py
@@ -13,6 +13,7 @@
 BF = jnp.bfloat16
 F32 = jnp.float32
 BAND = 32
+LONG = 10**10
 
 
 def shift(value, axis, step):
@@ -75,6 +76,12 @@
             keep_ref[i] = block
         else:
             send_ref[i - 2] = block.astype(BF)
+
+
+def pair_kernel(place_ref, keep_ref, arrived_ref, own_ref, send_ref):
+    del place_ref
+    own_ref[...] = keep_ref[0] + arrived_ref[0].astype(F32)
+    send_ref[...] = (keep_ref[1] + arrived_ref[1].astype(F32)).astype(BF)
 
 
 def spread_kernel(place_ref, in_ref, out_ref):
@@ -192,9 +199,12 @@
         flops, zl, weights, far_weights, near, far,
     )
     arrived = flip(send, "zl", 1)
-    back, arrived = lax.optimization_barrier((back, arrived))
-    passage_grad = keep[0] + arrived[0].astype(F32)
-    passage_grad += flip((keep[1] + arrived[1].astype(F32)).astype(BF), "zl", 2).astype(F32)
+    passage_grad, send = call(
+        pair_kernel,
+        [jax.ShapeDtypeStruct((count, width), F32), jax.ShapeDtypeStruct((count, width), BF)],
+        LONG, zl, keep, arrived,
+    )
+    passage_grad += flip(send, "zl", 2).astype(F32)
 
     back = exchange(back, COLUMN).reshape(n_zh, rows, width)
     query_grad = jnp.sum(back.astype(F32), axis=0)

time: 162 us -> 161 us (level)
  the two profiles are of different devices: /device:TPU:6 before, /device:TPU:8 now
where the time goes in v5:
time: 161 us; the launch traced here: 160 us
  starting transfers between devices  75.8 us (47%)
  waiting for transfers between devices  58.5 us (36%)
  blocking collectives  10.5 us (7%)
  Pallas kernels  8.73 us (5%)
  local copies, waits for them, and re-layouts  3.4 us (2%)
  other arithmetic  1.98 us (1%)
    all_to_all x6, waiting for transfers between devices, exchange(): return lax.all_to_all(blocks, axis, 0, 0, tiled=True)  44.4 us
    all_to_all x6, starting transfers between devices, exchange(): return lax.all_to_all(blocks, axis, 0, 0, tiled=True)  42.3 us
    ppermute x6, starting transfers between devices, shift(): return lax.ppermute(value, axis, [(i, (i + step) % n) for i in range(n)])  17.2 us
    ppermute x2, starting transfers between devices, flip(): lax.ppermute(value, axis, [(i, i ^ bit) for i in range(lax.axis_size(axis...  16.3 us
    ppermute x2, waiting for transfers between devices, flip(): lax.ppermute(value, axis, [(i, i ^ bit) for i in range(lax.axis_size(axis...  12.6 us
    all_to_all x1, blocking collectives, exchange(): return lax.all_to_all(blocks, axis, 0, 0, tiled=True)  10.5 us
    pallas_call x8, Pallas kernels, call(): pl.pallas_call(kernel, out_shape=outs, in_specs=[pl.BlockSpec(memory_spac...  8.73 us
  transfers between devices with their start and end apart: 14, of which 7 were waited for; matrix products, arithmetic and copies ran while one was open for 1% of the time, Pallas kernels for 4%

profile of v5, /device:TPU:8, one launch (start us, length us, event | category | flops | bytes accessed | tf_op | source)
XLA Modules:
  0.0 159.9 jit_solution(13354801585803490079)
XLA Ops:
  0.6 0.8 copy-done.1
  1.5 0.7 shard_map.50
  2.2 15.3 %all-to-all-start = ((bf16[16,32,256]{2,1,0:T(8,128)(2,1)}), bf16[16,32,256]{2,1,0:T(8,128)(2,1)S(1)}, u32[]{:S(2)}, u32[]{:S(2)}) async-start(bf16[16,32,256]{2,1,0:T(8,128)(2,1)} %shard_map.50), calls=%async_computation | async-start | bytes 524288 | tf_op jit(solution)/shard_map/all_to_all | solution.py:29
  17.6 3.8 %collective-permute-start = (bf16[256,256]{1,0:T(8,128)(2,1)S(1)}, bf16[256,256]{1,0:T(8,128)(2,1)S(1)}, u32[]{:S(2)}, u32[]{:S(2)}) collective-permute-start(bf16[256,256]{1,0:T(8,128)(2,1)S(1)} %copy-done.2), channel_id=1, source_target_pairs={{0,32},{32,64},{64,96},{96,0},{1,33},{33,65},{65,97},{97,1},{2,34}... | collective-permute-start | bytes 393224 | tf_op jit(solution)/shard_map/ppermute | solution.py:21
  21.4 4.3 %collective-permute-start.1 = (bf16[256,256]{1,0:T(8,128)(2,1)S(1)}, bf16[256,256]{1,0:T(8,128)(2,1)S(1)}, u32[]{:S(2)}, u32[]{:S(2)}) collective-permute-start(bf16[256,256]{1,0:T(8,128)(2,1)S(1)} %copy-done.2), channel_id=1, source_target_pairs={{0,64},{32,96},{64,0},{96,32},{1,65},{33,97},{65,1},{97,33},{2,66}... | collective-permute-start | bytes 393224 | tf_op jit(solution)/shard_map/ppermute | solution.py:21
  25.7 3.4 %collective-permute-start.2 = (bf16[256,256]{1,0:T(8,128)(2,1)S(1)}, bf16[256,256]{1,0:T(8,128)(2,1)S(1)}, u32[]{:S(2)}, u32[]{:S(2)}) collective-permute-start(bf16[256,256]{1,0:T(8,128)(2,1)S(1)} %copy-done.2), channel_id=1, source_target_pairs={{0,96},{32,0},{64,32},{96,64},{1,97},{33,1},{65,33},{97,65},{2,98}... | collective-permute-start | bytes 393224 | tf_op jit(solution)/shard_map/ppermute | solution.py:21
  29.2 9.2 %all-to-all-done.in_ref = bf16[16,32,256]{2,1,0:T(8,128)(2,1)S(1)} async-done(((bf16[16,32,256]{2,1,0:T(8,128)(2,1)}), bf16[16,32,256]{2,1,0:T(8,128)(2,1)S(1)}, u32[]{:S(2)}, u32[]{:S(2)}) %all-to-all-start) | async-done | bytes 262176 | tf_op jit(solution)/shard_map/all_to_all | solution.py:29
  38.4 1.1 shard_map.51
  39.5 4.3 %all-to-all-start.1 = ((bf16[4,128,1024]{2,1,0:T(8,128)(2,1)}), bf16[4,128,1024]{2,1,0:T(8,128)(2,1)S(1)}, u32[]{:S(2)}, u32[]{:S(2)}) async-start(bf16[4,128,1024]{2,1,0:T(8,128)(2,1)} %shard_map.51), calls=%async_computation.1 | async-start | bytes 2097152 | tf_op jit(solution)/shard_map/all_to_all | solution.py:29
  43.8 1.9 %collective-permute-start.3 = (bf16[256,1024]{1,0:T(8,128)(2,1)S(1)}, bf16[256,1024]{1,0:T(8,128)(2,1)S(1)}, u32[]{:S(2)}, u32[]{:S(2)}) collective-permute-start(bf16[256,1024]{1,0:T(8,128)(2,1)S(1)} %constant_dynamic-update-slice_fusion.p_ref), channel_id=1, source_target_pairs={{0,1},{1,0},{2,3},{3,2},{4,5},{5,4},{6,7},{7,6},{8,9},{9,8},{10,11... | collective-permute-start | bytes 1572872 | tf_op jit(solution)/shard_map/ppermute | solution.py:21
  45.8 8.9 %all-to-all-done.1 = bf16[4,128,1024]{2,1,0:T(8,128)(2,1)S(1)} async-done(((bf16[4,128,1024]{2,1,0:T(8,128)(2,1)}), bf16[4,128,1024]{2,1,0:T(8,128)(2,1)S(1)}, u32[]{:S(2)}, u32[]{:S(2)}) %all-to-all-start.1) | async-done | bytes 1048608 | tf_op jit(solution)/shard_map/all_to_all | solution.py:29
  54.7 1.7 %shard_map.52 = f32[4,128,512]{2,1,0:T(8,128)} custom-call(s32[1]{0:T(128)} %bitcast.place_ref.x_ref, bf16[512,1024]{1,0:T(8,128)(2,1)S(1)} %bitcast.23, bf16[256,1024]{1,0:T(8,128)(2,1)S(1)} %constant_dynamic-update-slice_fusion.p_ref, bf16[256,1024]{1,0:T(8,128)(2,1)S(1)} %collective-permute-done.3.p_other_ref), custom_call_target="tpu_custom_call" | custom-call | flops 536870912 | bytes 3145728 | tf_op jit(solution)/shard_map/pallas_call | solution.py:43
  56.4 4.9 %all-to-all-start.2 = ((f32[4,128,512]{2,1,0:T(8,128)}), f32[4,128,512]{2,1,0:T(8,128)S(1)}, u32[]{:S(2)}, u32[]{:S(2)}) async-start(f32[4,128,512]{2,1,0:T(8,128)} %shard_map.52), calls=%async_computation.2 | async-start | bytes 2097152 | tf_op jit(solution)/shard_map/all_to_all | solution.py:29
  62.0 8.7 %all-to-all-done.2 = f32[4,128,512]{2,1,0:T(8,128)S(1)} async-done(((f32[4,128,512]{2,1,0:T(8,128)}), f32[4,128,512]{2,1,0:T(8,128)S(1)}, u32[]{:S(2)}, u32[]{:S(2)}) %all-to-all-start.2) | async-done | bytes 1048608 | tf_op jit(solution)/shard_map/all_to_all | solution.py:29
  71.7 7.3 %all-to-all-start.3 = ((f32[16,1,384]{2,1,0:T(1,128)}), f32[16,1,384]{2,1,0:T(1,128)S(1)}, u32[]{:S(2)}, u32[]{:S(2)}) async-start(f32[16,1,384]{2,1,0:T(1,128)} %broadcast_in_dim.14), calls=%async_computation.3 | async-start | bytes 49152 | tf_op jit(solution)/shard_map/all_to_all | solution.py:29
  79.0 1.9 %collective-permute-start.5 = (bf16[512,1024]{1,0:T(8,128)(2,1)S(1)}, bf16[512,1024]{1,0:T(8,128)(2,1)}, u32[]{:S(2)}, u32[]{:S(2)}) collective-permute-start(bf16[512,1024]{1,0:T(8,128)(2,1)S(1)} %bitcast.24), channel_id=1, source_target_pairs={{0,1},{1,0},{2,3},{3,2},{4,5},{5,4},{6,7},{7,6},{8,9},{9,8},{10,11... | collective-permute-start | bytes 3145736 | tf_op jit(solution)/shard_map/ppermute | solution.py:21
  81.0 13.0 %all-to-all-done.3 = f32[16,1,384]{2,1,0:T(1,128)S(1)} async-done(((f32[16,1,384]{2,1,0:T(1,128)}), f32[16,1,384]{2,1,0:T(1,128)S(1)}, u32[]{:S(2)}, u32[]{:S(2)}) %all-to-all-start.3) | async-done | bytes 24608 | tf_op jit(solution)/shard_map/all_to_all | solution.py:29
  94.3 10.5 %all_to_all.39 = bf16[4,128,512]{2,1,0:T(8,128)(2,1)S(1)} all-to-all(bf16[4,128,512]{2,1,0:T(8,128)(2,1)S(1)} %broadcast_in_dim.15), channel_id=1, replica_groups=mesh['y'=4,'zl'=4,'zh'=4,'x'=4,'c'=2] {'y'}, dimensions={0} | all-to-all | bytes 1048576 | tf_op jit(solution)/shard_map/all_to_all | solution.py:29
  104.8 0.7 shard_map.54
  105.5 1.0 copy-done
  106.5 4.3 %all-to-all-start.5 = ((bf16[4,128,1024]{2,1,0:T(8,128)(2,1)}), bf16[4,128,1024]{2,1,0:T(8,128)(2,1)}, u32[]{:S(2)}, u32[]{:S(2)}) async-start(bf16[4,128,1024]{2,1,0:T(8,128)(2,1)} %copy-done), calls=%async_computation.5 | async-start | bytes 2097152 | tf_op jit(solution)/shard_map/all_to_all | solution.py:29
  110.8 1.9 %collective-permute-start.4 = (bf16[4,4,32,256]{3,2,1,0:T(8,128)(2,1)S(1)}, bf16[4,4,32,256]{3,2,1,0:T(8,128)(2,1)S(1)}, u32[]{:S(2)}, u32[]{:S(2)}) collective-permute-start(bf16[4,4,32,256]{3,2,1,0:T(8,128)(2,1)S(1)} %slice.39), channel_id=1, source_target_pairs={{0,1},{1,0},{2,3},{3,2},{4,5},{5,4},{6,7},{7,6},{8,9},{9,8},{10,11... | collective-permute-start | bytes 786440 | tf_op jit(solution)/shard_map/ppermute | solution.py:21
  112.8 1.5 collective-permute-done.4.far_w_ref
  114.2 2.0 %shard_map.56 = (f32[2,256,256]{2,1,0:T(8,128)S(1)}, bf16[2,256,256]{2,1,0:T(8,128)(2,1)S(1)}) custom-call(s32[1]{0:T(128)} %bitcast.6.zl_ref.place_ref, bf16[4,4,32,512]{3,2,1,0:T(8,128)(2,1)S(1)} %bitcast.21, bf16[4,4,32,256]{3,2,1,0:T(8,128)(2,1)S(1)} %collective-permute-done.4.far_w_ref, bf16[512,1024]{1,0:T(8,128)(2,1)S(1)} %bitcast.25, ...), custom_call_target="tpu_custom_call" | custom-call | flops 536870912 | bytes 3670016 | tf_op jit(solution)/shard_map/pallas_call | solution.py:43
  116.2 11.6 %collective-permute-start.6 = (bf16[2,256,256]{2,1,0:T(8,128)(2,1)S(1)}, bf16[2,256,256]{2,1,0:T(8,128)(2,1)S(1)}, u32[]{:S(2)}, u32[]{:S(2)}) collective-permute-start(bf16[2,256,256]{2,1,0:T(8,128)(2,1)S(1)} %get-tuple-element.11), channel_id=1, source_target_pairs={{0,32},{32,0},{64,96},{96,64},{1,33},{33,1},{65,97},{97,65},{2,34}... | collective-permute-start | bytes 786440 | tf_op jit(solution)/shard_map/ppermute | solution.py:25
  128.2 2.1 %shard_map.55 = bf16[16,32,256]{2,1,0:T(8,128)(2,1)} custom-call(s32[1]{0:T(128)} %bitcast.place_ref.x_ref, f32[128,1024]{1,0:T(8,128)S(1)} %shard_map.53.own_ref, bf16[4,128,1024]{2,1,0:T(8,128)(2,1)} %all-to-all-done.5.moved_ref), custom_call_target="tpu_custom_call" | custom-call | bytes 1835008 | tf_op jit(solution)/shard_map/pallas_call | solution.py:43
  130.3 6.2 %all-to-all-start.6 = ((bf16[16,32,256]{2,1,0:T(8,128)(2,1)}), bf16[16,32,256]{2,1,0:T(8,128)(2,1)S(1)}, u32[]{:S(2)}, u32[]{:S(2)}) async-start(bf16[16,32,256]{2,1,0:T(8,128)(2,1)} %shard_map.55), calls=%async_computation.6 | async-start | bytes 524288 | tf_op jit(solution)/shard_map/all_to_all | solution.py:29
  136.6 4.7 %collective-permute-start.7 = (bf16[256,256]{1,0:T(8,128)(2,1)S(1)}, bf16[256,256]{1,0:T(8,128)(2,1)S(1)}, u32[]{:S(2)}, u32[]{:S(2)}) collective-permute-start(bf16[256,256]{1,0:T(8,128)(2,1)S(1)} %get-tuple-element.13), channel_id=1, source_target_pairs={{0,64},{32,96},{64,0},{96,32},{1,65},{33,97},{65,1},{97,33},{2,66}... | collective-permute-start | bytes 393224 | tf_op jit(solution)/shard_map/ppermute | solution.py:25
  141.3 12.6 %collective-permute-done.7 = bf16[256,256]{1,0:T(8,128)(2,1)S(1)} collective-permute-done((bf16[256,256]{1,0:T(8,128)(2,1)S(1)}, bf16[256,256]{1,0:T(8,128)(2,1)S(1)}, u32[]{:S(2)}, u32[]{:S(2)}) %collective-permute-start.7) | collective-permute-done | bytes 131104 | tf_op jit(solution)/shard_map/ppermute | solution.py:25
  153.9 0.7 add_convert_fusion
  154.6 4.7 %all-to-all-done.6 = bf16[16,32,256]{2,1,0:T(8,128)(2,1)S(1)} async-done(((bf16[16,32,256]{2,1,0:T(8,128)(2,1)}), bf16[16,32,256]{2,1,0:T(8,128)(2,1)S(1)}, u32[]{:S(2)}, u32[]{:S(2)}) %all-to-all-start.6) | async-done | bytes 262176 | tf_op jit(solution)/shard_map/all_to_all | solution.py:29
  159.3 0.7 bitcast_reduce_fusion
  (37 shorter events, 2.6 us)
Async XLA Ops:
  0.6 0.8 copy-start.1
  2.2 15.3 %copy-start.2 = (bf16[256,256]{1,0:T(8,128)(2,1)S(1)}, bf16[256,256]{1,0:T(8,128)(2,1)}, u32[]{:S(2)}) copy-start(bf16[256,256]{1,0:T(8,128)(2,1)} %param.4) | copy-start | bytes 393220
  2.2 36.2 %all-to-all-start = ((bf16[16,32,256]{2,1,0:T(8,128)(2,1)}), bf16[16,32,256]{2,1,0:T(8,128)(2,1)S(1)}, u32[]{:S(2)}, u32[]{:S(2)}) async-start(bf16[16,32,256]{2,1,0:T(8,128)(2,1)} %shard_map.50), calls=%async_computation | async-start | bytes 524288 | tf_op jit(solution)/shard_map/all_to_all | solution.py:29
  17.6 26.2 %collective-permute-start = (bf16[256,256]{1,0:T(8,128)(2,1)S(1)}, bf16[256,256]{1,0:T(8,128)(2,1)S(1)}, u32[]{:S(2)}, u32[]{:S(2)}) collective-permute-start(bf16[256,256]{1,0:T(8,128)(2,1)S(1)} %copy-done.2), channel_id=1, source_target_pairs={{0,32},{32,64},{64,96},{96,0},{1,33},{33,65},{65,97},{97,1},{2,34}... | collective-permute-start | bytes 393224 | tf_op jit(solution)/shard_map/ppermute | solution.py:21
  21.4 22.4 %collective-permute-start.1 = (bf16[256,256]{1,0:T(8,128)(2,1)S(1)}, bf16[256,256]{1,0:T(8,128)(2,1)S(1)}, u32[]{:S(2)}, u32[]{:S(2)}) collective-permute-start(bf16[256,256]{1,0:T(8,128)(2,1)S(1)} %copy-done.2), channel_id=1, source_target_pairs={{0,64},{32,96},{64,0},{96,32},{1,65},{33,97},{65,1},{97,33},{2,66}... | collective-permute-start | bytes 393224 | tf_op jit(solution)/shard_map/ppermute | solution.py:21
  25.7 18.1 %collective-permute-start.2 = (bf16[256,256]{1,0:T(8,128)(2,1)S(1)}, bf16[256,256]{1,0:T(8,128)(2,1)S(1)}, u32[]{:S(2)}, u32[]{:S(2)}) collective-permute-start(bf16[256,256]{1,0:T(8,128)(2,1)S(1)} %copy-done.2), channel_id=1, source_target_pairs={{0,96},{32,0},{64,32},{96,64},{1,97},{33,1},{65,33},{97,65},{2,98}... | collective-permute-start | bytes 393224 | tf_op jit(solution)/shard_map/ppermute | solution.py:21
  39.5 15.2 %all-to-all-start.1 = ((bf16[4,128,1024]{2,1,0:T(8,128)(2,1)}), bf16[4,128,1024]{2,1,0:T(8,128)(2,1)S(1)}, u32[]{:S(2)}, u32[]{:S(2)}) async-start(bf16[4,128,1024]{2,1,0:T(8,128)(2,1)} %shard_map.51), calls=%async_computation.1 | async-start | bytes 2097152 | tf_op jit(solution)/shard_map/all_to_all | solution.py:29
  43.8 10.8 %collective-permute-start.3 = (bf16[256,1024]{1,0:T(8,128)(2,1)S(1)}, bf16[256,1024]{1,0:T(8,128)(2,1)S(1)}, u32[]{:S(2)}, u32[]{:S(2)}) collective-permute-start(bf16[256,1024]{1,0:T(8,128)(2,1)S(1)} %constant_dynamic-update-slice_fusion.p_ref), channel_id=1, source_target_pairs={{0,1},{1,0},{2,3},{3,2},{4,5},{5,4},{6,7},{7,6},{8,9},{9,8},{10,11... | collective-permute-start | bytes 1572872 | tf_op jit(solution)/shard_map/ppermute | solution.py:21
  56.4 14.3 %all-to-all-start.2 = ((f32[4,128,512]{2,1,0:T(8,128)}), f32[4,128,512]{2,1,0:T(8,128)S(1)}, u32[]{:S(2)}, u32[]{:S(2)}) async-start(f32[4,128,512]{2,1,0:T(8,128)} %shard_map.52), calls=%async_computation.2 | async-start | bytes 2097152 | tf_op jit(solution)/shard_map/all_to_all | solution.py:29
  61.3 0.7 copy-start.3
  71.7 22.2 %all-to-all-start.3 = ((f32[16,1,384]{2,1,0:T(1,128)}), f32[16,1,384]{2,1,0:T(1,128)S(1)}, u32[]{:S(2)}, u32[]{:S(2)}) async-start(f32[16,1,384]{2,1,0:T(1,128)} %broadcast_in_dim.14), calls=%async_computation.3 | async-start | bytes 49152 | tf_op jit(solution)/shard_map/all_to_all | solution.py:29
  79.0 33.7 %collective-permute-start.5 = (bf16[512,1024]{1,0:T(8,128)(2,1)S(1)}, bf16[512,1024]{1,0:T(8,128)(2,1)}, u32[]{:S(2)}, u32[]{:S(2)}) collective-permute-start(bf16[512,1024]{1,0:T(8,128)(2,1)S(1)} %bitcast.24), channel_id=1, source_target_pairs={{0,1},{1,0},{2,3},{3,2},{4,5},{5,4},{6,7},{7,6},{8,9},{9,8},{10,11... | collective-permute-start | bytes 3145736 | tf_op jit(solution)/shard_map/ppermute | solution.py:21
  105.5 1.0 copy-start
  106.5 21.6 %all-to-all-start.5 = ((bf16[4,128,1024]{2,1,0:T(8,128)(2,1)}), bf16[4,128,1024]{2,1,0:T(8,128)(2,1)}, u32[]{:S(2)}, u32[]{:S(2)}) async-start(bf16[4,128,1024]{2,1,0:T(8,128)(2,1)} %copy-done), calls=%async_computation.5 | async-start | bytes 2097152 | tf_op jit(solution)/shard_map/all_to_all | solution.py:29
  110.8 3.4 %collective-permute-start.4 = (bf16[4,4,32,256]{3,2,1,0:T(8,128)(2,1)S(1)}, bf16[4,4,32,256]{3,2,1,0:T(8,128)(2,1)S(1)}, u32[]{:S(2)}, u32[]{:S(2)}) collective-permute-start(bf16[4,4,32,256]{3,2,1,0:T(8,128)(2,1)S(1)} %slice.39), channel_id=1, source_target_pairs={{0,1},{1,0},{2,3},{3,2},{4,5},{5,4},{6,7},{7,6},{8,9},{9,8},{10,11... | collective-permute-start | bytes 786440 | tf_op jit(solution)/shard_map/ppermute | solution.py:21
  116.2 20.3 %collective-permute-start.6 = (bf16[2,256,256]{2,1,0:T(8,128)(2,1)S(1)}, bf16[2,256,256]{2,1,0:T(8,128)(2,1)S(1)}, u32[]{:S(2)}, u32[]{:S(2)}) collective-permute-start(bf16[2,256,256]{2,1,0:T(8,128)(2,1)S(1)} %get-tuple-element.11), channel_id=1, source_target_pairs={{0,32},{32,0},{64,96},{96,64},{1,33},{33,1},{65,97},{97,65},{2,34}... | collective-permute-start | bytes 786440 | tf_op jit(solution)/shard_map/ppermute | solution.py:25
  130.3 28.9 %all-to-all-start.6 = ((bf16[16,32,256]{2,1,0:T(8,128)(2,1)}), bf16[16,32,256]{2,1,0:T(8,128)(2,1)S(1)}, u32[]{:S(2)}, u32[]{:S(2)}) async-start(bf16[16,32,256]{2,1,0:T(8,128)(2,1)} %shard_map.55), calls=%async_computation.6 | async-start | bytes 524288 | tf_op jit(solution)/shard_map/all_to_all | solution.py:29
  136.6 17.3 %collective-permute-start.7 = (bf16[256,256]{1,0:T(8,128)(2,1)S(1)}, bf16[256,256]{1,0:T(8,128)(2,1)S(1)}, u32[]{:S(2)}, u32[]{:S(2)}) collective-permute-start(bf16[256,256]{1,0:T(8,128)(2,1)S(1)} %get-tuple-element.13), channel_id=1, source_target_pairs={{0,64},{32,96},{64,0},{96,32},{1,65},{33,97},{65,1},{97,33},{2,66}... | collective-permute-start | bytes 393224 | tf_op jit(solution)/shard_map/ppermute | solution.py:25

commit v6 on v5

--- a/solution.py
+++ b/solution.py
@@ -9,7 +9,7 @@
 
 ROWS = ("zh", "x", "c")
 FEATS = ("y", "zl")
-COLUMN = ("zh", "zl")
+COLUMN = ("zl", "zh")
 BF = jnp.bfloat16
 F32 = jnp.float32
 BAND = 32
@@ -89,7 +89,7 @@
     n, band, _ = out_ref.shape
     n_bands = in_ref.shape[0] // band
     for i in range(n):
-        out_ref[i] = in_ref[pl.ds(i % n_bands * band, band), :]
+        out_ref[i] = in_ref[pl.ds(i // (n // n_bands) * band, band), :]
 
 
 def collect_kernel(place_ref, in_ref, out_ref):
@@ -98,8 +98,8 @@
     n_zl = out_ref.shape[2] // width
     for i in range(n):
         for x in range(out_ref.shape[0]):
-            at = i // n_zl * band
-            out_ref[x, at : at + band, i % n_zl * width : (i % n_zl + 1) * width] = in_ref[i]
+            z, l = i % (n // n_zl), i // (n // n_zl)
+            out_ref[x, z * band : (z + 1) * band, l * width : (l + 1) * width] = in_ref[i]
 
 
 def query_block(w_ref, p_ref, p_other_ref, x):
@@ -127,7 +127,7 @@
         total = total + jnp.where(x_ref[0] == x, 0.0, moved_ref[x].astype(F32))
     for z in range(n_blocks // n_zl):
         for l in range(n_zl):
-            out_ref[z * n_zl + l] = total[z * band : (z + 1) * band, l * width : (l + 1) * width].astype(BF)
+            out_ref[l * (n_blocks // n_zl) + z] = total[z * band : (z + 1) * band, l * width : (l + 1) * width].astype(BF)
 
 
 def per_device(queries, passages, positive):
@@ -206,8 +206,8 @@
     )
     passage_grad += flip(send, "zl", 2).astype(F32)
 
-    back = exchange(back, COLUMN).reshape(n_zh, rows, width)
-    query_grad = jnp.sum(back.astype(F32), axis=0)
+    back = exchange(back, COLUMN).reshape(n_zl, n_zh, band, width)
+    query_grad = jnp.sum(back.astype(F32), axis=1).reshape(rows, width)
     return query_grad.astype(BF), passage_grad.astype(BF)
 
 

time: 161 us -> 152 us (0.944)
  the two profiles are of different devices: /device:TPU:8 before, /device:TPU:6 now
where the time goes in v6:
time: 152 us; the launch traced here: 149 us
  starting transfers between devices  71.8 us (47%)
  waiting for transfers between devices  51.9 us (34%)
  blocking collectives  10.5 us (7%)
  Pallas kernels  8.75 us (6%)
  local copies, waits for them, and re-layouts  3.39 us (2%)
  other arithmetic  1.98 us (1%)
    all_to_all x6, starting transfers between devices, exchange(): return lax.all_to_all(blocks, axis, 0, 0, tiled=True)  47.7 us
    all_to_all x6, waiting for transfers between devices, exchange(): return lax.all_to_all(blocks, axis, 0, 0, tiled=True)  36.3 us
    ppermute x6, starting transfers between devices, shift(): return lax.ppermute(value, axis, [(i, (i + step) % n) for i in range(n)])  17.2 us
    ppermute x2, waiting for transfers between devices, flip(): lax.ppermute(value, axis, [(i, i ^ bit) for i in range(lax.axis_size(axis...  14.1 us
    all_to_all x1, blocking collectives, exchange(): return lax.all_to_all(blocks, axis, 0, 0, tiled=True)  10.5 us
    pallas_call x8, Pallas kernels, call(): pl.pallas_call(kernel, out_shape=outs, in_specs=[pl.BlockSpec(memory_spac...  8.75 us
    ppermute x2, starting transfers between devices, flip(): lax.ppermute(value, axis, [(i, i ^ bit) for i in range(lax.axis_size(axis...  6.85 us
  transfers between devices with their start and end apart: 14, of which 8 were waited for; matrix products, arithmetic and copies ran while one was open for 1% of the time, Pallas kernels for 4%

profile of v6, /device:TPU:6, one launch (start us, length us, event | category | flops | bytes accessed | tf_op | source)
XLA Modules:
  0.0 149.3 jit_solution(8804796789337105775)
XLA Ops:
  0.6 0.8 copy-done.1
  1.5 0.7 shard_map.50
  2.2 15.3 %all-to-all-start = ((bf16[16,32,256]{2,1,0:T(8,128)(2,1)}), bf16[16,32,256]{2,1,0:T(8,128)(2,1)S(1)}, u32[]{:S(2)}, u32[]{:S(2)}) async-start(bf16[16,32,256]{2,1,0:T(8,128)(2,1)} %shard_map.50), calls=%async_computation | async-start | bytes 524288 | tf_op jit(solution)/shard_map/all_to_all | solution.py:29
  17.6 3.8 %collective-permute-start = (bf16[256,256]{1,0:T(8,128)(2,1)S(1)}, bf16[256,256]{1,0:T(8,128)(2,1)S(1)}, u32[]{:S(2)}, u32[]{:S(2)}) collective-permute-start(bf16[256,256]{1,0:T(8,128)(2,1)S(1)} %copy-done.2), channel_id=1, source_target_pairs={{0,32},{32,64},{64,96},{96,0},{1,33},{33,65},{65,97},{97,1},{2,34}... | collective-permute-start | bytes 393224 | tf_op jit(solution)/shard_map/ppermute | solution.py:21
  21.4 4.3 %collective-permute-start.1 = (bf16[256,256]{1,0:T(8,128)(2,1)S(1)}, bf16[256,256]{1,0:T(8,128)(2,1)S(1)}, u32[]{:S(2)}, u32[]{:S(2)}) collective-permute-start(bf16[256,256]{1,0:T(8,128)(2,1)S(1)} %copy-done.2), channel_id=1, source_target_pairs={{0,64},{32,96},{64,0},{96,32},{1,65},{33,97},{65,1},{97,33},{2,66}... | collective-permute-start | bytes 393224 | tf_op jit(solution)/shard_map/ppermute | solution.py:21
  25.7 3.4 %collective-permute-start.2 = (bf16[256,256]{1,0:T(8,128)(2,1)S(1)}, bf16[256,256]{1,0:T(8,128)(2,1)S(1)}, u32[]{:S(2)}, u32[]{:S(2)}) collective-permute-start(bf16[256,256]{1,0:T(8,128)(2,1)S(1)} %copy-done.2), channel_id=1, source_target_pairs={{0,96},{32,0},{64,32},{96,64},{1,97},{33,1},{65,33},{97,65},{2,98}... | collective-permute-start | bytes 393224 | tf_op jit(solution)/shard_map/ppermute | solution.py:21
  29.2 6.4 %all-to-all-done.in_ref = bf16[16,32,256]{2,1,0:T(8,128)(2,1)S(1)} async-done(((bf16[16,32,256]{2,1,0:T(8,128)(2,1)}), bf16[16,32,256]{2,1,0:T(8,128)(2,1)S(1)}, u32[]{:S(2)}, u32[]{:S(2)}) %all-to-all-start) | async-done | bytes 262176 | tf_op jit(solution)/shard_map/all_to_all | solution.py:29
  35.6 1.1 shard_map.51
  36.7 4.8 %all-to-all-start.1 = ((bf16[4,128,1024]{2,1,0:T(8,128)(2,1)}), bf16[4,128,1024]{2,1,0:T(8,128)(2,1)S(1)}, u32[]{:S(2)}, u32[]{:S(2)}) async-start(bf16[4,128,1024]{2,1,0:T(8,128)(2,1)} %shard_map.51), calls=%async_computation.1 | async-start | bytes 2097152 | tf_op jit(solution)/shard_map/all_to_all | solution.py:29
  41.5 1.9 %collective-permute-start.3 = (bf16[256,1024]{1,0:T(8,128)(2,1)S(1)}, bf16[256,1024]{1,0:T(8,128)(2,1)S(1)}, u32[]{:S(2)}, u32[]{:S(2)}) collective-permute-start(bf16[256,1024]{1,0:T(8,128)(2,1)S(1)} %constant_dynamic-update-slice_fusion.p_ref), channel_id=1, source_target_pairs={{0,1},{1,0},{2,3},{3,2},{4,5},{5,4},{6,7},{7,6},{8,9},{9,8},{10,11... | collective-permute-start | bytes 1572872 | tf_op jit(solution)/shard_map/ppermute | solution.py:21
  43.5 8.1 %all-to-all-done.1 = bf16[4,128,1024]{2,1,0:T(8,128)(2,1)S(1)} async-done(((bf16[4,128,1024]{2,1,0:T(8,128)(2,1)}), bf16[4,128,1024]{2,1,0:T(8,128)(2,1)S(1)}, u32[]{:S(2)}, u32[]{:S(2)}) %all-to-all-start.1) | async-done | bytes 1048608 | tf_op jit(solution)/shard_map/all_to_all | solution.py:29
  51.5 1.7 %shard_map.52 = f32[4,128,512]{2,1,0:T(8,128)} custom-call(s32[1]{0:T(128)} %bitcast.place_ref.x_ref, bf16[512,1024]{1,0:T(8,128)(2,1)S(1)} %bitcast.23, bf16[256,1024]{1,0:T(8,128)(2,1)S(1)} %constant_dynamic-update-slice_fusion.p_ref, bf16[256,1024]{1,0:T(8,128)(2,1)S(1)} %collective-permute-done.3.p_other_ref), custom_call_target="tpu_custom_call" | custom-call | flops 536870912 | bytes 3145728 | tf_op jit(solution)/shard_map/pallas_call | solution.py:43
  53.3 4.5 %all-to-all-start.2 = ((f32[4,128,512]{2,1,0:T(8,128)}), f32[4,128,512]{2,1,0:T(8,128)S(1)}, u32[]{:S(2)}, u32[]{:S(2)}) async-start(f32[4,128,512]{2,1,0:T(8,128)} %shard_map.52), calls=%async_computation.2 | async-start | bytes 2097152 | tf_op jit(solution)/shard_map/all_to_all | solution.py:29
  58.5 10.2 %all-to-all-done.2 = f32[4,128,512]{2,1,0:T(8,128)S(1)} async-done(((f32[4,128,512]{2,1,0:T(8,128)}), f32[4,128,512]{2,1,0:T(8,128)S(1)}, u32[]{:S(2)}, u32[]{:S(2)}) %all-to-all-start.2) | async-done | bytes 1048608 | tf_op jit(solution)/shard_map/all_to_all | solution.py:29
  69.6 12.5 %all-to-all-start.3 = ((f32[16,1,384]{2,1,0:T(1,128)}), f32[16,1,384]{2,1,0:T(1,128)S(1)}, u32[]{:S(2)}, u32[]{:S(2)}) async-start(f32[16,1,384]{2,1,0:T(1,128)} %broadcast_in_dim.14), calls=%async_computation.3 | async-start | bytes 49152 | tf_op jit(solution)/shard_map/all_to_all | solution.py:29
  82.1 1.9 %collective-permute-start.5 = (bf16[512,1024]{1,0:T(8,128)(2,1)S(1)}, bf16[512,1024]{1,0:T(8,128)(2,1)}, u32[]{:S(2)}, u32[]{:S(2)}) collective-permute-start(bf16[512,1024]{1,0:T(8,128)(2,1)S(1)} %bitcast.24), channel_id=1, source_target_pairs={{0,1},{1,0},{2,3},{3,2},{4,5},{5,4},{6,7},{7,6},{8,9},{9,8},{10,11... | collective-permute-start | bytes 3145736 | tf_op jit(solution)/shard_map/ppermute | solution.py:21
  84.0 10.9 %all-to-all-done.3 = f32[16,1,384]{2,1,0:T(1,128)S(1)} async-done(((f32[16,1,384]{2,1,0:T(1,128)}), f32[16,1,384]{2,1,0:T(1,128)S(1)}, u32[]{:S(2)}, u32[]{:S(2)}) %all-to-all-start.3) | async-done | bytes 24608 | tf_op jit(solution)/shard_map/all_to_all | solution.py:29
  95.3 10.5 %all_to_all.39 = bf16[4,128,512]{2,1,0:T(8,128)(2,1)S(1)} all-to-all(bf16[4,128,512]{2,1,0:T(8,128)(2,1)S(1)} %broadcast_in_dim.15), channel_id=1, replica_groups=mesh['y'=4,'zl'=4,'zh'=4,'x'=4,'c'=2] {'y'}, dimensions={0} | all-to-all | bytes 1048576 | tf_op jit(solution)/shard_map/all_to_all | solution.py:29
  105.8 0.7 shard_map.54
  106.5 1.0 copy-done
  107.5 6.3 %all-to-all-start.5 = ((bf16[4,128,1024]{2,1,0:T(8,128)(2,1)}), bf16[4,128,1024]{2,1,0:T(8,128)(2,1)}, u32[]{:S(2)}, u32[]{:S(2)}) async-start(bf16[4,128,1024]{2,1,0:T(8,128)(2,1)} %copy-done), calls=%async_computation.5 | async-start | bytes 2097152 | tf_op jit(solution)/shard_map/all_to_all | solution.py:29
  113.8 1.9 %collective-permute-start.4 = (bf16[4,4,32,256]{3,2,1,0:T(8,128)(2,1)S(1)}, bf16[4,4,32,256]{3,2,1,0:T(8,128)(2,1)S(1)}, u32[]{:S(2)}, u32[]{:S(2)}) collective-permute-start(bf16[4,4,32,256]{3,2,1,0:T(8,128)(2,1)S(1)} %slice.39), channel_id=1, source_target_pairs={{0,1},{1,0},{2,3},{3,2},{4,5},{5,4},{6,7},{7,6},{8,9},{9,8},{10,11... | collective-permute-start | bytes 786440 | tf_op jit(solution)/shard_map/ppermute | solution.py:21
  115.8 1.5 collective-permute-done.4.far_w_ref
  117.2 2.0 %shard_map.56 = (f32[2,256,256]{2,1,0:T(8,128)S(1)}, bf16[2,256,256]{2,1,0:T(8,128)(2,1)S(1)}) custom-call(s32[1]{0:T(128)} %bitcast.7.zl_ref.place_ref, bf16[4,4,32,512]{3,2,1,0:T(8,128)(2,1)S(1)} %bitcast.21, bf16[4,4,32,256]{3,2,1,0:T(8,128)(2,1)S(1)} %collective-permute-done.4.far_w_ref, bf16[512,1024]{1,0:T(8,128)(2,1)S(1)} %bitcast.25, ...), custom_call_target="tpu_custom_call" | custom-call | flops 536870912 | bytes 3670016 | tf_op jit(solution)/shard_map/pallas_call | solution.py:43
  119.2 2.4 %collective-permute-start.6 = (bf16[2,256,256]{2,1,0:T(8,128)(2,1)S(1)}, bf16[2,256,256]{2,1,0:T(8,128)(2,1)S(1)}, u32[]{:S(2)}, u32[]{:S(2)}) collective-permute-start(bf16[2,256,256]{2,1,0:T(8,128)(2,1)S(1)} %get-tuple-element.11), channel_id=1, source_target_pairs={{0,32},{32,0},{64,96},{96,64},{1,33},{33,1},{65,97},{97,65},{2,34}... | collective-permute-start | bytes 786440 | tf_op jit(solution)/shard_map/ppermute | solution.py:25
  121.9 0.8 all-to-all-done.5.moved_ref
  122.7 2.1 %shard_map.55 = bf16[16,32,256]{2,1,0:T(8,128)(2,1)} custom-call(s32[1]{0:T(128)} %bitcast.place_ref.x_ref, f32[128,1024]{1,0:T(8,128)S(1)} %shard_map.53.own_ref, bf16[4,128,1024]{2,1,0:T(8,128)(2,1)} %all-to-all-done.5.moved_ref), custom_call_target="tpu_custom_call" | custom-call | bytes 1835008 | tf_op jit(solution)/shard_map/pallas_call | solution.py:43
  124.9 4.3 %all-to-all-start.6 = ((bf16[16,32,256]{2,1,0:T(8,128)(2,1)}), bf16[16,32,256]{2,1,0:T(8,128)(2,1)S(1)}, u32[]{:S(2)}, u32[]{:S(2)}) async-start(bf16[16,32,256]{2,1,0:T(8,128)(2,1)} %shard_map.55), calls=%async_computation.6 | async-start | bytes 524288 | tf_op jit(solution)/shard_map/all_to_all | solution.py:29
  129.5 4.5 %collective-permute-start.7 = (bf16[256,256]{1,0:T(8,128)(2,1)S(1)}, bf16[256,256]{1,0:T(8,128)(2,1)S(1)}, u32[]{:S(2)}, u32[]{:S(2)}) collective-permute-start(bf16[256,256]{1,0:T(8,128)(2,1)S(1)} %get-tuple-element.13), channel_id=1, source_target_pairs={{0,64},{32,96},{64,0},{96,32},{1,65},{33,97},{65,1},{97,33},{2,66}... | collective-permute-start | bytes 393224 | tf_op jit(solution)/shard_map/ppermute | solution.py:25
  134.0 13.9 %collective-permute-done.7 = bf16[256,256]{1,0:T(8,128)(2,1)S(1)} collective-permute-done((bf16[256,256]{1,0:T(8,128)(2,1)S(1)}, bf16[256,256]{1,0:T(8,128)(2,1)S(1)}, u32[]{:S(2)}, u32[]{:S(2)}) %collective-permute-start.7) | collective-permute-done | bytes 131104 | tf_op jit(solution)/shard_map/ppermute | solution.py:25
  147.9 0.7 add_convert_fusion
  148.6 0.7 bitcast_reduce_fusion
  (37 shorter events, 2.8 us)
Async XLA Ops:
  0.6 0.8 copy-start.1
  2.2 15.3 %copy-start.2 = (bf16[256,256]{1,0:T(8,128)(2,1)S(1)}, bf16[256,256]{1,0:T(8,128)(2,1)}, u32[]{:S(2)}) copy-start(bf16[256,256]{1,0:T(8,128)(2,1)} %param.4) | copy-start | bytes 393220
  2.2 33.4 %all-to-all-start = ((bf16[16,32,256]{2,1,0:T(8,128)(2,1)}), bf16[16,32,256]{2,1,0:T(8,128)(2,1)S(1)}, u32[]{:S(2)}, u32[]{:S(2)}) async-start(bf16[16,32,256]{2,1,0:T(8,128)(2,1)} %shard_map.50), calls=%async_computation | async-start | bytes 524288 | tf_op jit(solution)/shard_map/all_to_all | solution.py:29
  17.6 23.9 %collective-permute-start = (bf16[256,256]{1,0:T(8,128)(2,1)S(1)}, bf16[256,256]{1,0:T(8,128)(2,1)S(1)}, u32[]{:S(2)}, u32[]{:S(2)}) collective-permute-start(bf16[256,256]{1,0:T(8,128)(2,1)S(1)} %copy-done.2), channel_id=1, source_target_pairs={{0,32},{32,64},{64,96},{96,0},{1,33},{33,65},{65,97},{97,1},{2,34}... | collective-permute-start | bytes 393224 | tf_op jit(solution)/shard_map/ppermute | solution.py:21
  21.4 20.1 %collective-permute-start.1 = (bf16[256,256]{1,0:T(8,128)(2,1)S(1)}, bf16[256,256]{1,0:T(8,128)(2,1)S(1)}, u32[]{:S(2)}, u32[]{:S(2)}) collective-permute-start(bf16[256,256]{1,0:T(8,128)(2,1)S(1)} %copy-done.2), channel_id=1, source_target_pairs={{0,64},{32,96},{64,0},{96,32},{1,65},{33,97},{65,1},{97,33},{2,66}... | collective-permute-start | bytes 393224 | tf_op jit(solution)/shard_map/ppermute | solution.py:21
  25.7 15.8 %collective-permute-start.2 = (bf16[256,256]{1,0:T(8,128)(2,1)S(1)}, bf16[256,256]{1,0:T(8,128)(2,1)S(1)}, u32[]{:S(2)}, u32[]{:S(2)}) collective-permute-start(bf16[256,256]{1,0:T(8,128)(2,1)S(1)} %copy-done.2), channel_id=1, source_target_pairs={{0,96},{32,0},{64,32},{96,64},{1,97},{33,1},{65,33},{97,65},{2,98}... | collective-permute-start | bytes 393224 | tf_op jit(solution)/shard_map/ppermute | solution.py:21
  36.7 14.9 %all-to-all-start.1 = ((bf16[4,128,1024]{2,1,0:T(8,128)(2,1)}), bf16[4,128,1024]{2,1,0:T(8,128)(2,1)S(1)}, u32[]{:S(2)}, u32[]{:S(2)}) async-start(bf16[4,128,1024]{2,1,0:T(8,128)(2,1)} %shard_map.51), calls=%async_computation.1 | async-start | bytes 2097152 | tf_op jit(solution)/shard_map/all_to_all | solution.py:29
  41.5 10.0 %collective-permute-start.3 = (bf16[256,1024]{1,0:T(8,128)(2,1)S(1)}, bf16[256,1024]{1,0:T(8,128)(2,1)S(1)}, u32[]{:S(2)}, u32[]{:S(2)}) collective-permute-start(bf16[256,1024]{1,0:T(8,128)(2,1)S(1)} %constant_dynamic-update-slice_fusion.p_ref), channel_id=1, source_target_pairs={{0,1},{1,0},{2,3},{3,2},{4,5},{5,4},{6,7},{7,6},{8,9},{9,8},{10,11... | collective-permute-start | bytes 1572872 | tf_op jit(solution)/shard_map/ppermute | solution.py:21
  53.3 15.4 %all-to-all-start.2 = ((f32[4,128,512]{2,1,0:T(8,128)}), f32[4,128,512]{2,1,0:T(8,128)S(1)}, u32[]{:S(2)}, u32[]{:S(2)}) async-start(f32[4,128,512]{2,1,0:T(8,128)} %shard_map.52), calls=%async_computation.2 | async-start | bytes 2097152 | tf_op jit(solution)/shard_map/all_to_all | solution.py:29
  57.7 0.7 copy-start.3
  69.6 25.3 %all-to-all-start.3 = ((f32[16,1,384]{2,1,0:T(1,128)}), f32[16,1,384]{2,1,0:T(1,128)S(1)}, u32[]{:S(2)}, u32[]{:S(2)}) async-start(f32[16,1,384]{2,1,0:T(1,128)} %broadcast_in_dim.14), calls=%async_computation.3 | async-start | bytes 49152 | tf_op jit(solution)/shard_map/all_to_all | solution.py:29
  82.1 33.7 %collective-permute-start.5 = (bf16[512,1024]{1,0:T(8,128)(2,1)S(1)}, bf16[512,1024]{1,0:T(8,128)(2,1)}, u32[]{:S(2)}, u32[]{:S(2)}) collective-permute-start(bf16[512,1024]{1,0:T(8,128)(2,1)S(1)} %bitcast.24), channel_id=1, source_target_pairs={{0,1},{1,0},{2,3},{3,2},{4,5},{5,4},{6,7},{7,6},{8,9},{9,8},{10,11... | collective-permute-start | bytes 3145736 | tf_op jit(solution)/shard_map/ppermute | solution.py:21
  106.5 1.0 copy-start
  107.5 15.2 %all-to-all-start.5 = ((bf16[4,128,1024]{2,1,0:T(8,128)(2,1)}), bf16[4,128,1024]{2,1,0:T(8,128)(2,1)}, u32[]{:S(2)}, u32[]{:S(2)}) async-start(bf16[4,128,1024]{2,1,0:T(8,128)(2,1)} %copy-done), calls=%async_computation.5 | async-start | bytes 2097152 | tf_op jit(solution)/shard_map/all_to_all | solution.py:29
  113.8 3.4 %collective-permute-start.4 = (bf16[4,4,32,256]{3,2,1,0:T(8,128)(2,1)S(1)}, bf16[4,4,32,256]{3,2,1,0:T(8,128)(2,1)S(1)}, u32[]{:S(2)}, u32[]{:S(2)}) collective-permute-start(bf16[4,4,32,256]{3,2,1,0:T(8,128)(2,1)S(1)} %slice.39), channel_id=1, source_target_pairs={{0,1},{1,0},{2,3},{3,2},{4,5},{5,4},{6,7},{7,6},{8,9},{9,8},{10,11... | collective-permute-start | bytes 786440 | tf_op jit(solution)/shard_map/ppermute | solution.py:21
  119.2 10.2 %collective-permute-start.6 = (bf16[2,256,256]{2,1,0:T(8,128)(2,1)S(1)}, bf16[2,256,256]{2,1,0:T(8,128)(2,1)S(1)}, u32[]{:S(2)}, u32[]{:S(2)}) collective-permute-start(bf16[2,256,256]{2,1,0:T(8,128)(2,1)S(1)} %get-tuple-element.11), channel_id=1, source_target_pairs={{0,32},{32,0},{64,96},{96,64},{1,33},{33,1},{65,97},{97,65},{2,34}... | collective-permute-start | bytes 786440 | tf_op jit(solution)/shard_map/ppermute | solution.py:25
  124.9 23.7 %all-to-all-start.6 = ((bf16[16,32,256]{2,1,0:T(8,128)(2,1)}), bf16[16,32,256]{2,1,0:T(8,128)(2,1)S(1)}, u32[]{:S(2)}, u32[]{:S(2)}) async-start(bf16[16,32,256]{2,1,0:T(8,128)(2,1)} %shard_map.55), calls=%async_computation.6 | async-start | bytes 524288 | tf_op jit(solution)/shard_map/all_to_all | solution.py:29
  129.5 18.4 %collective-permute-start.7 = (bf16[256,256]{1,0:T(8,128)(2,1)S(1)}, bf16[256,256]{1,0:T(8,128)(2,1)S(1)}, u32[]{:S(2)}, u32[]{:S(2)}) collective-permute-start(bf16[256,256]{1,0:T(8,128)(2,1)S(1)} %get-tuple-element.13), channel_id=1, source_target_pairs={{0,64},{32,96},{64,0},{96,32},{1,65},{33,97},{65,1},{97,33},{2,66}... | collective-permute-start | bytes 393224 | tf_op jit(solution)/shard_map/ppermute | solution.py:25

commit v7 on v6

--- a/solution.py
+++ b/solution.py
@@ -69,7 +69,7 @@
     order = [(z, x) for x in range(n_x) for z in range(n_zh)]
     w_near = jnp.concatenate([w_ref[z, x, :, :count] for z, x in order], axis=0)
     w_far = jnp.concatenate([far_w_ref[z, x] for z, x in order], axis=0)
-    for i, flip in enumerate((0, 2, 1, 3)):
+    for i, flip in enumerate((0, 1, 2, 3)):
         at = pl.ds(pl.multiple_of((zl_ref[0] ^ flip) * width, width), width)
         block = dot(w_near, near_ref[:, at], 0, 0) + dot(w_far, far_ref[:, at], 0, 0)
         if i < 2:
@@ -198,13 +198,13 @@
         [jax.ShapeDtypeStruct(pair, F32), jax.ShapeDtypeStruct(pair, BF)],
         flops, zl, weights, far_weights, near, far,
     )
-    arrived = flip(send, "zl", 1)
+    arrived = flip(send, "zl", 2)
     passage_grad, send = call(
         pair_kernel,
         [jax.ShapeDtypeStruct((count, width), F32), jax.ShapeDtypeStruct((count, width), BF)],
         LONG, zl, keep, arrived,
     )
-    passage_grad += flip(send, "zl", 2).astype(F32)
+    passage_grad += flip(send, "zl", 1).astype(F32)
 
     back = exchange(back, COLUMN).reshape(n_zl, n_zh, band, width)
     query_grad = jnp.sum(back.astype(F32), axis=1).reshape(rows, width)

time: 152 us -> 153 us (level); the launches traced: 149 us -> 152 us
  waiting for transfers between devices: 51.9 us -> 56.5 us
  starting transfers between devices: 71.8 us -> 70.1 us
    ppermute x2, waiting for transfers between devices: 14.1 us -> 19.5 us  [flip(): lax.ppermute(value, axis, [(i, i ^ bit) for i in range(lax.axis_size(axis...]
  transfers between devices with their start and end apart: 14 -> 14, of which waited for: 8 -> 7; matrix products, arithmetic and copies ran while one was open for 1% -> 1% of each run, Pallas kernels for 4% -> 4%
where the time goes in v7:
time: 153 us; the launch traced here: 152 us
  starting transfers between devices  70.1 us (46%)
  waiting for transfers between devices  56.5 us (37%)
  blocking collectives  10.5 us (7%)
  Pallas kernels  8.75 us (6%)
  local copies, waits for them, and re-layouts  3.39 us (2%)
  other arithmetic  1.98 us (1%)
    all_to_all x6, starting transfers between devices, exchange(): return lax.all_to_all(blocks, axis, 0, 0, tiled=True)  47.2 us
    all_to_all x6, waiting for transfers between devices, exchange(): return lax.all_to_all(blocks, axis, 0, 0, tiled=True)  35.5 us
    ppermute x2, waiting for transfers between devices, flip(): lax.ppermute(value, axis, [(i, i ^ bit) for i in range(lax.axis_size(axis...  19.5 us
    ppermute x6, starting transfers between devices, shift(): return lax.ppermute(value, axis, [(i, (i + step) % n) for i in range(n)])  17.2 us
    all_to_all x1, blocking collectives, exchange(): return lax.all_to_all(blocks, axis, 0, 0, tiled=True)  10.5 us
    pallas_call x8, Pallas kernels, call(): pl.pallas_call(kernel, out_shape=outs, in_specs=[pl.BlockSpec(memory_spac...  8.75 us
    ppermute x2, starting transfers between devices, flip(): lax.ppermute(value, axis, [(i, i ^ bit) for i in range(lax.axis_size(axis...  5.63 us
  transfers between devices with their start and end apart: 14, of which 7 were waited for; matrix products, arithmetic and copies ran while one was open for 1% of the time, Pallas kernels for 4%

profile of v7, /device:TPU:6, one launch (start us, length us, event | category | flops | bytes accessed | tf_op | source)
XLA Modules:
  0.0 152.2 jit_solution(2503866273462880244)
XLA Ops:
  0.6 0.8 copy-done.1
  1.5 0.7 shard_map.50
  2.2 15.3 %all-to-all-start = ((bf16[16,32,256]{2,1,0:T(8,128)(2,1)}), bf16[16,32,256]{2,1,0:T(8,128)(2,1)S(1)}, u32[]{:S(2)}, u32[]{:S(2)}) async-start(bf16[16,32,256]{2,1,0:T(8,128)(2,1)} %shard_map.50), calls=%async_computation | async-start | bytes 524288 | tf_op jit(solution)/shard_map/all_to_all | solution.py:29
  17.6 3.8 %collective-permute-start = (bf16[256,256]{1,0:T(8,128)(2,1)S(1)}, bf16[256,256]{1,0:T(8,128)(2,1)S(1)}, u32[]{:S(2)}, u32[]{:S(2)}) collective-permute-start(bf16[256,256]{1,0:T(8,128)(2,1)S(1)} %copy-done.2), channel_id=1, source_target_pairs={{0,32},{32,64},{64,96},{96,0},{1,33},{33,65},{65,97},{97,1},{2,34}... | collective-permute-start | bytes 393224 | tf_op jit(solution)/shard_map/ppermute | solution.py:21
  21.4 4.3 %collective-permute-start.1 = (bf16[256,256]{1,0:T(8,128)(2,1)S(1)}, bf16[256,256]{1,0:T(8,128)(2,1)S(1)}, u32[]{:S(2)}, u32[]{:S(2)}) collective-permute-start(bf16[256,256]{1,0:T(8,128)(2,1)S(1)} %copy-done.2), channel_id=1, source_target_pairs={{0,64},{32,96},{64,0},{96,32},{1,65},{33,97},{65,1},{97,33},{2,66}... | collective-permute-start | bytes 393224 | tf_op jit(solution)/shard_map/ppermute | solution.py:21
  25.7 3.4 %collective-permute-start.2 = (bf16[256,256]{1,0:T(8,128)(2,1)S(1)}, bf16[256,256]{1,0:T(8,128)(2,1)S(1)}, u32[]{:S(2)}, u32[]{:S(2)}) collective-permute-start(bf16[256,256]{1,0:T(8,128)(2,1)S(1)} %copy-done.2), channel_id=1, source_target_pairs={{0,96},{32,0},{64,32},{96,64},{1,97},{33,1},{65,33},{97,65},{2,98}... | collective-permute-start | bytes 393224 | tf_op jit(solution)/shard_map/ppermute | solution.py:21
  29.2 6.4 %all-to-all-done.in_ref = bf16[16,32,256]{2,1,0:T(8,128)(2,1)S(1)} async-done(((bf16[16,32,256]{2,1,0:T(8,128)(2,1)}), bf16[16,32,256]{2,1,0:T(8,128)(2,1)S(1)}, u32[]{:S(2)}, u32[]{:S(2)}) %all-to-all-start) | async-done | bytes 262176 | tf_op jit(solution)/shard_map/all_to_all | solution.py:29
  35.6 1.1 shard_map.51
  36.7 4.8 %all-to-all-start.1 = ((bf16[4,128,1024]{2,1,0:T(8,128)(2,1)}), bf16[4,128,1024]{2,1,0:T(8,128)(2,1)S(1)}, u32[]{:S(2)}, u32[]{:S(2)}) async-start(bf16[4,128,1024]{2,1,0:T(8,128)(2,1)} %shard_map.51), calls=%async_computation.1 | async-start | bytes 2097152 | tf_op jit(solution)/shard_map/all_to_all | solution.py:29
  41.5 1.9 %collective-permute-start.3 = (bf16[256,1024]{1,0:T(8,128)(2,1)S(1)}, bf16[256,1024]{1,0:T(8,128)(2,1)S(1)}, u32[]{:S(2)}, u32[]{:S(2)}) collective-permute-start(bf16[256,1024]{1,0:T(8,128)(2,1)S(1)} %constant_dynamic-update-slice_fusion.p_ref), channel_id=1, source_target_pairs={{0,1},{1,0},{2,3},{3,2},{4,5},{5,4},{6,7},{7,6},{8,9},{9,8},{10,11... | collective-permute-start | bytes 1572872 | tf_op jit(solution)/shard_map/ppermute | solution.py:21
  43.5 8.1 %all-to-all-done.1 = bf16[4,128,1024]{2,1,0:T(8,128)(2,1)S(1)} async-done(((bf16[4,128,1024]{2,1,0:T(8,128)(2,1)}), bf16[4,128,1024]{2,1,0:T(8,128)(2,1)S(1)}, u32[]{:S(2)}, u32[]{:S(2)}) %all-to-all-start.1) | async-done | bytes 1048608 | tf_op jit(solution)/shard_map/all_to_all | solution.py:29
  51.5 1.7 %shard_map.52 = f32[4,128,512]{2,1,0:T(8,128)} custom-call(s32[1]{0:T(128)} %bitcast.place_ref.x_ref, bf16[512,1024]{1,0:T(8,128)(2,1)S(1)} %bitcast.23, bf16[256,1024]{1,0:T(8,128)(2,1)S(1)} %constant_dynamic-update-slice_fusion.p_ref, bf16[256,1024]{1,0:T(8,128)(2,1)S(1)} %collective-permute-done.3.p_other_ref), custom_call_target="tpu_custom_call" | custom-call | flops 536870912 | bytes 3145728 | tf_op jit(solution)/shard_map/pallas_call | solution.py:43
  53.3 4.5 %all-to-all-start.2 = ((f32[4,128,512]{2,1,0:T(8,128)}), f32[4,128,512]{2,1,0:T(8,128)S(1)}, u32[]{:S(2)}, u32[]{:S(2)}) async-start(f32[4,128,512]{2,1,0:T(8,128)} %shard_map.52), calls=%async_computation.2 | async-start | bytes 2097152 | tf_op jit(solution)/shard_map/all_to_all | solution.py:29
  58.5 10.2 %all-to-all-done.2 = f32[4,128,512]{2,1,0:T(8,128)S(1)} async-done(((f32[4,128,512]{2,1,0:T(8,128)}), f32[4,128,512]{2,1,0:T(8,128)S(1)}, u32[]{:S(2)}, u32[]{:S(2)}) %all-to-all-start.2) | async-done | bytes 1048608 | tf_op jit(solution)/shard_map/all_to_all | solution.py:29
  69.6 12.5 %all-to-all-start.3 = ((f32[16,1,384]{2,1,0:T(1,128)}), f32[16,1,384]{2,1,0:T(1,128)S(1)}, u32[]{:S(2)}, u32[]{:S(2)}) async-start(f32[16,1,384]{2,1,0:T(1,128)} %broadcast_in_dim.14), calls=%async_computation.3 | async-start | bytes 49152 | tf_op jit(solution)/shard_map/all_to_all | solution.py:29
  82.1 1.9 %collective-permute-start.5 = (bf16[512,1024]{1,0:T(8,128)(2,1)S(1)}, bf16[512,1024]{1,0:T(8,128)(2,1)}, u32[]{:S(2)}, u32[]{:S(2)}) collective-permute-start(bf16[512,1024]{1,0:T(8,128)(2,1)S(1)} %bitcast.24), channel_id=1, source_target_pairs={{0,1},{1,0},{2,3},{3,2},{4,5},{5,4},{6,7},{7,6},{8,9},{9,8},{10,11... | collective-permute-start | bytes 3145736 | tf_op jit(solution)/shard_map/ppermute | solution.py:21
  84.0 10.9 %all-to-all-done.3 = f32[16,1,384]{2,1,0:T(1,128)S(1)} async-done(((f32[16,1,384]{2,1,0:T(1,128)}), f32[16,1,384]{2,1,0:T(1,128)S(1)}, u32[]{:S(2)}, u32[]{:S(2)}) %all-to-all-start.3) | async-done | bytes 24608 | tf_op jit(solution)/shard_map/all_to_all | solution.py:29
  95.3 10.5 %all_to_all.39 = bf16[4,128,512]{2,1,0:T(8,128)(2,1)S(1)} all-to-all(bf16[4,128,512]{2,1,0:T(8,128)(2,1)S(1)} %broadcast_in_dim.15), channel_id=1, replica_groups=mesh['y'=4,'zl'=4,'zh'=4,'x'=4,'c'=2] {'y'}, dimensions={0} | all-to-all | bytes 1048576 | tf_op jit(solution)/shard_map/all_to_all | solution.py:29
  105.8 0.7 shard_map.54
  106.5 1.0 copy-done
  107.5 6.3 %all-to-all-start.5 = ((bf16[4,128,1024]{2,1,0:T(8,128)(2,1)}), bf16[4,128,1024]{2,1,0:T(8,128)(2,1)}, u32[]{:S(2)}, u32[]{:S(2)}) async-start(bf16[4,128,1024]{2,1,0:T(8,128)(2,1)} %copy-done), calls=%async_computation.5 | async-start | bytes 2097152 | tf_op jit(solution)/shard_map/all_to_all | solution.py:29
  113.8 1.9 %collective-permute-start.4 = (bf16[4,4,32,256]{3,2,1,0:T(8,128)(2,1)S(1)}, bf16[4,4,32,256]{3,2,1,0:T(8,128)(2,1)S(1)}, u32[]{:S(2)}, u32[]{:S(2)}) collective-permute-start(bf16[4,4,32,256]{3,2,1,0:T(8,128)(2,1)S(1)} %slice.39), channel_id=1, source_target_pairs={{0,1},{1,0},{2,3},{3,2},{4,5},{5,4},{6,7},{7,6},{8,9},{9,8},{10,11... | collective-permute-start | bytes 786440 | tf_op jit(solution)/shard_map/ppermute | solution.py:21
  115.8 1.5 collective-permute-done.4.far_w_ref
  117.2 2.0 %shard_map.56 = (f32[2,256,256]{2,1,0:T(8,128)S(1)}, bf16[2,256,256]{2,1,0:T(8,128)(2,1)S(1)}) custom-call(s32[1]{0:T(128)} %bitcast.7.zl_ref.place_ref, bf16[4,4,32,512]{3,2,1,0:T(8,128)(2,1)S(1)} %bitcast.21, bf16[4,4,32,256]{3,2,1,0:T(8,128)(2,1)S(1)} %collective-permute-done.4.far_w_ref, bf16[512,1024]{1,0:T(8,128)(2,1)S(1)} %bitcast.25, ...), custom_call_target="tpu_custom_call" | custom-call | flops 536870912 | bytes 3670016 | tf_op jit(solution)/shard_map/pallas_call | solution.py:43
  119.2 3.6 %collective-permute-start.6 = (bf16[2,256,256]{2,1,0:T(8,128)(2,1)S(1)}, bf16[2,256,256]{2,1,0:T(8,128)(2,1)S(1)}, u32[]{:S(2)}, u32[]{:S(2)}) collective-permute-start(bf16[2,256,256]{2,1,0:T(8,128)(2,1)S(1)} %get-tuple-element.11), channel_id=1, source_target_pairs={{0,64},{32,96},{64,0},{96,32},{1,65},{33,97},{65,1},{97,33},{2,66}... | collective-permute-start | bytes 786440 | tf_op jit(solution)/shard_map/ppermute | solution.py:25
  123.2 2.1 %shard_map.55 = bf16[16,32,256]{2,1,0:T(8,128)(2,1)} custom-call(s32[1]{0:T(128)} %bitcast.place_ref.x_ref, f32[128,1024]{1,0:T(8,128)S(1)} %shard_map.53.own_ref, bf16[4,128,1024]{2,1,0:T(8,128)(2,1)} %all-to-all-done.5.moved_ref), custom_call_target="tpu_custom_call" | custom-call | bytes 1835008 | tf_op jit(solution)/shard_map/pallas_call | solution.py:43
  125.3 3.9 %all-to-all-start.6 = ((bf16[16,32,256]{2,1,0:T(8,128)(2,1)}), bf16[16,32,256]{2,1,0:T(8,128)(2,1)S(1)}, u32[]{:S(2)}, u32[]{:S(2)}) async-start(bf16[16,32,256]{2,1,0:T(8,128)(2,1)} %shard_map.55), calls=%async_computation.6 | async-start | bytes 524288 | tf_op jit(solution)/shard_map/all_to_all | solution.py:29
  129.2 14.4 %collective-permute-done.6.arrived_ref = bf16[2,256,256]{2,1,0:T(8,128)(2,1)S(1)} collective-permute-done((bf16[2,256,256]{2,1,0:T(8,128)(2,1)S(1)}, bf16[2,256,256]{2,1,0:T(8,128)(2,1)S(1)}, u32[]{:S(2)}, u32[]{:S(2)}) %collective-permute-start.6) | collective-permute-done | bytes 262176 | tf_op jit(solution)/shard_map/ppermute | solution.py:25
  143.6 2.0 %collective-permute-start.7 = (bf16[256,256]{1,0:T(8,128)(2,1)S(1)}, bf16[256,256]{1,0:T(8,128)(2,1)S(1)}, u32[]{:S(2)}, u32[]{:S(2)}) collective-permute-start(bf16[256,256]{1,0:T(8,128)(2,1)S(1)} %get-tuple-element.13), channel_id=1, source_target_pairs={{0,32},{32,0},{64,96},{96,64},{1,33},{33,1},{65,97},{97,65},{2,34}... | collective-permute-start | bytes 393224 | tf_op jit(solution)/shard_map/ppermute | solution.py:25
  145.6 5.2 %collective-permute-done.7 = bf16[256,256]{1,0:T(8,128)(2,1)S(1)} collective-permute-done((bf16[256,256]{1,0:T(8,128)(2,1)S(1)}, bf16[256,256]{1,0:T(8,128)(2,1)S(1)}, u32[]{:S(2)}, u32[]{:S(2)}) %collective-permute-start.7) | collective-permute-done | bytes 131104 | tf_op jit(solution)/shard_map/ppermute | solution.py:25
  150.8 0.7 add_convert_fusion
  151.5 0.7 bitcast_reduce_fusion
  (37 shorter events, 2.6 us)
Async XLA Ops:
  0.6 0.8 copy-start.1
  2.2 15.3 %copy-start.2 = (bf16[256,256]{1,0:T(8,128)(2,1)S(1)}, bf16[256,256]{1,0:T(8,128)(2,1)}, u32[]{:S(2)}) copy-start(bf16[256,256]{1,0:T(8,128)(2,1)} %param.4) | copy-start | bytes 393220
  2.2 33.4 %all-to-all-start = ((bf16[16,32,256]{2,1,0:T(8,128)(2,1)}), bf16[16,32,256]{2,1,0:T(8,128)(2,1)S(1)}, u32[]{:S(2)}, u32[]{:S(2)}) async-start(bf16[16,32,256]{2,1,0:T(8,128)(2,1)} %shard_map.50), calls=%async_computation | async-start | bytes 524288 | tf_op jit(solution)/shard_map/all_to_all | solution.py:29
  17.6 23.9 %collective-permute-start = (bf16[256,256]{1,0:T(8,128)(2,1)S(1)}, bf16[256,256]{1,0:T(8,128)(2,1)S(1)}, u32[]{:S(2)}, u32[]{:S(2)}) collective-permute-start(bf16[256,256]{1,0:T(8,128)(2,1)S(1)} %copy-done.2), channel_id=1, source_target_pairs={{0,32},{32,64},{64,96},{96,0},{1,33},{33,65},{65,97},{97,1},{2,34}... | collective-permute-start | bytes 393224 | tf_op jit(solution)/shard_map/ppermute | solution.py:21
  21.4 20.1 %collective-permute-start.1 = (bf16[256,256]{1,0:T(8,128)(2,1)S(1)}, bf16[256,256]{1,0:T(8,128)(2,1)S(1)}, u32[]{:S(2)}, u32[]{:S(2)}) collective-permute-start(bf16[256,256]{1,0:T(8,128)(2,1)S(1)} %copy-done.2), channel_id=1, source_target_pairs={{0,64},{32,96},{64,0},{96,32},{1,65},{33,97},{65,1},{97,33},{2,66}... | collective-permute-start | bytes 393224 | tf_op jit(solution)/shard_map/ppermute | solution.py:21
  25.7 15.8 %collective-permute-start.2 = (bf16[256,256]{1,0:T(8,128)(2,1)S(1)}, bf16[256,256]{1,0:T(8,128)(2,1)S(1)}, u32[]{:S(2)}, u32[]{:S(2)}) collective-permute-start(bf16[256,256]{1,0:T(8,128)(2,1)S(1)} %copy-done.2), channel_id=1, source_target_pairs={{0,96},{32,0},{64,32},{96,64},{1,97},{33,1},{65,33},{97,65},{2,98}... | collective-permute-start | bytes 393224 | tf_op jit(solution)/shard_map/ppermute | solution.py:21
  36.7 14.9 %all-to-all-start.1 = ((bf16[4,128,1024]{2,1,0:T(8,128)(2,1)}), bf16[4,128,1024]{2,1,0:T(8,128)(2,1)S(1)}, u32[]{:S(2)}, u32[]{:S(2)}) async-start(bf16[4,128,1024]{2,1,0:T(8,128)(2,1)} %shard_map.51), calls=%async_computation.1 | async-start | bytes 2097152 | tf_op jit(solution)/shard_map/all_to_all | solution.py:29
  41.5 10.0 %collective-permute-start.3 = (bf16[256,1024]{1,0:T(8,128)(2,1)S(1)}, bf16[256,1024]{1,0:T(8,128)(2,1)S(1)}, u32[]{:S(2)}, u32[]{:S(2)}) collective-permute-start(bf16[256,1024]{1,0:T(8,128)(2,1)S(1)} %constant_dynamic-update-slice_fusion.p_ref), channel_id=1, source_target_pairs={{0,1},{1,0},{2,3},{3,2},{4,5},{5,4},{6,7},{7,6},{8,9},{9,8},{10,11... | collective-permute-start | bytes 1572872 | tf_op jit(solution)/shard_map/ppermute | solution.py:21
  53.3 15.4 %all-to-all-start.2 = ((f32[4,128,512]{2,1,0:T(8,128)}), f32[4,128,512]{2,1,0:T(8,128)S(1)}, u32[]{:S(2)}, u32[]{:S(2)}) async-start(f32[4,128,512]{2,1,0:T(8,128)} %shard_map.52), calls=%async_computation.2 | async-start | bytes 2097152 | tf_op jit(solution)/shard_map/all_to_all | solution.py:29
  57.7 0.7 copy-start.3
  69.6 25.3 %all-to-all-start.3 = ((f32[16,1,384]{2,1,0:T(1,128)}), f32[16,1,384]{2,1,0:T(1,128)S(1)}, u32[]{:S(2)}, u32[]{:S(2)}) async-start(f32[16,1,384]{2,1,0:T(1,128)} %broadcast_in_dim.14), calls=%async_computation.3 | async-start | bytes 49152 | tf_op jit(solution)/shard_map/all_to_all | solution.py:29
  82.1 33.7 %collective-permute-start.5 = (bf16[512,1024]{1,0:T(8,128)(2,1)S(1)}, bf16[512,1024]{1,0:T(8,128)(2,1)}, u32[]{:S(2)}, u32[]{:S(2)}) collective-permute-start(bf16[512,1024]{1,0:T(8,128)(2,1)S(1)} %bitcast.24), channel_id=1, source_target_pairs={{0,1},{1,0},{2,3},{3,2},{4,5},{5,4},{6,7},{7,6},{8,9},{9,8},{10,11... | collective-permute-start | bytes 3145736 | tf_op jit(solution)/shard_map/ppermute | solution.py:21
  106.5 1.0 copy-start
  107.5 15.7 %all-to-all-start.5 = ((bf16[4,128,1024]{2,1,0:T(8,128)(2,1)}), bf16[4,128,1024]{2,1,0:T(8,128)(2,1)}, u32[]{:S(2)}, u32[]{:S(2)}) async-start(bf16[4,128,1024]{2,1,0:T(8,128)(2,1)} %copy-done), calls=%async_computation.5 | async-start | bytes 2097152 | tf_op jit(solution)/shard_map/all_to_all | solution.py:29
  113.8 3.4 %collective-permute-start.4 = (bf16[4,4,32,256]{3,2,1,0:T(8,128)(2,1)S(1)}, bf16[4,4,32,256]{3,2,1,0:T(8,128)(2,1)S(1)}, u32[]{:S(2)}, u32[]{:S(2)}) collective-permute-start(bf16[4,4,32,256]{3,2,1,0:T(8,128)(2,1)S(1)} %slice.39), channel_id=1, source_target_pairs={{0,1},{1,0},{2,3},{3,2},{4,5},{5,4},{6,7},{7,6},{8,9},{9,8},{10,11... | collective-permute-start | bytes 786440 | tf_op jit(solution)/shard_map/ppermute | solution.py:21
  119.2 24.3 %collective-permute-start.6 = (bf16[2,256,256]{2,1,0:T(8,128)(2,1)S(1)}, bf16[2,256,256]{2,1,0:T(8,128)(2,1)S(1)}, u32[]{:S(2)}, u32[]{:S(2)}) collective-permute-start(bf16[2,256,256]{2,1,0:T(8,128)(2,1)S(1)} %get-tuple-element.11), channel_id=1, source_target_pairs={{0,64},{32,96},{64,0},{96,32},{1,65},{33,97},{65,1},{97,33},{2,66}... | collective-permute-start | bytes 786440 | tf_op jit(solution)/shard_map/ppermute | solution.py:25
  125.3 26.2 %all-to-all-start.6 = ((bf16[16,32,256]{2,1,0:T(8,128)(2,1)}), bf16[16,32,256]{2,1,0:T(8,128)(2,1)S(1)}, u32[]{:S(2)}, u32[]{:S(2)}) async-start(bf16[16,32,256]{2,1,0:T(8,128)(2,1)} %shard_map.55), calls=%async_computation.6 | async-start | bytes 524288 | tf_op jit(solution)/shard_map/all_to_all | solution.py:29
  143.6 7.2 %collective-permute-start.7 = (bf16[256,256]{1,0:T(8,128)(2,1)S(1)}, bf16[256,256]{1,0:T(8,128)(2,1)S(1)}, u32[]{:S(2)}, u32[]{:S(2)}) collective-permute-start(bf16[256,256]{1,0:T(8,128)(2,1)S(1)} %get-tuple-element.13), channel_id=1, source_target_pairs={{0,32},{32,0},{64,96},{96,64},{1,33},{33,1},{65,97},{97,65},{2,34}... | collective-permute-start | bytes 393224 | tf_op jit(solution)/shard_map/ppermute | solution.py:25

commit v8 on v6

--- a/solution.py
+++ b/solution.py
@@ -84,14 +84,6 @@
     send_ref[...] = (keep_ref[1] + arrived_ref[1].astype(F32)).astype(BF)
 
 
-def spread_kernel(place_ref, in_ref, out_ref):
-    del place_ref
-    n, band, _ = out_ref.shape
-    n_bands = in_ref.shape[0] // band
-    for i in range(n):
-        out_ref[i] = in_ref[pl.ds(i // (n // n_bands) * band, band), :]
-
-
 def collect_kernel(place_ref, in_ref, out_ref):
     del place_ref
     n, band, width = in_ref.shape
@@ -145,7 +137,7 @@
 
     bands = jax.ShapeDtypeStruct((n_zh * n_zl, band, width), BF)
     spread = jax.ShapeDtypeStruct((n_x, n_zh * band, strip), BF)
-    (mine,) = call(spread_kernel, [bands], 0, x, queries)
+    mine = jnp.broadcast_to(queries.reshape(n_zl, 1, band, width), (n_zl, n_zh, band, width)).reshape(bands.shape)
     (mine,) = call(collect_kernel, [spread], 0, x, exchange(mine, COLUMN))
     near = exchange(mine, "x").reshape(n_half, strip)
 

time: 152 us -> 152 us (level)
    broadcast_in_dim x0 -> x1, local copies, waits for them, and re-layouts: none -> 1.56 us  [per_device(): jnp.broadcast_to(queries.reshape(n_zl, 1, band, width), (n_zl, n_zh, band...]
    pallas_call x8 -> x7, Pallas kernels: 8.75 us -> 8 us  [call(): pl.pallas_call(kernel, out_shape=outs, in_specs=[pl.BlockSpec(memory_spac...]
where the time goes in v8:
time: 152 us; the launch traced here: 149 us
  starting transfers between devices  71.8 us (47%)
  waiting for transfers between devices  51.9 us (34%)
  blocking collectives  10.5 us (7%)
  Pallas kernels  8 us (5%)
  local copies, waits for them, and re-layouts  4.13 us (3%)
  other arithmetic  1.98 us (1%)
    all_to_all x6, starting transfers between devices, exchange(): return lax.all_to_all(blocks, axis, 0, 0, tiled=True)  47.7 us
    all_to_all x6, waiting for transfers between devices, exchange(): return lax.all_to_all(blocks, axis, 0, 0, tiled=True)  36.3 us
    ppermute x6, starting transfers between devices, shift(): return lax.ppermute(value, axis, [(i, (i + step) % n) for i in range(n)])  17.2 us
    ppermute x2, waiting for transfers between devices, flip(): lax.ppermute(value, axis, [(i, i ^ bit) for i in range(lax.axis_size(axis...  14.1 us
    all_to_all x1, blocking collectives, exchange(): return lax.all_to_all(blocks, axis, 0, 0, tiled=True)  10.5 us
    pallas_call x7, Pallas kernels, call(): pl.pallas_call(kernel, out_shape=outs, in_specs=[pl.BlockSpec(memory_spac...  8 us
    ppermute x2, starting transfers between devices, flip(): lax.ppermute(value, axis, [(i, i ^ bit) for i in range(lax.axis_size(axis...  6.89 us
  transfers between devices with their start and end apart: 14, of which 8 were waited for; matrix products, arithmetic and copies ran while one was open for 1% of the time, Pallas kernels for 4%

profile of v8, /device:TPU:6, one launch (start us, length us, event | category | flops | bytes accessed | tf_op | source)
XLA Modules:
  0.0 149.2 jit_solution(12748079901228888760)
XLA Ops:
  0.6 1.6 %broadcast_in_dim.21 = bf16[4,4,32,256]{3,2,1,0:T(8,128)(2,1)} broadcast(bf16[4,32,256]{2,1,0:T(8,128)(2,1)} %bitcast.31), dimensions={0,2,3} | broadcast | bytes 327680 | tf_op jit(solution)/shard_map/broadcast_in_dim | solution.py:140
  2.2 15.3 %all-to-all-start = ((bf16[16,32,256]{2,1,0:T(8,128)(2,1)}), bf16[16,32,256]{2,1,0:T(8,128)(2,1)S(1)}, u32[]{:S(2)}, u32[]{:S(2)}) async-start(bf16[16,32,256]{2,1,0:T(8,128)(2,1)} %bitcast.2), calls=%async_computation | async-start | bytes 524288 | tf_op jit(solution)/shard_map/all_to_all | solution.py:29
  17.5 3.8 %collective-permute-start = (bf16[256,256]{1,0:T(8,128)(2,1)S(1)}, bf16[256,256]{1,0:T(8,128)(2,1)S(1)}, u32[]{:S(2)}, u32[]{:S(2)}) collective-permute-start(bf16[256,256]{1,0:T(8,128)(2,1)S(1)} %copy-done.1), channel_id=1, source_target_pairs={{0,32},{32,64},{64,96},{96,0},{1,33},{33,65},{65,97},{97,1},{2,34}... | collective-permute-start | bytes 393224 | tf_op jit(solution)/shard_map/ppermute | solution.py:21
  21.4 4.3 %collective-permute-start.1 = (bf16[256,256]{1,0:T(8,128)(2,1)S(1)}, bf16[256,256]{1,0:T(8,128)(2,1)S(1)}, u32[]{:S(2)}, u32[]{:S(2)}) collective-permute-start(bf16[256,256]{1,0:T(8,128)(2,1)S(1)} %copy-done.1), channel_id=1, source_target_pairs={{0,64},{32,96},{64,0},{96,32},{1,65},{33,97},{65,1},{97,33},{2,66}... | collective-permute-start | bytes 393224 | tf_op jit(solution)/shard_map/ppermute | solution.py:21
  25.7 3.4 %collective-permute-start.2 = (bf16[256,256]{1,0:T(8,128)(2,1)S(1)}, bf16[256,256]{1,0:T(8,128)(2,1)S(1)}, u32[]{:S(2)}, u32[]{:S(2)}) collective-permute-start(bf16[256,256]{1,0:T(8,128)(2,1)S(1)} %copy-done.1), channel_id=1, source_target_pairs={{0,96},{32,0},{64,32},{96,64},{1,97},{33,1},{65,33},{97,65},{2,98}... | collective-permute-start | bytes 393224 | tf_op jit(solution)/shard_map/ppermute | solution.py:21
  29.2 6.4 %all-to-all-done.in_ref = bf16[16,32,256]{2,1,0:T(8,128)(2,1)S(1)} async-done(((bf16[16,32,256]{2,1,0:T(8,128)(2,1)}), bf16[16,32,256]{2,1,0:T(8,128)(2,1)S(1)}, u32[]{:S(2)}, u32[]{:S(2)}) %all-to-all-start) | async-done | bytes 262176 | tf_op jit(solution)/shard_map/all_to_all | solution.py:29
  35.6 1.1 shard_map.50
  36.7 4.8 %all-to-all-start.1 = ((bf16[4,128,1024]{2,1,0:T(8,128)(2,1)}), bf16[4,128,1024]{2,1,0:T(8,128)(2,1)S(1)}, u32[]{:S(2)}, u32[]{:S(2)}) async-start(bf16[4,128,1024]{2,1,0:T(8,128)(2,1)} %shard_map.50), calls=%async_computation.1 | async-start | bytes 2097152 | tf_op jit(solution)/shard_map/all_to_all | solution.py:29
  41.5 1.9 %collective-permute-start.3 = (bf16[256,1024]{1,0:T(8,128)(2,1)S(1)}, bf16[256,1024]{1,0:T(8,128)(2,1)S(1)}, u32[]{:S(2)}, u32[]{:S(2)}) collective-permute-start(bf16[256,1024]{1,0:T(8,128)(2,1)S(1)} %constant_dynamic-update-slice_fusion.p_ref), channel_id=1, source_target_pairs={{0,1},{1,0},{2,3},{3,2},{4,5},{5,4},{6,7},{7,6},{8,9},{9,8},{10,11... | collective-permute-start | bytes 1572872 | tf_op jit(solution)/shard_map/ppermute | solution.py:21
  43.4 8.1 %all-to-all-done.1 = bf16[4,128,1024]{2,1,0:T(8,128)(2,1)S(1)} async-done(((bf16[4,128,1024]{2,1,0:T(8,128)(2,1)}), bf16[4,128,1024]{2,1,0:T(8,128)(2,1)S(1)}, u32[]{:S(2)}, u32[]{:S(2)}) %all-to-all-start.1) | async-done | bytes 1048608 | tf_op jit(solution)/shard_map/all_to_all | solution.py:29
  51.5 1.7 %shard_map.51 = f32[4,128,512]{2,1,0:T(8,128)} custom-call(s32[1]{0:T(128)} %bitcast.place_ref.x_ref, bf16[512,1024]{1,0:T(8,128)(2,1)S(1)} %bitcast.25, bf16[256,1024]{1,0:T(8,128)(2,1)S(1)} %constant_dynamic-update-slice_fusion.p_ref, bf16[256,1024]{1,0:T(8,128)(2,1)S(1)} %collective-permute-done.3.p_other_ref), custom_call_target="tpu_custom_call" | custom-call | flops 536870912 | bytes 3145728 | tf_op jit(solution)/shard_map/pallas_call | solution.py:43
  53.2 4.5 %all-to-all-start.2 = ((f32[4,128,512]{2,1,0:T(8,128)}), f32[4,128,512]{2,1,0:T(8,128)S(1)}, u32[]{:S(2)}, u32[]{:S(2)}) async-start(f32[4,128,512]{2,1,0:T(8,128)} %shard_map.51), calls=%async_computation.2 | async-start | bytes 2097152 | tf_op jit(solution)/shard_map/all_to_all | solution.py:29
  57.7 0.7 copy-done.2
  58.4 10.2 %all-to-all-done.2 = f32[4,128,512]{2,1,0:T(8,128)S(1)} async-done(((f32[4,128,512]{2,1,0:T(8,128)}), f32[4,128,512]{2,1,0:T(8,128)S(1)}, u32[]{:S(2)}, u32[]{:S(2)}) %all-to-all-start.2) | async-done | bytes 1048608 | tf_op jit(solution)/shard_map/all_to_all | solution.py:29
  69.5 12.5 %all-to-all-start.3 = ((f32[16,1,384]{2,1,0:T(1,128)}), f32[16,1,384]{2,1,0:T(1,128)S(1)}, u32[]{:S(2)}, u32[]{:S(2)}) async-start(f32[16,1,384]{2,1,0:T(1,128)} %broadcast_in_dim.23), calls=%async_computation.3 | async-start | bytes 49152 | tf_op jit(solution)/shard_map/all_to_all | solution.py:29
  82.0 1.9 %collective-permute-start.5 = (bf16[512,1024]{1,0:T(8,128)(2,1)S(1)}, bf16[512,1024]{1,0:T(8,128)(2,1)}, u32[]{:S(2)}, u32[]{:S(2)}) collective-permute-start(bf16[512,1024]{1,0:T(8,128)(2,1)S(1)} %bitcast.26), channel_id=1, source_target_pairs={{0,1},{1,0},{2,3},{3,2},{4,5},{5,4},{6,7},{7,6},{8,9},{9,8},{10,11... | collective-permute-start | bytes 3145736 | tf_op jit(solution)/shard_map/ppermute | solution.py:21
  84.0 10.9 %all-to-all-done.3 = f32[16,1,384]{2,1,0:T(1,128)S(1)} async-done(((f32[16,1,384]{2,1,0:T(1,128)}), f32[16,1,384]{2,1,0:T(1,128)S(1)}, u32[]{:S(2)}, u32[]{:S(2)}) %all-to-all-start.3) | async-done | bytes 24608 | tf_op jit(solution)/shard_map/all_to_all | solution.py:29
  95.2 10.5 %all_to_all.39 = bf16[4,128,512]{2,1,0:T(8,128)(2,1)S(1)} all-to-all(bf16[4,128,512]{2,1,0:T(8,128)(2,1)S(1)} %broadcast_in_dim.24), channel_id=1, replica_groups=mesh['y'=4,'zl'=4,'zh'=4,'x'=4,'c'=2] {'y'}, dimensions={0} | all-to-all | bytes 1048576 | tf_op jit(solution)/shard_map/all_to_all | solution.py:29
  105.7 0.7 shard_map.53
  106.5 1.0 copy-done
  107.5 6.3 %all-to-all-start.5 = ((bf16[4,128,1024]{2,1,0:T(8,128)(2,1)}), bf16[4,128,1024]{2,1,0:T(8,128)(2,1)}, u32[]{:S(2)}, u32[]{:S(2)}) async-start(bf16[4,128,1024]{2,1,0:T(8,128)(2,1)} %copy-done), calls=%async_computation.5 | async-start | bytes 2097152 | tf_op jit(solution)/shard_map/all_to_all | solution.py:29
  113.8 1.9 %collective-permute-start.4 = (bf16[4,4,32,256]{3,2,1,0:T(8,128)(2,1)S(1)}, bf16[4,4,32,256]{3,2,1,0:T(8,128)(2,1)S(1)}, u32[]{:S(2)}, u32[]{:S(2)}) collective-permute-start(bf16[4,4,32,256]{3,2,1,0:T(8,128)(2,1)S(1)} %slice.39), channel_id=1, source_target_pairs={{0,1},{1,0},{2,3},{3,2},{4,5},{5,4},{6,7},{7,6},{8,9},{9,8},{10,11... | collective-permute-start | bytes 786440 | tf_op jit(solution)/shard_map/ppermute | solution.py:21
  115.7 1.5 collective-permute-done.4.far_w_ref
  117.2 2.0 %shard_map.55 = (f32[2,256,256]{2,1,0:T(8,128)S(1)}, bf16[2,256,256]{2,1,0:T(8,128)(2,1)S(1)}) custom-call(s32[1]{0:T(128)} %bitcast.9.zl_ref.place_ref, bf16[4,4,32,512]{3,2,1,0:T(8,128)(2,1)S(1)} %bitcast.23, bf16[4,4,32,256]{3,2,1,0:T(8,128)(2,1)S(1)} %collective-permute-done.4.far_w_ref, bf16[512,1024]{1,0:T(8,128)(2,1)S(1)} %bitcast.27, ...), custom_call_target="tpu_custom_call" | custom-call | flops 536870912 | bytes 3670016 | tf_op jit(solution)/shard_map/pallas_call | solution.py:43
  119.2 2.4 %collective-permute-start.6 = (bf16[2,256,256]{2,1,0:T(8,128)(2,1)S(1)}, bf16[2,256,256]{2,1,0:T(8,128)(2,1)S(1)}, u32[]{:S(2)}, u32[]{:S(2)}) collective-permute-start(bf16[2,256,256]{2,1,0:T(8,128)(2,1)S(1)} %get-tuple-element.11), channel_id=1, source_target_pairs={{0,32},{32,0},{64,96},{96,64},{1,33},{33,1},{65,97},{97,65},{2,34}... | collective-permute-start | bytes 786440 | tf_op jit(solution)/shard_map/ppermute | solution.py:25
  121.9 0.8 all-to-all-done.5.moved_ref
  122.7 2.1 %shard_map.54 = bf16[16,32,256]{2,1,0:T(8,128)(2,1)} custom-call(s32[1]{0:T(128)} %bitcast.place_ref.x_ref, f32[128,1024]{1,0:T(8,128)S(1)} %shard_map.52.own_ref, bf16[4,128,1024]{2,1,0:T(8,128)(2,1)} %all-to-all-done.5.moved_ref), custom_call_target="tpu_custom_call" | custom-call | bytes 1835008 | tf_op jit(solution)/shard_map/pallas_call | solution.py:43
  124.8 4.4 %all-to-all-start.6 = ((bf16[16,32,256]{2,1,0:T(8,128)(2,1)}), bf16[16,32,256]{2,1,0:T(8,128)(2,1)S(1)}, u32[]{:S(2)}, u32[]{:S(2)}) async-start(bf16[16,32,256]{2,1,0:T(8,128)(2,1)} %shard_map.54), calls=%async_computation.6 | async-start | bytes 524288 | tf_op jit(solution)/shard_map/all_to_all | solution.py:29
  129.5 4.5 %collective-permute-start.7 = (bf16[256,256]{1,0:T(8,128)(2,1)S(1)}, bf16[256,256]{1,0:T(8,128)(2,1)S(1)}, u32[]{:S(2)}, u32[]{:S(2)}) collective-permute-start(bf16[256,256]{1,0:T(8,128)(2,1)S(1)} %get-tuple-element.13), channel_id=1, source_target_pairs={{0,64},{32,96},{64,0},{96,32},{1,65},{33,97},{65,1},{97,33},{2,66}... | collective-permute-start | bytes 393224 | tf_op jit(solution)/shard_map/ppermute | solution.py:25
  134.0 13.9 %collective-permute-done.7 = bf16[256,256]{1,0:T(8,128)(2,1)S(1)} collective-permute-done((bf16[256,256]{1,0:T(8,128)(2,1)S(1)}, bf16[256,256]{1,0:T(8,128)(2,1)S(1)}, u32[]{:S(2)}, u32[]{:S(2)}) %collective-permute-start.7) | collective-permute-done | bytes 131104 | tf_op jit(solution)/shard_map/ppermute | solution.py:25
  147.9 0.7 add_convert_fusion
  148.6 0.7 bitcast_reduce_fusion
  (35 shorter events, 2.1 us)
Async XLA Ops:
  2.2 15.3 %copy-start.1 = (bf16[256,256]{1,0:T(8,128)(2,1)S(1)}, bf16[256,256]{1,0:T(8,128)(2,1)}, u32[]{:S(2)}) copy-start(bf16[256,256]{1,0:T(8,128)(2,1)} %param.4) | copy-start | bytes 393220
  2.2 33.4 %all-to-all-start = ((bf16[16,32,256]{2,1,0:T(8,128)(2,1)}), bf16[16,32,256]{2,1,0:T(8,128)(2,1)S(1)}, u32[]{:S(2)}, u32[]{:S(2)}) async-start(bf16[16,32,256]{2,1,0:T(8,128)(2,1)} %bitcast.2), calls=%async_computation | async-start | bytes 524288 | tf_op jit(solution)/shard_map/all_to_all | solution.py:29
  17.5 23.9 %collective-permute-start = (bf16[256,256]{1,0:T(8,128)(2,1)S(1)}, bf16[256,256]{1,0:T(8,128)(2,1)S(1)}, u32[]{:S(2)}, u32[]{:S(2)}) collective-permute-start(bf16[256,256]{1,0:T(8,128)(2,1)S(1)} %copy-done.1), channel_id=1, source_target_pairs={{0,32},{32,64},{64,96},{96,0},{1,33},{33,65},{65,97},{97,1},{2,34}... | collective-permute-start | bytes 393224 | tf_op jit(solution)/shard_map/ppermute | solution.py:21
  21.4 20.1 %collective-permute-start.1 = (bf16[256,256]{1,0:T(8,128)(2,1)S(1)}, bf16[256,256]{1,0:T(8,128)(2,1)S(1)}, u32[]{:S(2)}, u32[]{:S(2)}) collective-permute-start(bf16[256,256]{1,0:T(8,128)(2,1)S(1)} %copy-done.1), channel_id=1, source_target_pairs={{0,64},{32,96},{64,0},{96,32},{1,65},{33,97},{65,1},{97,33},{2,66}... | collective-permute-start | bytes 393224 | tf_op jit(solution)/shard_map/ppermute | solution.py:21
  25.7 15.8 %collective-permute-start.2 = (bf16[256,256]{1,0:T(8,128)(2,1)S(1)}, bf16[256,256]{1,0:T(8,128)(2,1)S(1)}, u32[]{:S(2)}, u32[]{:S(2)}) collective-permute-start(bf16[256,256]{1,0:T(8,128)(2,1)S(1)} %copy-done.1), channel_id=1, source_target_pairs={{0,96},{32,0},{64,32},{96,64},{1,97},{33,1},{65,33},{97,65},{2,98}... | collective-permute-start | bytes 393224 | tf_op jit(solution)/shard_map/ppermute | solution.py:21
  36.7 14.9 %all-to-all-start.1 = ((bf16[4,128,1024]{2,1,0:T(8,128)(2,1)}), bf16[4,128,1024]{2,1,0:T(8,128)(2,1)S(1)}, u32[]{:S(2)}, u32[]{:S(2)}) async-start(bf16[4,128,1024]{2,1,0:T(8,128)(2,1)} %shard_map.50), calls=%async_computation.1 | async-start | bytes 2097152 | tf_op jit(solution)/shard_map/all_to_all | solution.py:29
  41.5 10.0 %collective-permute-start.3 = (bf16[256,1024]{1,0:T(8,128)(2,1)S(1)}, bf16[256,1024]{1,0:T(8,128)(2,1)S(1)}, u32[]{:S(2)}, u32[]{:S(2)}) collective-permute-start(bf16[256,1024]{1,0:T(8,128)(2,1)S(1)} %constant_dynamic-update-slice_fusion.p_ref), channel_id=1, source_target_pairs={{0,1},{1,0},{2,3},{3,2},{4,5},{5,4},{6,7},{7,6},{8,9},{9,8},{10,11... | collective-permute-start | bytes 1572872 | tf_op jit(solution)/shard_map/ppermute | solution.py:21
  53.2 15.4 %all-to-all-start.2 = ((f32[4,128,512]{2,1,0:T(8,128)}), f32[4,128,512]{2,1,0:T(8,128)S(1)}, u32[]{:S(2)}, u32[]{:S(2)}) async-start(f32[4,128,512]{2,1,0:T(8,128)} %shard_map.51), calls=%async_computation.2 | async-start | bytes 2097152 | tf_op jit(solution)/shard_map/all_to_all | solution.py:29
  57.7 0.7 copy-start.2
  69.5 25.3 %all-to-all-start.3 = ((f32[16,1,384]{2,1,0:T(1,128)}), f32[16,1,384]{2,1,0:T(1,128)S(1)}, u32[]{:S(2)}, u32[]{:S(2)}) async-start(f32[16,1,384]{2,1,0:T(1,128)} %broadcast_in_dim.23), calls=%async_computation.3 | async-start | bytes 49152 | tf_op jit(solution)/shard_map/all_to_all | solution.py:29
  82.0 33.6 %collective-permute-start.5 = (bf16[512,1024]{1,0:T(8,128)(2,1)S(1)}, bf16[512,1024]{1,0:T(8,128)(2,1)}, u32[]{:S(2)}, u32[]{:S(2)}) collective-permute-start(bf16[512,1024]{1,0:T(8,128)(2,1)S(1)} %bitcast.26), channel_id=1, source_target_pairs={{0,1},{1,0},{2,3},{3,2},{4,5},{5,4},{6,7},{7,6},{8,9},{9,8},{10,11... | collective-permute-start | bytes 3145736 | tf_op jit(solution)/shard_map/ppermute | solution.py:21
  106.4 1.0 copy-start
  107.5 15.2 %all-to-all-start.5 = ((bf16[4,128,1024]{2,1,0:T(8,128)(2,1)}), bf16[4,128,1024]{2,1,0:T(8,128)(2,1)}, u32[]{:S(2)}, u32[]{:S(2)}) async-start(bf16[4,128,1024]{2,1,0:T(8,128)(2,1)} %copy-done), calls=%async_computation.5 | async-start | bytes 2097152 | tf_op jit(solution)/shard_map/all_to_all | solution.py:29
  113.8 3.4 %collective-permute-start.4 = (bf16[4,4,32,256]{3,2,1,0:T(8,128)(2,1)S(1)}, bf16[4,4,32,256]{3,2,1,0:T(8,128)(2,1)S(1)}, u32[]{:S(2)}, u32[]{:S(2)}) collective-permute-start(bf16[4,4,32,256]{3,2,1,0:T(8,128)(2,1)S(1)} %slice.39), channel_id=1, source_target_pairs={{0,1},{1,0},{2,3},{3,2},{4,5},{5,4},{6,7},{7,6},{8,9},{9,8},{10,11... | collective-permute-start | bytes 786440 | tf_op jit(solution)/shard_map/ppermute | solution.py:21
  119.2 10.2 %collective-permute-start.6 = (bf16[2,256,256]{2,1,0:T(8,128)(2,1)S(1)}, bf16[2,256,256]{2,1,0:T(8,128)(2,1)S(1)}, u32[]{:S(2)}, u32[]{:S(2)}) collective-permute-start(bf16[2,256,256]{2,1,0:T(8,128)(2,1)S(1)} %get-tuple-element.11), channel_id=1, source_target_pairs={{0,32},{32,0},{64,96},{96,64},{1,33},{33,1},{65,97},{97,65},{2,34}... | collective-permute-start | bytes 786440 | tf_op jit(solution)/shard_map/ppermute | solution.py:25
  124.8 23.8 %all-to-all-start.6 = ((bf16[16,32,256]{2,1,0:T(8,128)(2,1)}), bf16[16,32,256]{2,1,0:T(8,128)(2,1)S(1)}, u32[]{:S(2)}, u32[]{:S(2)}) async-start(bf16[16,32,256]{2,1,0:T(8,128)(2,1)} %shard_map.54), calls=%async_computation.6 | async-start | bytes 524288 | tf_op jit(solution)/shard_map/all_to_all | solution.py:29
  129.5 18.4 %collective-permute-start.7 = (bf16[256,256]{1,0:T(8,128)(2,1)S(1)}, bf16[256,256]{1,0:T(8,128)(2,1)S(1)}, u32[]{:S(2)}, u32[]{:S(2)}) collective-permute-start(bf16[256,256]{1,0:T(8,128)(2,1)S(1)} %get-tuple-element.13), channel_id=1, source_target_pairs={{0,64},{32,96},{64,0},{96,32},{1,65},{33,97},{65,1},{97,33},{2,66}... | collective-permute-start | bytes 393224 | tf_op jit(solution)/shard_map/ppermute | solution.py:25
